TPU v7x, 32 devices: a whole 2x2x4 slice. The times are simulated.
32 devices in a mesh: row: 8 (over z, y), col: 4 (over x, core).
Axes of the slice: x: 2, y: 2, z: 4, core: 2. Of those that a mesh axis runs over, the one named last changes fastest.
Arguments:
- inputs: bfloat16 [512, 12288], P('row', 'col'), may hold values from -6 to 6
- hidden_pre: bfloat16 [512, 24576], P(None, 'row'), may hold values from -8 to 8
- out_grad: bfloat16 [512, 12288], P('row', 'col'), may hold values from -6 to 6
- weight_in: bfloat16 [12288, 24576], P('col', 'row'), may hold values from -0.0546875 to 0.0546875
- weight_out: bfloat16 [24576, 12288], P('row', 'col'), may hold values from -0.0390625 to 0.0390625
Outputs:
- grad_in: bfloat16 [512, 12288], P('row', 'col')
- grad_weight_in: bfloat16 [12288, 24576], P('col', 'row')
- grad_weight_out: bfloat16 [24576, 12288], P('row', 'col')
All inputs are finite; a program needn't handle non-finite values.
Results may differ from a plain program's by a relative error of at most 0.0049.
Values may be sent and summed in bfloat16 or wider, within the bound.
No kernel may reach another device: no remote copies, remote signals or barrier semaphores. Data moves between devices by JAX's collectives and lax.ppermute only.
A program may use at most 192 MiB of HBM per device.

v0:
```python
import jax
import jax.numpy as jnp
from jax import lax
from jax.sharding import PartitionSpec as P


def gelu_parts(hidden_pre):
    hval = hidden_pre.astype(jnp.float32)
    inner = 0.7978845608 * (hval + 0.044715 * hval * hval * hval)
    tval = jnp.tanh(inner)
    act = 0.5 * hval * (1.0 + tval)
    slope = 0.5 * (1.0 + tval) + 0.5 * hval * (1.0 - tval * tval) * 0.7978845608 * (
        1.0 + 3.0 * 0.044715 * hval * hval
    )
    return (act, slope)


def contract_rows(left, right):
    return lax.dot_general(
        left, right, (((0,), (0,)), ((), ())), preferred_element_type=jnp.float32
    )


def contract_cols(left, right):
    return lax.dot_general(
        left, right, (((1,), (1,)), ((), ())), preferred_element_type=jnp.float32
    )


def body(inputs, hidden_pre, out_grad, weight_in, weight_out):
    act, slope = gelu_parts(hidden_pre)
    act_b = act.astype(jnp.bfloat16)
    grad_all, input_all = (
        lax.all_gather(out_grad, "row", axis=0, tiled=True),
        lax.all_gather(inputs, "row", axis=0, tiled=True),
    )
    grad_weight_out = contract_rows(act_b, grad_all).astype(jnp.bfloat16)
    col_rows = grad_all.shape[0] // lax.axis_size("col")
    piece = grad_all
    d_act = lax.psum_scatter(
        contract_cols(piece, weight_out), "col", scatter_dimension=0, tiled=True
    )
    slope_mine = lax.dynamic_slice_in_dim(slope, lax.axis_index("col") * col_rows, col_rows, 0)
    d_mine = (d_act * slope_mine).astype(jnp.bfloat16)
    d_hid = lax.all_gather(d_mine, "col", axis=0, tiled=True)
    piece = d_hid
    grad_in = lax.psum_scatter(
        contract_cols(piece, weight_in), "row", scatter_dimension=0, tiled=True
    ).astype(jnp.bfloat16)
    grad_weight_in = contract_rows(input_all, d_hid).astype(jnp.bfloat16)
    return (grad_in, grad_weight_in, grad_weight_out)


def solution(mesh):
    return jax.shard_map(
        body,
        mesh=mesh,
        in_specs=(
            P("row", "col"),
            P(None, "row"),
            P("row", "col"),
            P("col", "row"),
            P("row", "col"),
        ),
        out_specs=(P("row", "col"), P("col", "row"), P("row", "col")),
        check_vma=False,
    )
```

profile of v0, /device:TPU:0, one launch (start us, length us, event | category | flops | bytes accessed | tf_op | source)
XLA Modules:
  0.0 372.2 jit_solution(12768882832182549941)
XLA Ops:
  7.2 0.0 all-gather.4.cloned.1.call-start
  7.2 0.7 all-gather.4.cloned.1.call-update
  7.9 0.0 reduce-scatter.3.cloned.1.call-start
  7.9 65.4 %all-gather.4.cloned.1.call-done = bf16[512,3072]{1,0:T(8,128)(2,1)} async-done(((bf16[64,3072]{1,0:T(8,128)(2,1)}), bf16[512,3072]{1,0:T(8,128)(2,1)}) %all-gather.4.cloned.1.call-update) | async-done | bytes 3145744 | tf_op jit(solution)/shard_map/all_gather | solution.py:34
  73.4 16.4 %fusion.11 = f32[512,3072]{1,0:T(8,128)} fusion(bf16[512,3072]{1,0:T(8,128)(2,1)} %all-gather.4.cloned.1.call-done, bf16[3072,3072]{1,0:T(8,128)(2,1)} %param.9), kind=kOutput, calls=%fused_computation.20 | convolution fusion | flops 9663676416 | bytes 28311552 | tf_op jit(solution)/shard_map/dot_general | solution.py:25
  89.7 0.0 copy-start
  89.7 0.0 reduce-scatter.3.cloned.1.call-update
  89.8 0.0 all-gather.6.cloned.1.call-start
  89.8 1.8 copy-done
  91.6 3.9 %convert_element_type.21 = f32[512,3072]{1,0:T(8,128)} convert(bf16[512,3072]{1,0:T(8,128)(2,1)S(1)} %copy-done) | non-fusion elementwise | flops 1572864 | bytes 9437184 | tf_op jit(solution)/shard_map/convert_element_type | solution.py:8
  95.6 8.7 %fusion.1 = (f32[512,3072]{1,0:T(8,128)}, f32[512,3072]{1,0:T(8,128)}, f32[512,3072]{1,0:T(8,128)}) fusion(bf16[512,3072]{1,0:T(8,128)(2,1)S(1)} %copy-done), kind=kLoop, calls=%fused_computation.4 | loop fusion | flops 12582912 | bytes 22020096 | tf_op jit(solution)/shard_map/tanh | solution.py:10
  104.3 42.6 %reduce-scatter.3.cloned.1.call-done = f32[128,3072]{1,0:T(8,128)} async-done(((f32[512,3072]{1,0:T(8,128)}), f32[128,3072]{1,0:T(8,128)}) %reduce-scatter.3.cloned.1.call-update) | async-done | bytes 1572880 | tf_op jit(solution)/shard_map/reduce_scatter | solution.py:40
  146.9 5.0 %fusion.6 = bf16[128,3072]{1,0:T(8,128)(2,1)} fusion(f32[128,3072]{1,0:T(8,128)} %reduce-scatter.3.cloned.1.call-done, f32[512,3072]{1,0:T(8,128)} %get-tuple-element.7, s32[]{:T(128)S(6)} %select_n.3, f32[512,3072]{1,0:T(8,128)} %get-tuple-element.8, f32[512,3072]{1,0:T(8,128)} %convert_element_type.21, f32[512,3072]{1,0:T(8,128)} %get-tuple-element.6), kind=kLoop, calls=%fused_computation.13 | loop fusion | flops 4718592 | bytes 8650756 | tf_op jit(solution)/shard_map/convert_element_type | solution.py:44
  151.9 0.0 all-gather.6.cloned.1.call-update
  151.9 0.0 all-gather.8.cloned.1.call-start
  151.9 0.5 all-gather.8.cloned.1.call-update
  152.5 0.2 reduce-scatter.5.cloned.1.call-start
  152.7 27.9 %all-gather.6.cloned.1.call-done = bf16[512,3072]{1,0:T(8,128)(2,1)} async-done(((bf16[128,3072]{1,0:T(8,128)(2,1)}), bf16[512,3072]{1,0:T(8,128)(2,1)}) %all-gather.6.cloned.1.call-update) | async-done | bytes 3145744 | tf_op jit(solution)/shard_map/all_gather | solution.py:45
  180.6 16.4 %fusion.12 = f32[512,3072]{1,0:T(8,128)} fusion(bf16[512,3072]{1,0:T(8,128)(2,1)} %all-gather.6.cloned.1.call-done, bf16[3072,3072]{1,0:T(8,128)(2,1)} %param.8), kind=kOutput, calls=%fused_computation.21 | convolution fusion | flops 9663676416 | bytes 28311552 | tf_op jit(solution)/shard_map/dot_general | solution.py:25
  197.0 0.0 reduce-scatter.5.cloned.1.call-update
  197.0 16.1 %convolution_convert_fusion = bf16[3072,3072]{1,0:T(8,128)(2,1)} fusion(bf16[512,3072]{1,0:T(8,128)(2,1)} %all-gather.4.cloned.1.call-done, bf16[512,3072]{1,0:T(8,128)(2,1)S(1)} %copy-done), kind=kOutput, calls=%fused_computation.1 | convolution fusion | flops 9688842240 | bytes 25165824 | tf_op jit(solution)/shard_map/dot_general | solution.py:19
  213.2 30.2 %all-gather.8.cloned.1.call-done = bf16[512,3072]{1,0:T(8,128)(2,1)} async-done(((bf16[64,3072]{1,0:T(8,128)(2,1)}), bf16[512,3072]{1,0:T(8,128)(2,1)}) %all-gather.8.cloned.1.call-update) | async-done | bytes 3145744 | tf_op jit(solution)/shard_map/all_gather | solution.py:35
  243.3 16.3 %convert_bitcast_fusion = bf16[3072,3072]{0,1:T(8,128)(2,1)} fusion(bf16[512,3072]{1,0:T(8,128)(2,1)} %all-gather.6.cloned.1.call-done, bf16[512,3072]{1,0:T(8,128)(2,1)} %all-gather.8.cloned.1.call-done), kind=kOutput, calls=%fused_computation | convolution fusion | flops 9673113600 | bytes 25165824 | tf_op jit(solution)/shard_map/dot_general | solution.py:19
  259.6 24.8 %copy.8 = bf16[3072,3072]{1,0:T(8,128)(2,1)} copy(bf16[3072,3072]{0,1:T(8,128)(2,1)} %convert_bitcast_fusion) | data formatting | bytes 37748736
  284.3 79.4 %reduce-scatter.5.cloned.1.call-done = f32[64,3072]{1,0:T(8,128)} async-done(((f32[512,3072]{1,0:T(8,128)}), f32[64,3072]{1,0:T(8,128)}) %reduce-scatter.5.cloned.1.call-update) | async-done | bytes 786448 | tf_op jit(solution)/shard_map/reduce_scatter | solution.py:47
  363.8 1.9 convert_element_type.23
Async XLA Ops:
  7.2 66.2 %all-gather.4.cloned.1.call-start = ((), (), s32[]{:S(2)}) async-start(), calls=%async_computation.2 | async-start | bytes 3538944 | tf_op jit(solution)/shard_map/all_gather | solution.py:34
  7.9 139.0 %reduce-scatter.3.cloned.1.call-start = ((), (), s32[]{:S(2)}) async-start(), calls=%async_computation.3 | async-start | bytes 7864320 | tf_op jit(solution)/shard_map/reduce_scatter | solution.py:40
  89.7 1.9 copy-start
  89.8 90.8 %all-gather.6.cloned.1.call-start = ((), (), s32[]{:S(2)}) async-start(), calls=%async_computation.4 | async-start | bytes 3932160 | tf_op jit(solution)/shard_map/all_gather | solution.py:45
  151.9 91.4 %all-gather.8.cloned.1.call-start = ((), (), s32[]{:S(2)}) async-start(), calls=%async_computation.6 | async-start | bytes 3538944 | tf_op jit(solution)/shard_map/all_gather | solution.py:35
  152.5 211.3 %reduce-scatter.5.cloned.1.call-start = ((), (), s32[]{:S(2)}) async-start(), calls=%async_computation.5 | async-start | bytes 7077888 | tf_op jit(solution)/shard_map/reduce_scatter | solution.py:47
Sparse Core Ops, SparseCore 0:
  10.2 63.1 all-gather.3
  89.9 56.9 reduce-scatter.2
  152.0 28.5 all-gather.5
  182.8 60.4 all-gather.7
  247.2 116.5 reduce-scatter.4
where the time goes:
time: 373 us; the launch traced here: 372 us
  waiting for transfers between devices  247 us (66%)
  matrix products  65.2 us (17%)
  local copies, waits for them, and re-layouts  26.6 us (7%)
  other arithmetic  19.6 us (5%)
  between operations  13.8 us (4%)
    reduce_scatter x1, waiting for transfers between devices, body(): lax.psum_scatter(contract_cols(piece, weight_in), 'row', scatter_dimensio...  79.4 us
    all_gather x1, waiting for transfers between devices, body(): lax.all_gather(out_grad, 'row', axis=0, tiled=True)  65.4 us
    reduce_scatter x1, waiting for transfers between devices, body(): lax.psum_scatter(contract_cols(piece, weight_out), 'col', scatter_dimensi...  42.6 us
    dot_general x2, matrix products, contract_cols(): lax.dot_general(left, right, (((1,), (1,)), ((), ())), preferred_element_...  32.8 us
    dot_general x2, matrix products, contract_rows(): lax.dot_general(left, right, (((0,), (0,)), ((), ())), preferred_element_...  32.4 us
    all_gather x1, waiting for transfers between devices, body(): lax.all_gather(inputs, 'row', axis=0, tiled=True)  30.2 us
    all_gather x1, waiting for transfers between devices, body(): d_hid = lax.all_gather(d_mine, 'col', axis=0, tiled=True)  27.9 us
    unnamed x3, local copies, waits for them, and re-layouts  26.6 us
  transfers between devices with their start and end apart: 5, of which 5 were waited for; matrix products, arithmetic and copies ran while one was open for 23% of the time, Pallas kernels for 0%

commit v1 on v0

v1 whole, which is shorter than its diff:
```python
import functools

import jax
import jax.numpy as jnp
from jax import lax
from jax.experimental import pallas as pl
from jax.experimental.pallas import tpu as pltpu
from jax.sharding import PartitionSpec as P

VMEM_BYTES = 48 * 2**20


def row_cycle(mesh):
    first = mesh.devices[:, 0]
    places = [getattr(device, "coords", None) for device in first]
    if any(place is None for place in places):
        return list(range(len(first)))
    at = {(place[2], place[1]): index for index, place in enumerate(places)}
    zs, ys = (sorted({key[i] for key in at}) for i in (0, 1))
    if len(at) != len(places) or len(at) != len(zs) * len(ys) or len(ys) < 2:
        return list(range(len(first)))
    walk = []
    for step, z in enumerate(zs):
        walk += [at[z, y] for y in (ys[1:] if step % 2 == 0 else ys[:0:-1])]
    return walk + [at[z, ys[0]] for z in reversed(zs)]


def pieces_of(length, want):
    return max(n for n in range(1, want + 1) if length % (128 * n) == 0 or n == 1)


def tile_of(length, most):
    return max(t for t in range(1, most + 1) if length % t == 0 and (t % 128 == 0 or t == length))


def gelu_parts(hidden_pre):
    hval = hidden_pre.astype(jnp.float32)
    inner = 0.7978845608 * (hval + 0.044715 * hval * hval * hval)
    tval = jnp.tanh(inner)
    act = 0.5 * hval * (1.0 + tval)
    slope = 0.5 * (1.0 + tval) + 0.5 * hval * (1.0 - tval * tval) * 0.7978845608 * (
        1.0 + 3.0 * 0.044715 * hval * hval
    )
    return (act, slope)


def gelu_piece(order, hidden_pre, count, part, parts, held):
    tokens, hidden = hidden_pre.shape
    share = tokens // count
    half = hidden // 2
    steps = count // parts
    first = part * steps

    def kernel(order_ref, h_ref, *refs):
        act_ref, slope_ref = refs[-2:]
        for index in range(2):
            act, slope = gelu_parts(h_ref[:, index * half : (index + 1) * half])
            act_ref[:, index * half : (index + 1) * half] = act.astype(jnp.bfloat16)

            @pl.when(order_ref[count] == index)
            def _():
                slope_ref[...] = slope

    return pl.pallas_call(
        kernel,
        grid_spec=pltpu.PrefetchScalarGridSpec(
            num_scalar_prefetch=1,
            grid=(steps,),
            in_specs=[pl.BlockSpec((share, hidden), lambda i, s: (s[first + i], 0))]
            + ([] if held is None else [pl.BlockSpec(memory_space=pl.ANY)] * 2),
            out_specs=[
                pl.BlockSpec((share, hidden), lambda i, s: (first + i, 0)),
                pl.BlockSpec((share, half), lambda i, s: (first + i, 0)),
            ],
        ),
        out_shape=[
            jax.ShapeDtypeStruct((tokens, hidden), jnp.bfloat16),
            jax.ShapeDtypeStruct((tokens, half), jnp.float32),
        ],
        input_output_aliases={} if held is None else {2: 0, 3: 1},
        compiler_params=pltpu.CompilerParams(vmem_limit_bytes=VMEM_BYTES),
        cost_estimate=cost(20 * tokens * hidden // parts, 6 * tokens * hidden // parts),
        name="gelu_piece",
    )(order, hidden_pre, *(held or ()))


def after(value, *others):
    return lax.optimization_barrier((value, *others))[0]


def ring_gather(value, cycle):
    count = len(cycle)
    ahead = [(cycle[i], cycle[(i + 1) % count]) for i in range(count)]
    behind = [(b, a) for a, b in ahead]
    blocks = {0: value}
    state = [value, value]

    def step(k, *others):
        fore, back = state
        if 2 * k == count:
            cut = value.shape[0] // 2
            fore, back = fore[:cut], back[cut:]
        if others:
            fore, back = lax.optimization_barrier((fore, back, *others))[:2]
        state[:] = lax.ppermute(fore, "row", ahead), lax.ppermute(back, "row", behind)
        if 2 * k == count:
            blocks[k] = jnp.concatenate(state, 0)
        else:
            blocks[count - k], blocks[k] = state

    return step, lambda: jnp.concatenate([blocks[k] for k in range(count)], 0)


def ring_sum(partial, cycle, dtype, fill):
    count = len(cycle)
    share = partial.shape[0] // count
    width = partial.shape[1]
    half = width // 2
    ahead = [(cycle[i], cycle[(i + 1) % count]) for i in range(count)]
    behind = [(b, a) for a, b in ahead]

    def block(shift):
        start = shift % count * share
        return partial[start : start + share]

    def plus(left, right):
        return left.astype(jnp.float32) + right.astype(jnp.float32)

    def move(first, second):
        sent = (first.astype(jnp.bfloat16), second.astype(jnp.bfloat16))
        return fill(sent, (lax.ppermute(sent[0], "row", ahead), lax.ppermute(sent[1], "row", behind)))

    most = count // 2
    if count == 1:
        return partial.astype(dtype)
    fore = back = None
    if count % 2 == 0:
        far = block(most)
        fore, back = move(far[:, :half], far[:, half:])
        most -= 1
    for shift in range(most, 0, -1):
        first, second = block(shift), block(-shift)
        if fore is not None and fore.shape[1] < width:
            first = jnp.concatenate([plus(first[:, :half], fore), first[:, half:]], 1)
            second = jnp.concatenate([second[:, :half], plus(second[:, half:], back)], 1)
        elif fore is not None:
            first, second = plus(first, fore), plus(second, back)
        fore, back = move(first, second)
    own = block(0)
    if fore.shape[1] < width:
        return jnp.concatenate([plus(own[:, :half], fore), plus(own[:, half:], back)], 1).astype(dtype)
    return (plus(own, fore) + back.astype(jnp.float32)).astype(dtype)


def cost(flops, moved):
    return pl.CostEstimate(flops=flops, bytes_accessed=moved, transcendentals=0)


def act_grad_piece(start, grads, weight_out, width, dtype):
    tokens, depth = grads.shape
    tile = tile_of(width, 256)

    def kernel(_, g_ref, w_ref, o_ref):
        o_ref[...] = lax.dot_general(
            g_ref[...], w_ref[...], (((1,), (1,)), ((), ())), preferred_element_type=jnp.float32
        ).astype(dtype)

    return pl.pallas_call(
        kernel,
        grid_spec=pltpu.PrefetchScalarGridSpec(
            num_scalar_prefetch=1,
            grid=(width // tile,),
            in_specs=[
                pl.BlockSpec((tokens, depth), lambda i, s: (0, 0)),
                pl.BlockSpec((tile, depth), lambda i, s: (s[0] * (width // tile) + i, 0)),
            ],
            out_specs=pl.BlockSpec((tokens, tile), lambda i, s: (0, i)),
        ),
        out_shape=jax.ShapeDtypeStruct((tokens, width), dtype),
        compiler_params=pltpu.CompilerParams(vmem_limit_bytes=VMEM_BYTES),
        cost_estimate=cost(2 * tokens * depth * width, 2 * width * depth + 4 * tokens * width),
        name="act_grad_piece",
    )(start, grads, weight_out)


def input_grad_piece(where, mine, other, weight_in, total, dtype):
    tokens, width = mine.shape
    out = weight_in.shape[0]
    tile = tile_of(out, 512)

    def kernel(_, m_ref, o_ref, wm_ref, wo_ref, *refs):
        dims = (((1,), (1,)), ((), ()))
        value = lax.dot_general(m_ref[...], wm_ref[...], dims, preferred_element_type=jnp.float32)
        value += lax.dot_general(o_ref[...], wo_ref[...], dims, preferred_element_type=jnp.float32)
        if len(refs) > 1:
            value += refs[0][...]
        refs[-1][...] = value.astype(dtype)

    block = pl.BlockSpec((tokens, tile), lambda i, s: (0, i))
    held = pl.BlockSpec((tokens, width), lambda i, s: (0, 0))
    return pl.pallas_call(
        kernel,
        grid_spec=pltpu.PrefetchScalarGridSpec(
            num_scalar_prefetch=1,
            grid=(out // tile,),
            in_specs=[
                held,
                held,
                pl.BlockSpec((tile, width), lambda i, s: (i, s[0])),
                pl.BlockSpec((tile, width), lambda i, s: (i, s[1])),
            ]
            + ([] if total is None else [block]),
            out_specs=block,
        ),
        out_shape=jax.ShapeDtypeStruct((tokens, out), dtype),
        compiler_params=pltpu.CompilerParams(vmem_limit_bytes=VMEM_BYTES),
        cost_estimate=cost(4 * tokens * width * out, 4 * width * out + 8 * tokens * out),
        name="input_grad_piece",
    )(where, mine, other, weight_in, weight_in, *([] if total is None else [total]))


def weight_out_grad_piece(act, grads, part, parts, held):
    tokens, rows = act.shape
    columns = grads.shape[1]
    share = rows // parts
    tile = tile_of(share, 512)
    first = part * (share // tile)

    def kernel(a_ref, g_ref, *refs):
        refs[-1][...] = lax.dot_general(
            a_ref[...], g_ref[...], (((0,), (0,)), ((), ())), preferred_element_type=jnp.float32
        ).astype(jnp.bfloat16)

    return pl.pallas_call(
        kernel,
        grid=(share // tile,),
        in_specs=[
            pl.BlockSpec((tokens, tile), lambda i: (0, first + i)),
            pl.BlockSpec((tokens, columns), lambda i: (0, 0)),
        ]
        + ([] if held is None else [pl.BlockSpec(memory_space=pl.ANY)]),
        out_specs=pl.BlockSpec((tile, columns), lambda i: (first + i, 0)),
        out_shape=jax.ShapeDtypeStruct((rows, columns), jnp.bfloat16),
        input_output_aliases={} if held is None else {2: 0},
        compiler_params=pltpu.CompilerParams(vmem_limit_bytes=VMEM_BYTES),
        cost_estimate=cost(2 * tokens * share * columns, 2 * share * columns + 2 * tokens * columns),
        name="weight_out_grad_piece",
    )(act, grads, *([] if held is None else [held]))


def weight_in_grad_piece(where, inputs, hid_pieces, part, parts, held):
    tokens, rows = inputs.shape
    count = len(hid_pieces)
    width = hid_pieces[0].shape[1]
    columns = width * count
    share = rows // parts
    tile = tile_of(share, 512)
    first = part * (share // tile)

    def kernel(where_ref, i_ref, *refs):
        left = i_ref[...].T
        for index in range(count):
            at = pl.multiple_of(where_ref[index] * width, 128)
            refs[-1][:, pl.ds(at, width)] = jnp.dot(
                left, refs[index][...], preferred_element_type=jnp.float32
            ).astype(jnp.bfloat16)

    return pl.pallas_call(
        kernel,
        grid_spec=pltpu.PrefetchScalarGridSpec(
            num_scalar_prefetch=1,
            grid=(share // tile,),
            in_specs=[pl.BlockSpec((tokens, tile), lambda i, s: (0, first + i))]
            + [pl.BlockSpec((tokens, width), lambda i, s: (0, 0))] * count
            + ([] if held is None else [pl.BlockSpec(memory_space=pl.ANY)]),
            out_specs=pl.BlockSpec((tile, columns), lambda i, s: (first + i, 0)),
        ),
        out_shape=jax.ShapeDtypeStruct((rows, columns), jnp.bfloat16),
        input_output_aliases={} if held is None else {2 + count: 0},
        compiler_params=pltpu.CompilerParams(vmem_limit_bytes=VMEM_BYTES),
        cost_estimate=cost(2 * tokens * share * columns, 2 * share * columns + 4 * tokens * columns),
        name="weight_in_grad_piece",
    )(where, inputs, *hid_pieces, *([] if held is None else [held]))


def body(cycle, inputs, hidden_pre, out_grad, weight_in, weight_out):
    cols = lax.axis_size("col")
    core = lax.axis_index("col") % 2
    twin = [(i, i ^ 1) for i in range(cols)]
    hops = [[(i, (i + 2 * hop) % cols) for i in range(cols)] for hop in range(1, cols // 2)]
    rows = len(cycle)
    place = lax.axis_index("row")
    order = [
        sum(jnp.where(place == row, cycle[(spot + shift) % rows], 0) for spot, row in enumerate(cycle))
        for shift in range(rows)
    ]
    half = hidden_pre.shape[1] // 2
    parts = pieces_of(half, 2)
    width = half // parts

    def at(*indices):
        return jnp.stack(indices).astype(jnp.int32)

    cut = out_grad.shape[1] // 2
    lanes = [ring_gather(out_grad[:, :cut], cycle), ring_gather(out_grad[:, cut:], cycle)]
    order = at(*order, core)
    gelu, runs = None, max(n for n in (1, 2) if rows % n == 0)
    for k in range(1, rows // 2 + 1):
        for step, _ in lanes:
            step(k)
        if k <= runs:
            gelu = gelu_piece(order, hidden_pre, rows, k - 1, runs, gelu)
    grad_all = jnp.concatenate([whole() for _, whole in lanes], 1)
    act, slope = gelu
    grad_all, act, slope = lax.optimization_barrier((grad_all, act, slope))
    input_step, input_whole = ring_gather(inputs, cycle)
    due = list(range(1, rows // 2 + 1))

    def input_steps(count, *others):
        for _ in range(min(count, len(due))):
            input_step(due.pop(0), *others)

    sums, arrived, last = [], [], grad_all
    for part in range(parts):
        start = after(at((1 - core) * parts + part), last)
        given = act_grad_piece(start, grad_all, weight_out, width, jnp.bfloat16)
        taken = lax.ppermute(given, "col", twin)
        start = after(at(core * parts + part), given)
        kept = act_grad_piece(start, grad_all, weight_out, width, jnp.float32)
        total = kept + taken.astype(jnp.float32)
        last = total.astype(jnp.bfloat16)
        if part == 0:
            input_steps(rows // 8, given)
        sums.append(total)
        arrived.append([lax.ppermute(last, "col", hop) for hop in hops])

    input_steps(rows // 8, last)
    grad_weight_out = weight_out_grad_piece(after(act, last), grad_all, 0, 2, None)

    hid_pieces, where, partial = [], [], None
    for part in range(parts):
        if part == 0:
            arrived[part], grad_weight_out = lax.optimization_barrier((arrived[part], grad_weight_out))
        else:
            arrived[part], partial = lax.optimization_barrier((arrived[part], partial))
        total = sums[part]
        for value in arrived[part]:
            total = total + value.astype(jnp.float32)
        mine = (total * slope[:, part * width : (part + 1) * width]).astype(jnp.bfloat16)
        other = lax.ppermute(mine, "col", twin)
        here = [core * parts + part, (1 - core) * parts + part]
        place_here = at(*here)
        if part == 0:
            input_steps(rows // 8, mine)
            grad_weight_out = weight_out_grad_piece(after(act, mine), grad_all, 1, 2, grad_weight_out)
            place_here, grad_weight_out = lax.optimization_barrier((place_here, grad_weight_out))
        if part == 0:
            input_steps(rows, place_here)
        partial = input_grad_piece(place_here, mine, other, weight_in, partial, jnp.float32)
        hid_pieces += [mine, other]
        where += here

    input_all = input_whole()

    tiles = inputs.shape[1] // tile_of(inputs.shape[1], 512)
    slots = max(n for n in range(1, 4) if tiles % n == 0)
    state = {"next": 0, "grad": None}

    def fill(sent, received):
        if state["next"] == slots:
            return received
        state["grad"] = weight_in_grad_piece(
            after(at(*where), *sent), input_all, hid_pieces, state["next"], slots, state["grad"]
        )
        state["next"] += 1
        received, state["grad"] = lax.optimization_barrier((received, state["grad"]))
        return received

    grad_in = ring_sum(partial, cycle, jnp.bfloat16, fill)
    while state["next"] < slots:
        fill([], [])
    return (grad_in, state["grad"], grad_weight_out)


def solution(mesh):
    return jax.shard_map(
        functools.partial(body, row_cycle(mesh)),
        mesh=mesh,
        in_specs=(
            P("row", "col"),
            P(None, "row"),
            P("row", "col"),
            P("col", "row"),
            P("row", "col"),
        ),
        out_specs=(P("row", "col"), P("col", "row"), P("row", "col")),
        check_vma=False,
    )
```

time: 373 us -> 182 us (0.49)
  waiting for transfers between devices: 247 us -> 24.9 us
  Pallas kernels: 0 us -> 95.1 us
  matrix products: 65.2 us -> 0 us
  starting transfers between devices: 0.38 us -> 37 us
  local copies, waits for them, and re-layouts: 26.6 us -> 10.7 us
  between operations: 13.8 us -> 1.05 us
  other arithmetic: 19.6 us -> 12.1 us
    all_gather x3 -> x0, waiting for transfers between devices: 123 us -> none  [the longest x1 65.4 us: body(): lax.all_gather(out_grad, 'row', axis=0, tiled=True)]
    reduce_scatter x2 -> x0, waiting for transfers between devices: 122 us -> none  [the longest x1 79.4 us: body(): lax.psum_scatter(contract_cols(piece, weight_in), 'row', scatter_dimensio...]
    pallas_call x0 -> x13, Pallas kernels: none -> 95.1 us  [the longest x2 23 us: input_grad_piece(): pl.pallas_call(kernel, grid_spec=pltpu.PrefetchScalarGridSpec(num_scalar_...]
    dot_general x4 -> x0, matrix products: 65.2 us -> none  [the longest x2 32.8 us: contract_cols(): lax.dot_general(left, right, (((1,), (1,)), ((), ())), preferred_element_...]
    ppermute x0 -> x38, starting transfers between devices: none -> 37 us  [the longest x12 19.8 us: step(): lax.ppermute(fore, 'row', ahead)]
    ppermute x0 -> x38, waiting for transfers between devices: none -> 24.9 us  [the longest x12 12.5 us: step(): lax.ppermute(fore, 'row', ahead)]
    unnamed x3 -> x44, local copies, waits for them, and re-layouts: 26.6 us -> 8.06 us
    tanh x1 -> x0, other arithmetic: 8.74 us -> none  [gelu_parts(): tval = jnp.tanh(inner)]
  transfers between devices with their start and end apart: 5 -> 38, of which waited for: 5 -> 16; matrix products, arithmetic and copies ran while one was open for 23% -> 6% of each run, Pallas kernels for 0% -> 42%
where the time goes in v1:
time: 182 us; the launch traced here: 181 us
  Pallas kernels  95.1 us (52%)
  starting transfers between devices  37 us (20%)
  waiting for transfers between devices  24.9 us (14%)
  other arithmetic  12.1 us (7%)
  local copies, waits for them, and re-layouts  10.7 us (6%)
    pallas_call x2, Pallas kernels, input_grad_piece(): pl.pallas_call(kernel, grid_spec=pltpu.PrefetchScalarGridSpec(num_scalar_...  23 us
    pallas_call x3, Pallas kernels, weight_in_grad_piece(): pl.pallas_call(kernel, grid_spec=pltpu.PrefetchScalarGridSpec(num_scalar_...  21.9 us
    pallas_call x4, Pallas kernels, act_grad_piece(): pl.pallas_call(kernel, grid_spec=pltpu.PrefetchScalarGridSpec(num_scalar_...  21.5 us
    ppermute x12, starting transfers between devices, step(): lax.ppermute(fore, 'row', ahead)  19.8 us
    pallas_call x2, Pallas kernels, weight_out_grad_piece(): pl.pallas_call(kernel, grid=(share // tile,), in_specs=[pl.BlockSpec((tok...  18.3 us
    ppermute x12, waiting for transfers between devices, step(): lax.ppermute(fore, 'row', ahead)  12.5 us
    pallas_call x2, Pallas kernels, gelu_piece(): pl.pallas_call(kernel, grid_spec=pltpu.PrefetchScalarGridSpec(num_scalar_...  10.4 us
    ppermute x4, waiting for transfers between devices, move(): lax.ppermute(sent[0], 'row', ahead)  8.5 us
  transfers between devices with their start and end apart: 38, of which 16 were waited for; matrix products, arithmetic and copies ran while one was open for 6% of the time, Pallas kernels for 42%

profile of v1, /device:TPU:0, one launch (start us, length us, event | category | flops | bytes accessed | tf_op | source)
XLA Modules:
  0.0 180.9 jit_solution(5647600892080349297)
XLA Ops:
  0.6 1.8 fusion.11
  2.4 3.0 %collective-permute-start.3 = (bf16[64,1536]{1,0:T(8,128)(2,1)S(1)}, bf16[64,1536]{1,0:T(8,128)(2,1)S(1)}, u32[]{:S(2)}, u32[]{:S(2)}) collective-permute-start(bf16[64,1536]{1,0:T(8,128)(2,1)S(1)} %get-tuple-element.91), channel_id=1, source_target_pairs={{4,12},{12,20},{20,28},{28,24},{24,16},{16,8},{8,0},{0,4},{5,13},{... | collective-permute-start | bytes 589832 | tf_op jit(solution)/shard_map/ppermute | solution.py:105
  5.4 2.0 %collective-permute-start.11 = (bf16[64,1536]{1,0:T(8,128)(2,1)S(1)}, bf16[64,1536]{1,0:T(8,128)(2,1)S(1)}, u32[]{:S(2)}, u32[]{:S(2)}) collective-permute-start(bf16[64,1536]{1,0:T(8,128)(2,1)S(1)} %get-tuple-element.94), channel_id=1, source_target_pairs={{4,12},{12,20},{20,28},{28,24},{24,16},{16,8},{8,0},{0,4},{5,13},{... | collective-permute-start | bytes 589832 | tf_op jit(solution)/shard_map/ppermute | solution.py:105
  7.5 5.2 %gelu_piece.2 = (bf16[512,3072]{1,0:T(8,128)(2,1)S(1)}, f32[512,1536]{1,0:T(8,128)}) custom-call(s32[9]{0:T(128)S(1)} %stack.83.order_ref, bf16[512,3072]{1,0:T(8,128)(2,1)} %h_ref.3), custom_call_target="tpu_custom_call" | custom-call | flops 15728640 | bytes 4718592 | tf_op jit(solution)/shard_map/gelu_piece/pallas_call | solution.py:64
  12.7 5.2 %gelu_piece.3 = (bf16[512,3072]{1,0:T(8,128)(2,1)S(1)}, f32[512,1536]{1,0:T(8,128)}) custom-call(s32[9]{0:T(128)S(1)} %stack.83.order_ref, bf16[512,3072]{1,0:T(8,128)(2,1)} %h_ref.3, bf16[512,3072]{1,0:T(8,128)(2,1)S(1)} %get-tuple-element.42.refs_0_, f32[512,1536]{1,0:T(8,128)} %get-tuple-element.43.refs_1_), custom_call_target="tpu_custom_call", output_to_operand_aliasing={{0}: (2, {}), {1}: (3, {})} | custom-call | flops 15728640 | bytes 4718592 | tf_op jit(solution)/shard_map/gelu_piece/pallas_call | solution.py:64
  17.9 2.0 %collective-permute-start.4 = (bf16[64,1536]{1,0:T(8,128)(2,1)S(1)}, bf16[64,1536]{1,0:T(8,128)(2,1)S(1)}, u32[]{:S(2)}, u32[]{:S(2)}) collective-permute-start(bf16[64,1536]{1,0:T(8,128)(2,1)S(1)} %collective-permute-done.3), channel_id=1, source_target_pairs={{4,12},{12,20},{20,28},{28,24},{24,16},{16,8},{8,0},{0,4},{5,13},{... | collective-permute-start | bytes 589832 | tf_op jit(solution)/shard_map/ppermute | solution.py:105
  20.0 1.9 %collective-permute-start.12 = (bf16[64,1536]{1,0:T(8,128)(2,1)S(1)}, bf16[64,1536]{1,0:T(8,128)(2,1)S(1)}, u32[]{:S(2)}, u32[]{:S(2)}) collective-permute-start(bf16[64,1536]{1,0:T(8,128)(2,1)S(1)} %collective-permute-done.11), channel_id=1, source_target_pairs={{4,12},{12,20},{20,28},{28,24},{24,16},{16,8},{8,0},{0,4},{5,13},{... | collective-permute-start | bytes 589832 | tf_op jit(solution)/shard_map/ppermute | solution.py:105
  22.8 2.9 %collective-permute-done.4 = bf16[64,1536]{1,0:T(8,128)(2,1)S(1)} collective-permute-done((bf16[64,1536]{1,0:T(8,128)(2,1)S(1)}, bf16[64,1536]{1,0:T(8,128)(2,1)S(1)}, u32[]{:S(2)}, u32[]{:S(2)}) %collective-permute-start.4) | collective-permute-done | bytes 196640 | tf_op jit(solution)/shard_map/ppermute | solution.py:105
  25.7 2.0 %collective-permute-start.5 = (bf16[64,1536]{1,0:T(8,128)(2,1)S(1)}, bf16[64,1536]{1,0:T(8,128)(2,1)S(1)}, u32[]{:S(2)}, u32[]{:S(2)}) collective-permute-start(bf16[64,1536]{1,0:T(8,128)(2,1)S(1)} %collective-permute-done.4), channel_id=1, source_target_pairs={{4,12},{12,20},{20,28},{28,24},{24,16},{16,8},{8,0},{0,4},{5,13},{... | collective-permute-start | bytes 589832 | tf_op jit(solution)/shard_map/ppermute | solution.py:105
  27.8 2.1 %collective-permute-done.12 = bf16[64,1536]{1,0:T(8,128)(2,1)S(1)} collective-permute-done((bf16[64,1536]{1,0:T(8,128)(2,1)S(1)}, bf16[64,1536]{1,0:T(8,128)(2,1)S(1)}, u32[]{:S(2)}, u32[]{:S(2)}) %collective-permute-start.12) | collective-permute-done | bytes 196640 | tf_op jit(solution)/shard_map/ppermute | solution.py:105
  30.0 2.0 %collective-permute-start.13 = (bf16[64,1536]{1,0:T(8,128)(2,1)S(1)}, bf16[64,1536]{1,0:T(8,128)(2,1)S(1)}, u32[]{:S(2)}, u32[]{:S(2)}) collective-permute-start(bf16[64,1536]{1,0:T(8,128)(2,1)S(1)} %collective-permute-done.12), channel_id=1, source_target_pairs={{4,12},{12,20},{20,28},{28,24},{24,16},{16,8},{8,0},{0,4},{5,13},{... | collective-permute-start | bytes 589832 | tf_op jit(solution)/shard_map/ppermute | solution.py:105
  34.2 2.0 %collective-permute-start.6 = (bf16[32,1536]{1,0:T(8,128)(2,1)S(1)}, bf16[32,1536]{1,0:T(8,128)(2,1)S(1)}, u32[]{:S(2)}, u32[]{:S(2)}) collective-permute-start(bf16[32,1536]{1,0:T(8,128)(2,1)S(1)} %slice.97), channel_id=1, source_target_pairs={{4,12},{12,20},{20,28},{28,24},{24,16},{16,8},{8,0},{0,4},{5,13},{... | collective-permute-start | bytes 294920 | tf_op jit(solution)/shard_map/ppermute | solution.py:105
  37.7 2.0 %collective-permute-start.14 = (bf16[32,1536]{1,0:T(8,128)(2,1)S(1)}, bf16[32,1536]{1,0:T(8,128)(2,1)S(1)}, u32[]{:S(2)}, u32[]{:S(2)}) collective-permute-start(bf16[32,1536]{1,0:T(8,128)(2,1)S(1)} %slice.99), channel_id=1, source_target_pairs={{4,12},{12,20},{20,28},{28,24},{24,16},{16,8},{8,0},{0,4},{5,13},{... | collective-permute-start | bytes 294920 | tf_op jit(solution)/shard_map/ppermute | solution.py:105
  47.1 2.2 %pad_maximum_fusion.g_ref = bf16[512,3072]{1,0:T(8,128)(2,1)S(1)} fusion(bf16[512,1536]{1,0:T(8,128)(2,1)} %constant_dynamic-update-slice_fusion.9, bf16[512,1536]{1,0:T(8,128)(2,1)} %copy-done.5), kind=kLoop, calls=%fused_computation | loop fusion | flops 6291456 | bytes 6291456 | tf_op jit(solution)/shard_map/concatenate | solution.py:313
  49.3 6.8 %act_grad_piece.4 = bf16[512,768]{1,0:T(8,128)(2,1)} custom-call(s32[1]{0:T(128)} %bitcast.3._, bf16[512,3072]{1,0:T(8,128)(2,1)S(1)} %pad_maximum_fusion.g_ref, bf16[3072,3072]{1,0:T(8,128)(2,1)} %w_ref.7), custom_call_target="tpu_custom_call" | custom-call | flops 2415919104 | bytes 6291456 | tf_op jit(solution)/shard_map/act_grad_piece/pallas_call | solution.py:168
  57.9 4.9 %act_grad_piece.5 = f32[512,768]{1,0:T(8,128)S(1)} custom-call(s32[1]{0:T(128)} %bitcast.2._, bf16[512,3072]{1,0:T(8,128)(2,1)S(1)} %pad_maximum_fusion.g_ref, bf16[3072,3072]{1,0:T(8,128)(2,1)} %w_ref.7), custom_call_target="tpu_custom_call" | custom-call | flops 2415919104 | bytes 6291456 | tf_op jit(solution)/shard_map/act_grad_piece/pallas_call | solution.py:168
  64.2 4.9 %act_grad_piece.6 = bf16[512,768]{1,0:T(8,128)(2,1)S(1)} custom-call(s32[1]{0:T(128)} %bitcast.1._, bf16[512,3072]{1,0:T(8,128)(2,1)S(1)} %pad_maximum_fusion.g_ref, bf16[3072,3072]{1,0:T(8,128)(2,1)} %w_ref.7), custom_call_target="tpu_custom_call" | custom-call | flops 2415919104 | bytes 6291456 | tf_op jit(solution)/shard_map/act_grad_piece/pallas_call | solution.py:168
  72.6 4.9 %act_grad_piece.7 = f32[512,768]{1,0:T(8,128)S(1)} custom-call(s32[1]{0:T(128)} %bitcast._, bf16[512,3072]{1,0:T(8,128)(2,1)S(1)} %pad_maximum_fusion.g_ref, bf16[3072,3072]{1,0:T(8,128)(2,1)} %w_ref.7), custom_call_target="tpu_custom_call" | custom-call | flops 2415919104 | bytes 6291456 | tf_op jit(solution)/shard_map/act_grad_piece/pallas_call | solution.py:168
  78.4 2.7 %collective-permute-done.25 = bf16[64,3072]{1,0:T(8,128)(2,1)S(1)} collective-permute-done((bf16[64,3072]{1,0:T(8,128)(2,1)}, bf16[64,3072]{1,0:T(8,128)(2,1)S(1)}, u32[]{:S(2)}, u32[]{:S(2)}) %collective-permute-start.25) | collective-permute-done | bytes 393248 | tf_op jit(solution)/shard_map/ppermute | solution.py:105
  83.1 9.2 %weight_out_grad_piece.2.refs_0_ = bf16[3072,3072]{1,0:T(8,128)(2,1)} custom-call(bf16[512,3072]{1,0:T(8,128)(2,1)S(1)} %copy-done.2, bf16[512,3072]{1,0:T(8,128)(2,1)} %copy-done), custom_call_target="tpu_custom_call" | custom-call | flops 4831838208 | bytes 12582912 | tf_op jit(solution)/shard_map/weight_out_grad_piece/pallas_call | solution.py:234
  92.3 1.9 %multiply_convert_fusion.1.m_ref.refs_0_ = bf16[512,768]{1,0:T(8,128)(2,1)S(1)} fusion(f32[512,1536]{1,0:T(8,128)S(1)} %copy-done.4, bf16[512,768]{1,0:T(8,128)(2,1)} %collective-permute-done.19, f32[512,768]{1,0:T(8,128)S(1)} %act_grad_piece.5, bf16[512,768]{1,0:T(8,128)(2,1)} %collective-permute-done.16), kind=kLoop, calls=%fused_computation.2 | loop fusion | flops 2359296 | bytes 5505024 | tf_op jit(solution)/shard_map/convert_element_type | solution.py:349
  94.2 1.6 collective-permute-start.28
  96.3 9.2 %weight_out_grad_piece.3 = bf16[3072,3072]{1,0:T(8,128)(2,1)} custom-call(bf16[512,3072]{1,0:T(8,128)(2,1)S(1)} %copy-done.2, bf16[512,3072]{1,0:T(8,128)(2,1)} %copy-done, bf16[3072,3072]{1,0:T(8,128)(2,1)} %weight_out_grad_piece.2.refs_0_), custom_call_target="tpu_custom_call", output_to_operand_aliasing={{}: (2, {})} | custom-call | flops 4831838208 | bytes 12582912 | tf_op jit(solution)/shard_map/weight_out_grad_piece/pallas_call | solution.py:234
  109.4 10.7 %input_grad_piece.2.refs_0_ = f32[512,3072]{1,0:T(8,128)} custom-call(s32[2]{0:T(128)S(1)} %pad_add_fusion.1._, bf16[512,768]{1,0:T(8,128)(2,1)S(1)} %multiply_convert_fusion.1.m_ref.refs_0_, bf16[512,768]{1,0:T(8,128)(2,1)S(1)} %collective-permute-done.20.o_ref.refs_1_, bf16[3072,3072]{1,0:T(8,128)(2,1)} %wo_ref.3, bf16[3072,3072]{1,0:T(8,128)(2,1)} %wo_ref.3), custom_call_target="tpu_custom_call" | custom-call | flops 4831838208 | bytes 22020096 | tf_op jit(solution)/shard_map/input_grad_piece/pallas_call | solution.py:201
  120.1 1.6 multiply_convert_fusion.m_ref.refs_2_
  124.1 12.2 %input_grad_piece.3 = f32[512,3072]{1,0:T(8,128)} custom-call(s32[2]{0:T(128)S(1)} %pad_add_fusion._, bf16[512,768]{1,0:T(8,128)(2,1)S(1)} %multiply_convert_fusion.m_ref.refs_2_, bf16[512,768]{1,0:T(8,128)(2,1)S(1)} %collective-permute-done.21.o_ref.refs_3_, bf16[3072,3072]{1,0:T(8,128)(2,1)} %wo_ref.3, bf16[3072,3072]{1,0:T(8,128)(2,1)} %wo_ref.3, ...), custom_call_target="tpu_custom_call" | custom-call | flops 4831838208 | bytes 22020096 | tf_op jit(solution)/shard_map/input_grad_piece/pallas_call | solution.py:201
  136.3 3.2 %convert.14 = bf16[512,3072]{1,0:T(8,128)(2,1)S(1)} convert(f32[512,3072]{1,0:T(8,128)} %input_grad_piece.3) | non-fusion elementwise | flops 1572864 | bytes 9437184 | tf_op jit(solution)/shard_map/convert.7
  139.6 1.6 collective-permute-start.23
  141.7 7.6 %weight_in_grad_piece.3.refs_4_ = bf16[3072,3072]{1,0:T(8,128)(2,1)} custom-call(s32[4]{0:T(128)S(1)} %pad_add_fusion.2.where_ref, bf16[512,3072]{1,0:T(8,128)(2,1)} %copy-done.3, bf16[512,768]{1,0:T(8,128)(2,1)S(1)} %multiply_convert_fusion.1.m_ref.refs_0_, bf16[512,768]{1,0:T(8,128)(2,1)S(1)} %collective-permute-done.20.o_ref.refs_1_, ...), custom_call_target="tpu_custom_call" | custom-call | flops 3221225472 | bytes 12582912 | tf_op jit(solution)/shard_map/weight_in_grad_piece/pallas_call | solution.py:268
  151.7 7.1 %weight_in_grad_piece.4.refs_4_ = bf16[3072,3072]{1,0:T(8,128)(2,1)} custom-call(s32[4]{0:T(128)S(1)} %pad_add_fusion.2.where_ref, bf16[512,3072]{1,0:T(8,128)(2,1)} %copy-done.3, bf16[512,768]{1,0:T(8,128)(2,1)S(1)} %multiply_convert_fusion.1.m_ref.refs_0_, ...), custom_call_target="tpu_custom_call", output_to_operand_aliasing={{}: (6, {})} | custom-call | flops 3221225472 | bytes 12582912 | tf_op jit(solution)/shard_map/weight_in_grad_piece/pallas_call | solution.py:268
  162.9 7.2 %weight_in_grad_piece.5 = bf16[3072,3072]{1,0:T(8,128)(2,1)} custom-call(s32[4]{0:T(128)S(1)} %pad_add_fusion.2.where_ref, bf16[512,3072]{1,0:T(8,128)(2,1)} %copy-done.3, bf16[512,768]{1,0:T(8,128)(2,1)S(1)} %multiply_convert_fusion.1.m_ref.refs_0_, bf16[512,768]{1,0:T(8,128)(2,1)S(1)} %collective-permute-done.20.o_ref.refs_1_, ...), custom_call_target="tpu_custom_call", output_to_operand_aliasing={{}: (6, {})} | custom-call | flops 3221225472 | bytes 12582912 | tf_op jit(solution)/shard_map/weight_in_grad_piece/pallas_call | solution.py:268
  173.4 6.2 %collective-permute-done.36 = bf16[64,3072]{1,0:T(8,128)(2,1)S(1)} collective-permute-done((bf16[64,3072]{1,0:T(8,128)(2,1)S(1)}, bf16[64,3072]{1,0:T(8,128)(2,1)S(1)}, u32[]{:S(2)}, u32[]{:S(2)}) %collective-permute-start.36) | collective-permute-done | bytes 393248 | tf_op jit(solution)/shard_map/ppermute | solution.py:131
  (129 shorter events, 40.1 us)
Async XLA Ops:
  2.4 15.5 %collective-permute-start.3 = (bf16[64,1536]{1,0:T(8,128)(2,1)S(1)}, bf16[64,1536]{1,0:T(8,128)(2,1)S(1)}, u32[]{:S(2)}, u32[]{:S(2)}) collective-permute-start(bf16[64,1536]{1,0:T(8,128)(2,1)S(1)} %get-tuple-element.91), channel_id=1, source_target_pairs={{4,12},{12,20},{20,28},{28,24},{24,16},{16,8},{8,0},{0,4},{5,13},{... | collective-permute-start | bytes 589832 | tf_op jit(solution)/shard_map/ppermute | solution.py:105
  5.4 14.5 %collective-permute-start = (bf16[64,1536]{1,0:T(8,128)(2,1)S(1)}, bf16[64,1536]{1,0:T(8,128)(2,1)S(1)}, u32[]{:S(2)}, u32[]{:S(2)}) collective-permute-start(bf16[64,1536]{1,0:T(8,128)(2,1)S(1)} %get-tuple-element.91), channel_id=1, source_target_pairs={{12,4},{20,12},{28,20},{24,28},{16,24},{8,16},{0,8},{4,0},{13,5},{... | collective-permute-start | bytes 589832 | tf_op jit(solution)/shard_map/ppermute | solution.py:105
  5.4 14.6 %collective-permute-start.11 = (bf16[64,1536]{1,0:T(8,128)(2,1)S(1)}, bf16[64,1536]{1,0:T(8,128)(2,1)S(1)}, u32[]{:S(2)}, u32[]{:S(2)}) collective-permute-start(bf16[64,1536]{1,0:T(8,128)(2,1)S(1)} %get-tuple-element.94), channel_id=1, source_target_pairs={{4,12},{12,20},{20,28},{28,24},{24,16},{16,8},{8,0},{0,4},{5,13},{... | collective-permute-start | bytes 589832 | tf_op jit(solution)/shard_map/ppermute | solution.py:105
  7.4 14.5 %collective-permute-start.8 = (bf16[64,1536]{1,0:T(8,128)(2,1)S(1)}, bf16[64,1536]{1,0:T(8,128)(2,1)S(1)}, u32[]{:S(2)}, u32[]{:S(2)}) collective-permute-start(bf16[64,1536]{1,0:T(8,128)(2,1)S(1)} %get-tuple-element.94), channel_id=1, source_target_pairs={{12,4},{20,12},{28,20},{24,28},{16,24},{8,16},{0,8},{4,0},{13,5},{... | collective-permute-start | bytes 589832 | tf_op jit(solution)/shard_map/ppermute | solution.py:105
  17.9 7.8 %collective-permute-start.4 = (bf16[64,1536]{1,0:T(8,128)(2,1)S(1)}, bf16[64,1536]{1,0:T(8,128)(2,1)S(1)}, u32[]{:S(2)}, u32[]{:S(2)}) collective-permute-start(bf16[64,1536]{1,0:T(8,128)(2,1)S(1)} %collective-permute-done.3), channel_id=1, source_target_pairs={{4,12},{12,20},{20,28},{28,24},{24,16},{16,8},{8,0},{0,4},{5,13},{... | collective-permute-start | bytes 589832 | tf_op jit(solution)/shard_map/ppermute | solution.py:105
  19.9 7.8 %collective-permute-start.1 = (bf16[64,1536]{1,0:T(8,128)(2,1)S(1)}, bf16[64,1536]{1,0:T(8,128)(2,1)S(1)}, u32[]{:S(2)}, u32[]{:S(2)}) collective-permute-start(bf16[64,1536]{1,0:T(8,128)(2,1)S(1)} %collective-permute-done), channel_id=1, source_target_pairs={{12,4},{20,12},{28,20},{24,28},{16,24},{8,16},{0,8},{4,0},{13,5},{... | collective-permute-start | bytes 589832 | tf_op jit(solution)/shard_map/ppermute | solution.py:105
  20.0 10.0 %collective-permute-start.12 = (bf16[64,1536]{1,0:T(8,128)(2,1)S(1)}, bf16[64,1536]{1,0:T(8,128)(2,1)S(1)}, u32[]{:S(2)}, u32[]{:S(2)}) collective-permute-start(bf16[64,1536]{1,0:T(8,128)(2,1)S(1)} %collective-permute-done.11), channel_id=1, source_target_pairs={{4,12},{12,20},{20,28},{28,24},{24,16},{16,8},{8,0},{0,4},{5,13},{... | collective-permute-start | bytes 589832 | tf_op jit(solution)/shard_map/ppermute | solution.py:105
  21.9 10.0 %collective-permute-start.9 = (bf16[64,1536]{1,0:T(8,128)(2,1)S(1)}, bf16[64,1536]{1,0:T(8,128)(2,1)S(1)}, u32[]{:S(2)}, u32[]{:S(2)}) collective-permute-start(bf16[64,1536]{1,0:T(8,128)(2,1)S(1)} %collective-permute-done.8), channel_id=1, source_target_pairs={{12,4},{20,12},{28,20},{24,28},{16,24},{8,16},{0,8},{4,0},{13,5},{... | collective-permute-start | bytes 589832 | tf_op jit(solution)/shard_map/ppermute | solution.py:105
  25.7 8.4 %collective-permute-start.5 = (bf16[64,1536]{1,0:T(8,128)(2,1)S(1)}, bf16[64,1536]{1,0:T(8,128)(2,1)S(1)}, u32[]{:S(2)}, u32[]{:S(2)}) collective-permute-start(bf16[64,1536]{1,0:T(8,128)(2,1)S(1)} %collective-permute-done.4), channel_id=1, source_target_pairs={{4,12},{12,20},{20,28},{28,24},{24,16},{16,8},{8,0},{0,4},{5,13},{... | collective-permute-start | bytes 589832 | tf_op jit(solution)/shard_map/ppermute | solution.py:105
  27.7 8.5 %collective-permute-start.2 = (bf16[64,1536]{1,0:T(8,128)(2,1)S(1)}, bf16[64,1536]{1,0:T(8,128)(2,1)S(1)}, u32[]{:S(2)}, u32[]{:S(2)}) collective-permute-start(bf16[64,1536]{1,0:T(8,128)(2,1)S(1)} %collective-permute-done.1), channel_id=1, source_target_pairs={{12,4},{20,12},{28,20},{24,28},{16,24},{8,16},{0,8},{4,0},{13,5},{... | collective-permute-start | bytes 589832 | tf_op jit(solution)/shard_map/ppermute | solution.py:105
  30.0 7.7 %collective-permute-start.13 = (bf16[64,1536]{1,0:T(8,128)(2,1)S(1)}, bf16[64,1536]{1,0:T(8,128)(2,1)S(1)}, u32[]{:S(2)}, u32[]{:S(2)}) collective-permute-start(bf16[64,1536]{1,0:T(8,128)(2,1)S(1)} %collective-permute-done.12), channel_id=1, source_target_pairs={{4,12},{12,20},{20,28},{28,24},{24,16},{16,8},{8,0},{0,4},{5,13},{... | collective-permute-start | bytes 589832 | tf_op jit(solution)/shard_map/ppermute | solution.py:105
  31.9 7.7 %collective-permute-start.10 = (bf16[64,1536]{1,0:T(8,128)(2,1)S(1)}, bf16[64,1536]{1,0:T(8,128)(2,1)S(1)}, u32[]{:S(2)}, u32[]{:S(2)}) collective-permute-start(bf16[64,1536]{1,0:T(8,128)(2,1)S(1)} %collective-permute-done.9), channel_id=1, source_target_pairs={{12,4},{20,12},{28,20},{24,28},{16,24},{8,16},{0,8},{4,0},{13,5},{... | collective-permute-start | bytes 589832 | tf_op jit(solution)/shard_map/ppermute | solution.py:105
  57.2 13.7 %collective-permute-start.24 = (bf16[64,3072]{1,0:T(8,128)(2,1)}, bf16[64,3072]{1,0:T(8,128)(2,1)S(1)}, u32[]{:S(2)}, u32[]{:S(2)}) collective-permute-start(bf16[64,3072]{1,0:T(8,128)(2,1)} %param.5), channel_id=1, source_target_pairs={{12,4},{20,12},{28,20},{24,28},{16,24},{8,16},{0,8},{4,0},{13,5},{... | collective-permute-start | bytes 1179656 | tf_op jit(solution)/shard_map/ppermute | solution.py:105
  69.1 8.4 %collective-permute-start.17 = (bf16[512,768]{1,0:T(8,128)(2,1)S(1)}, bf16[512,768]{1,0:T(8,128)(2,1)S(1)}, u32[]{:S(2)}, u32[]{:S(2)}) collective-permute-start(bf16[512,768]{1,0:T(8,128)(2,1)S(1)} %act_grad_piece.6), channel_id=1, source_target_pairs={{0,1},{1,0},{2,3},{3,2},{4,5},{5,4},{6,7},{7,6},{8,9},{9,8},{10,11... | collective-permute-start | bytes 2359304 | tf_op jit(solution)/shard_map/ppermute | solution.py:327
  69.6 11.5 %collective-permute-start.25 = (bf16[64,3072]{1,0:T(8,128)(2,1)}, bf16[64,3072]{1,0:T(8,128)(2,1)S(1)}, u32[]{:S(2)}, u32[]{:S(2)}) collective-permute-start(bf16[64,3072]{1,0:T(8,128)(2,1)} %param.5), channel_id=1, source_target_pairs={{4,12},{12,20},{20,28},{28,24},{24,16},{16,8},{8,0},{0,4},{5,13},{... | collective-permute-start | bytes 1179656 | tf_op jit(solution)/shard_map/ppermute | solution.py:105
  71.0 21.3 %collective-permute-start.19 = (bf16[512,768]{1,0:T(8,128)(2,1)S(1)}, bf16[512,768]{1,0:T(8,128)(2,1)}, u32[]{:S(2)}, u32[]{:S(2)}) collective-permute-start(bf16[512,768]{1,0:T(8,128)(2,1)S(1)} %fusion), channel_id=1, source_target_pairs={{0,2},{1,3},{2,0},{3,1},{4,6},{5,7},{6,4},{7,5},{8,10},{9,11},{10,... | collective-permute-start | bytes 2359304 | tf_op jit(solution)/shard_map/ppermute | solution.py:335
  77.7 42.4 %collective-permute-start.18 = (bf16[512,768]{1,0:T(8,128)(2,1)S(1)}, bf16[512,768]{1,0:T(8,128)(2,1)}, u32[]{:S(2)}, u32[]{:S(2)}) collective-permute-start(bf16[512,768]{1,0:T(8,128)(2,1)S(1)} %fusion.1), channel_id=1, source_target_pairs={{0,2},{1,3},{2,0},{3,1},{4,6},{5,7},{6,4},{7,5},{8,10},{9,11},{10,... | collective-permute-start | bytes 2359304 | tf_op jit(solution)/shard_map/ppermute | solution.py:335
  81.1 13.1 %collective-permute-start.26 = (bf16[64,3072]{1,0:T(8,128)(2,1)}, bf16[64,3072]{1,0:T(8,128)(2,1)}, u32[]{:S(2)}, u32[]{:S(2)}) collective-permute-start(bf16[64,3072]{1,0:T(8,128)(2,1)} %copy-done.8), channel_id=1, source_target_pairs={{12,4},{20,12},{28,20},{24,28},{16,24},{8,16},{0,8},{4,0},{13,5},{... | collective-permute-start | bytes 1179656 | tf_op jit(solution)/shard_map/ppermute | solution.py:105
  82.7 11.6 %collective-permute-start.27 = (bf16[64,3072]{1,0:T(8,128)(2,1)S(1)}, bf16[64,3072]{1,0:T(8,128)(2,1)}, u32[]{:S(2)}, u32[]{:S(2)}) collective-permute-start(bf16[64,3072]{1,0:T(8,128)(2,1)S(1)} %collective-permute-done.25), channel_id=1, source_target_pairs={{4,12},{12,20},{20,28},{28,24},{24,16},{16,8},{8,0},{0,4},{5,13},{... | collective-permute-start | bytes 1179656 | tf_op jit(solution)/shard_map/ppermute | solution.py:105
  94.1 15.2 %collective-permute-start.20 = (bf16[512,768]{1,0:T(8,128)(2,1)S(1)}, bf16[512,768]{1,0:T(8,128)(2,1)S(1)}, u32[]{:S(2)}, u32[]{:S(2)}) collective-permute-start(bf16[512,768]{1,0:T(8,128)(2,1)S(1)} %multiply_convert_fusion.1.m_ref.refs_0_), channel_id=1, source_target_pairs={{0,1},{1,0},{2,3},{3,2},{4,5},{5,4},{6,7},{7,6},{8,9},{9,8},{10,11... | collective-permute-start | bytes 2359304 | tf_op jit(solution)/shard_map/ppermute | solution.py:350
  94.2 12.3 %collective-permute-start.28 = (bf16[64,3072]{1,0:T(8,128)(2,1)}, bf16[64,3072]{1,0:T(8,128)(2,1)S(1)}, u32[]{:S(2)}, u32[]{:S(2)}) collective-permute-start(bf16[64,3072]{1,0:T(8,128)(2,1)} %collective-permute-done.26), channel_id=1, source_target_pairs={{12,4},{20,12},{28,20},{24,28},{16,24},{8,16},{0,8},{4,0},{13,5},{... | collective-permute-start | bytes 1179656 | tf_op jit(solution)/shard_map/ppermute | solution.py:105
  95.9 11.4 %collective-permute-start.29 = (bf16[64,3072]{1,0:T(8,128)(2,1)}, bf16[64,3072]{1,0:T(8,128)(2,1)S(1)}, u32[]{:S(2)}, u32[]{:S(2)}) collective-permute-start(bf16[64,3072]{1,0:T(8,128)(2,1)} %collective-permute-done.27), channel_id=1, source_target_pairs={{4,12},{12,20},{20,28},{28,24},{24,16},{16,8},{8,0},{0,4},{5,13},{... | collective-permute-start | bytes 1179656 | tf_op jit(solution)/shard_map/ppermute | solution.py:105
  107.3 14.6 %collective-permute-start.30 = (bf16[32,3072]{1,0:T(8,128)(2,1)S(1)}, bf16[32,3072]{1,0:T(8,128)(2,1)S(1)}, u32[]{:S(2)}, u32[]{:S(2)}) collective-permute-start(bf16[32,3072]{1,0:T(8,128)(2,1)S(1)} %slice.107), channel_id=1, source_target_pairs={{4,12},{12,20},{20,28},{28,24},{24,16},{16,8},{8,0},{0,4},{5,13},{... | collective-permute-start | bytes 589832 | tf_op jit(solution)/shard_map/ppermute | solution.py:105
  108.0 13.8 %collective-permute-start.31 = (bf16[32,3072]{1,0:T(8,128)(2,1)S(1)}, bf16[32,3072]{1,0:T(8,128)(2,1)S(1)}, u32[]{:S(2)}, u32[]{:S(2)}) collective-permute-start(bf16[32,3072]{1,0:T(8,128)(2,1)S(1)} %slice.108), channel_id=1, source_target_pairs={{12,4},{20,12},{28,20},{24,28},{16,24},{8,16},{0,8},{4,0},{13,5},{... | collective-permute-start | bytes 589832 | tf_op jit(solution)/shard_map/ppermute | solution.py:105
  139.6 9.7 %collective-permute-start.23 = (bf16[64,1536]{1,0:T(8,128)(2,1)S(1)}, bf16[64,1536]{1,0:T(8,128)(2,1)S(1)}, u32[]{:S(2)}, u32[]{:S(2)}) collective-permute-start(bf16[64,1536]{1,0:T(8,128)(2,1)S(1)} %get-tuple-element.89), channel_id=1, source_target_pairs={{12,4},{20,12},{28,20},{24,28},{16,24},{8,16},{0,8},{4,0},{13,5},{... | collective-permute-start | bytes 589832 | tf_op jit(solution)/shard_map/ppermute | solution.py:131
  141.3 8.1 %collective-permute-start.22 = (bf16[64,1536]{1,0:T(8,128)(2,1)S(1)}, bf16[64,1536]{1,0:T(8,128)(2,1)S(1)}, u32[]{:S(2)}, u32[]{:S(2)}) collective-permute-start(bf16[64,1536]{1,0:T(8,128)(2,1)S(1)} %get-tuple-element.90), channel_id=1, source_target_pairs={{4,12},{12,20},{20,28},{28,24},{24,16},{16,8},{8,0},{0,4},{5,13},{... | collective-permute-start | bytes 589832 | tf_op jit(solution)/shard_map/ppermute | solution.py:131
  149.5 10.5 %collective-permute-start.32 = (bf16[64,3072]{1,0:T(8,128)(2,1)S(1)}, bf16[64,3072]{1,0:T(8,128)(2,1)S(1)}, u32[]{:S(2)}, u32[]{:S(2)}) collective-permute-start(bf16[64,3072]{1,0:T(8,128)(2,1)S(1)} %pad_maximum_fusion.1), channel_id=1, source_target_pairs={{4,12},{12,20},{20,28},{28,24},{24,16},{16,8},{8,0},{0,4},{5,13},{... | collective-permute-start | bytes 1179656 | tf_op jit(solution)/shard_map/ppermute | solution.py:131
  150.4 10.3 %collective-permute-start.33 = (bf16[64,3072]{1,0:T(8,128)(2,1)S(1)}, bf16[64,3072]{1,0:T(8,128)(2,1)S(1)}, u32[]{:S(2)}, u32[]{:S(2)}) collective-permute-start(bf16[64,3072]{1,0:T(8,128)(2,1)S(1)} %pad_maximum_fusion.2), channel_id=1, source_target_pairs={{12,4},{20,12},{28,20},{24,28},{16,24},{8,16},{0,8},{4,0},{13,5},{... | collective-permute-start | bytes 1179656 | tf_op jit(solution)/shard_map/ppermute | solution.py:131
  160.8 9.3 %collective-permute-start.35 = (bf16[64,3072]{1,0:T(8,128)(2,1)S(1)}, bf16[64,3072]{1,0:T(8,128)(2,1)S(1)}, u32[]{:S(2)}, u32[]{:S(2)}) collective-permute-start(bf16[64,3072]{1,0:T(8,128)(2,1)S(1)} %get-tuple-element.83), channel_id=1, source_target_pairs={{12,4},{20,12},{28,20},{24,28},{16,24},{8,16},{0,8},{4,0},{13,5},{... | collective-permute-start | bytes 1179656 | tf_op jit(solution)/shard_map/ppermute | solution.py:131
  162.1 9.1 %collective-permute-start.34 = (bf16[64,3072]{1,0:T(8,128)(2,1)S(1)}, bf16[64,3072]{1,0:T(8,128)(2,1)S(1)}, u32[]{:S(2)}, u32[]{:S(2)}) collective-permute-start(bf16[64,3072]{1,0:T(8,128)(2,1)S(1)} %get-tuple-element.84), channel_id=1, source_target_pairs={{4,12},{12,20},{20,28},{28,24},{24,16},{16,8},{8,0},{0,4},{5,13},{... | collective-permute-start | bytes 1179656 | tf_op jit(solution)/shard_map/ppermute | solution.py:131
  171.4 8.3 %collective-permute-start.36 = (bf16[64,3072]{1,0:T(8,128)(2,1)S(1)}, bf16[64,3072]{1,0:T(8,128)(2,1)S(1)}, u32[]{:S(2)}, u32[]{:S(2)}) collective-permute-start(bf16[64,3072]{1,0:T(8,128)(2,1)S(1)} %get-tuple-element.81), channel_id=1, source_target_pairs={{4,12},{12,20},{20,28},{28,24},{24,16},{16,8},{8,0},{0,4},{5,13},{... | collective-permute-start | bytes 1179656 | tf_op jit(solution)/shard_map/ppermute | solution.py:131
  172.1 7.9 %collective-permute-start.37 = (bf16[64,3072]{1,0:T(8,128)(2,1)S(1)}, bf16[64,3072]{1,0:T(8,128)(2,1)S(1)}, u32[]{:S(2)}, u32[]{:S(2)}) collective-permute-start(bf16[64,3072]{1,0:T(8,128)(2,1)S(1)} %get-tuple-element.82), channel_id=1, source_target_pairs={{12,4},{20,12},{28,20},{24,28},{16,24},{8,16},{0,8},{4,0},{13,5},{... | collective-permute-start | bytes 1179656 | tf_op jit(solution)/shard_map/ppermute | solution.py:131
  (17 other events, 144.5 us)

commit v2 on v1

v2 whole, which is shorter than its diff:
```python
import functools

import jax
import jax.numpy as jnp
from jax import lax
from jax.experimental import pallas as pl
from jax.experimental.pallas import tpu as pltpu
from jax.sharding import PartitionSpec as P

VMEM_BYTES = 20 * 2**20
STREAM_VMEM_BYTES = 47 * 2**20


def row_cycle(mesh):
    first = mesh.devices[:, 0]
    places = [getattr(device, "coords", None) for device in first]
    if any(place is None for place in places):
        return list(range(len(first)))
    at = {(place[2], place[1]): index for index, place in enumerate(places)}
    zs, ys = (sorted({key[i] for key in at}) for i in (0, 1))
    if len(at) != len(places) or len(at) != len(zs) * len(ys) or len(ys) < 2:
        return list(range(len(first)))
    walk = []
    for step, z in enumerate(zs):
        walk += [at[z, y] for y in (ys[1:] if step % 2 == 0 else ys[:0:-1])]
    return walk + [at[z, ys[0]] for z in reversed(zs)]


def pieces_of(length, want):
    return max(n for n in range(1, want + 1) if length % (128 * n) == 0 or n == 1)


def tile_of(length, most):
    return max(t for t in range(1, most + 1) if length % t == 0 and (t % 128 == 0 or t == length))


def gelu_parts(hidden_pre):
    hval = hidden_pre.astype(jnp.float32)
    inner = 0.7978845608 * (hval + 0.044715 * hval * hval * hval)
    tval = jnp.tanh(inner)
    act = 0.5 * hval * (1.0 + tval)
    slope = 0.5 * (1.0 + tval) + 0.5 * hval * (1.0 - tval * tval) * 0.7978845608 * (
        1.0 + 3.0 * 0.044715 * hval * hval
    )
    return (act, slope)


def gelu_blocks(order, hidden_pre, count):
    tokens, hidden = hidden_pre.shape
    share = tokens // count
    half = hidden // 2

    def kernel(order_ref, h_ref, act_ref, slope_ref):
        for index in range(2):
            at = slice(index * half, (index + 1) * half)

            @pl.when(order_ref[count] == index)
            def _():
                act, slope = gelu_parts(h_ref[:, at])
                act_ref[:, at] = act.astype(jnp.bfloat16)
                slope_ref[...] = slope

            @pl.when(order_ref[count] != index)
            def _():
                act_ref[:, at] = gelu_parts(h_ref[:, at])[0].astype(jnp.bfloat16)

    return pl.pallas_call(
        kernel,
        grid_spec=pltpu.PrefetchScalarGridSpec(
            num_scalar_prefetch=1,
            grid=(count,),
            in_specs=[pl.BlockSpec((share, hidden), lambda i, s: (s[i], 0))],
            out_specs=[
                pl.BlockSpec((share, hidden), lambda i, s: (i, 0)),
                pl.BlockSpec((share, half), lambda i, s: (i, 0)),
            ],
        ),
        out_shape=[
            jax.ShapeDtypeStruct((tokens, hidden), jnp.bfloat16),
            jax.ShapeDtypeStruct((tokens, half), jnp.float32),
        ],
        compiler_params=pltpu.CompilerParams(vmem_limit_bytes=VMEM_BYTES),
        cost_estimate=cost(20 * tokens * hidden, 6 * tokens * hidden),
        name="gelu_blocks",
    )(order, hidden_pre)


def after(value, *others):
    return lax.optimization_barrier((value, *others))[0]


def ring_gather(value, cycle):
    count = len(cycle)
    ahead = [(cycle[i], cycle[(i + 1) % count]) for i in range(count)]
    behind = [(b, a) for a, b in ahead]
    blocks = {0: [value]}
    state = [value, value]

    def step(k, *others):
        fore, back = state
        if 2 * k == count:
            cut = value.shape[0] // 2
            fore, back = fore[:cut], back[cut:]
        if others:
            fore, back = lax.optimization_barrier((fore, back, *others))[:2]
        state[:] = lax.ppermute(fore, "row", ahead), lax.ppermute(back, "row", behind)
        share = value.shape[0]
        if 2 * k == count:
            blocks[k] = list(state)
            return [(k * share, state[0]), (k * share + cut, state[1])]
        blocks[count - k], blocks[k] = [state[0]], [state[1]]
        return [((count - k) * share, state[0]), (k * share, state[1])]

    return step, lambda: [piece for k in sorted(blocks) for piece in blocks[k]]


def ring_sum(block, cycle, share, width, dtype, fill):
    count = len(cycle)
    half = width // 2
    ahead = [(cycle[i], cycle[(i + 1) % count]) for i in range(count)]
    behind = [(b, a) for a, b in ahead]

    def plus(left, right):
        return left.astype(jnp.float32) + right.astype(jnp.float32)

    def move(first, second):
        sent = (first.astype(jnp.bfloat16), second.astype(jnp.bfloat16))
        return fill(sent, (lax.ppermute(sent[0], "row", ahead), lax.ppermute(sent[1], "row", behind)))

    most = count // 2
    if count == 1:
        return block(0).astype(dtype)
    fore = back = None
    if count % 2 == 0:
        far = block(most)
        fore, back = move(far[:, :half], far[:, half:])
        most -= 1
    for shift in range(most, 0, -1):
        first, second = block(shift), block(-shift)
        if fore is not None and fore.shape[1] < width:
            fore = jnp.pad(fore, ((0, 0), (0, width - half)))
            back = jnp.pad(back, ((0, 0), (half, 0)))
        if fore is not None:
            first, second = plus(first, fore), plus(second, back)
        fore, back = move(first, second)
    own = block(0)
    if fore.shape[1] < width:
        return jnp.concatenate([plus(own[:, :half], fore), plus(own[:, half:], back)], 1).astype(dtype)
    return (plus(own, fore) + back.astype(jnp.float32)).astype(dtype)


def cost(flops, moved):
    return pl.CostEstimate(flops=flops // 4, bytes_accessed=moved // 4, transcendentals=0)


NEAR = pl.BlockSpec(memory_space=pltpu.VMEM)
FAR = pl.BlockSpec(memory_space=pltpu.HBM)
SCALAR = pl.BlockSpec(memory_space=pltpu.SMEM)
LAST_DIMS = (((1,), (1,)), ((), ()))


def run_of(length, first):
    return [(0, first), (first, length - first)] if first < length else [(0, length)]


def act_grad_piece(start, grads, weight_out, width, dtype):
    tokens, depth = grads.shape
    runs = run_of(width, tile_of(width, 256))

    def kernel(start_ref, g_ref, w_ref, o_ref, near, sem):
        copies = [
            pltpu.make_async_copy(
                w_ref.at[pl.ds(pl.multiple_of(start_ref[0] * width + at, 128), size)],
                near.at[pl.ds(at, size)],
                sem.at[index],
            )
            for index, (at, size) in enumerate(runs)
        ]
        for copy in copies:
            copy.start()
        for copy, (at, size) in zip(copies, runs):
            copy.wait()
            o_ref[:, at : at + size] = lax.dot_general(
                g_ref[...], near[at : at + size, :], LAST_DIMS, preferred_element_type=jnp.float32
            ).astype(dtype)

    return pl.pallas_call(
        kernel,
        in_specs=[SCALAR, NEAR, FAR],
        out_specs=NEAR,
        out_shape=jax.ShapeDtypeStruct((tokens, width), dtype),
        scratch_shapes=[pltpu.VMEM((width, depth), jnp.bfloat16), pltpu.SemaphoreType.DMA((len(runs),))],
        compiler_params=pltpu.CompilerParams(vmem_limit_bytes=STREAM_VMEM_BYTES),
        cost_estimate=cost(2 * tokens * depth * width, 2 * width * depth + 4 * tokens * width),
        name="act_grad_piece",
    )(start, grads, weight_out)


def input_grad_piece(where, mine, other, weight_in, total, share, far):
    tokens, width = mine.shape
    out = weight_in.shape[0]
    tile = tile_of(out, 768)

    def kernel(_, m_ref, *refs):
        theirs = jnp.concatenate([ref[...] for ref in refs[: len(other)]], 0)
        wm_ref, wo_ref, *refs = refs[len(other) :]
        value = lax.dot_general(m_ref[...], wm_ref[...], LAST_DIMS, preferred_element_type=jnp.float32)
        value += lax.dot_general(theirs, wo_ref[...], LAST_DIMS, preferred_element_type=jnp.float32)
        if total is not None:
            value += refs[0][...]
            refs = refs[1:]
        refs[0][...] = value
        if far is not None:
            refs[1][...] = value[far * share : (far + 1) * share].astype(jnp.bfloat16)

    block = pl.BlockSpec((tokens, tile), lambda i, s: (0, i))
    out_specs, out_shape = [block], [jax.ShapeDtypeStruct((tokens, out), jnp.float32)]
    if far is not None:
        out_specs.append(pl.BlockSpec((share, tile), lambda i, s: (0, i)))
        out_shape.append(jax.ShapeDtypeStruct((share, out), jnp.bfloat16))
    return pl.pallas_call(
        kernel,
        grid_spec=pltpu.PrefetchScalarGridSpec(
            num_scalar_prefetch=1,
            grid=(out // tile,),
            in_specs=[NEAR] * (1 + len(other))
            + [
                pl.BlockSpec((tile, width), lambda i, s: (i, s[0])),
                pl.BlockSpec((tile, width), lambda i, s: (i, s[1])),
            ]
            + ([] if total is None else [block]),
            out_specs=out_specs,
        ),
        out_shape=out_shape,
        compiler_params=pltpu.CompilerParams(vmem_limit_bytes=STREAM_VMEM_BYTES),
        cost_estimate=cost(4 * tokens * width * out, 4 * width * out + 8 * tokens * out),
        name="input_grad_piece",
    )(where, mine, *other, weight_in, weight_in, *([] if total is None else [total]))


def weight_out_grad_piece(act, grads, part, parts, held):
    tokens, rows = act.shape
    columns = grads.shape[1]
    share = rows // parts
    tile = tile_of(share, 512)
    first = part * (share // tile)

    def kernel(a_ref, g_ref, *refs):
        refs[-1][...] = lax.dot_general(
            a_ref[...], g_ref[...], (((0,), (0,)), ((), ())), preferred_element_type=jnp.float32
        ).astype(jnp.bfloat16)

    return pl.pallas_call(
        kernel,
        grid=(share // tile,),
        in_specs=[
            pl.BlockSpec((tokens, tile), lambda i: (0, first + i)),
            NEAR,
        ]
        + ([] if held is None else [pl.BlockSpec(memory_space=pl.ANY)]),
        out_specs=pl.BlockSpec((tile, columns), lambda i: (first + i, 0)),
        out_shape=jax.ShapeDtypeStruct((rows, columns), jnp.bfloat16),
        input_output_aliases={} if held is None else {2: 0},
        compiler_params=pltpu.CompilerParams(vmem_limit_bytes=VMEM_BYTES),
        cost_estimate=cost(2 * tokens * share * columns, 2 * share * columns + 2 * tokens * columns),
        name="weight_out_grad_piece",
    )(act, grads, *([] if held is None else [held]))


def weight_in_grad_piece(where, input_pieces, hid_pieces, first, tiles, tile, held):
    rows = input_pieces[0].shape[1]
    tokens, width = hid_pieces[0][0].shape
    count, blocks = len(hid_pieces), len(input_pieces)
    hid_blocks = [block for piece in hid_pieces for block in piece]
    columns = width * count

    def kernel(where_ref, *refs):
        left = jnp.concatenate([ref[...] for ref in refs[:blocks]], 0).T
        spot = blocks
        for index, piece in enumerate(hid_pieces):
            at = pl.multiple_of(where_ref[index] * width, 128)
            right = jnp.concatenate([ref[...] for ref in refs[spot : spot + len(piece)]], 0)
            spot += len(piece)
            refs[-1][:, pl.ds(at, width)] = jnp.dot(left, right, preferred_element_type=jnp.float32).astype(
                jnp.bfloat16
            )

    return pl.pallas_call(
        kernel,
        grid_spec=pltpu.PrefetchScalarGridSpec(
            num_scalar_prefetch=1,
            grid=(tiles,),
            in_specs=[pl.BlockSpec((piece.shape[0], tile), lambda i, s: (0, first + i)) for piece in input_pieces]
            + [NEAR] * len(hid_blocks)
            + ([] if held is None else [pl.BlockSpec(memory_space=pl.ANY)]),
            out_specs=pl.BlockSpec((tile, columns), lambda i, s: (first + i, 0)),
        ),
        out_shape=jax.ShapeDtypeStruct((rows, columns), jnp.bfloat16),
        input_output_aliases={} if held is None else {1 + blocks + len(hid_blocks): 0},
        compiler_params=pltpu.CompilerParams(vmem_limit_bytes=VMEM_BYTES),
        cost_estimate=cost(2 * tokens * tiles * tile * columns, 2 * tiles * tile * columns),
        name="weight_in_grad_piece",
    )(where, *input_pieces, *hid_blocks, *([] if held is None else [held]))


def body(cycle, inputs, hidden_pre, out_grad, weight_in, weight_out):
    cols = lax.axis_size("col")
    core = lax.axis_index("col") % 2
    twin = [(i, i ^ 1) for i in range(cols)]
    hops = [[(i, (i + 2 * hop) % cols) for i in range(cols)] for hop in range(1, cols // 2)]
    rows, share = len(cycle), out_grad.shape[0]
    place = lax.axis_index("row")
    order = [
        sum(jnp.where(place == row, cycle[(spot + shift) % rows], 0) for spot, row in enumerate(cycle))
        for shift in range(rows)
    ]
    half = hidden_pre.shape[1] // 2
    parts = pieces_of(half, 2)
    width = half // parts

    def at(*indices):
        return jnp.stack(indices).astype(jnp.int32)

    steps = rows // 2
    order = at(*order, core)
    grad_step, grad_pieces = ring_gather(out_grad, cycle)
    grad_all = jnp.zeros((rows * share, out_grad.shape[1]), out_grad.dtype)

    def put(pieces):
        whole = grad_all
        for start, piece in pieces:
            whole = lax.dynamic_update_slice_in_dim(whole, piece, start, 0)
        return whole

    new = [(0, out_grad)]
    act = slope = None
    for k in range(1, steps + 1):
        fresh = grad_step(k, *([] if k == 1 else [act, slope, grad_all]))
        if k == 1:
            act, slope = gelu_blocks(order, hidden_pre, rows)
        grad_all = put(new)
        new = fresh
    grad_all = put(new)
    grad_all, act, slope = lax.optimization_barrier((grad_all, act, slope))
    input_step, input_pieces = ring_gather(inputs, cycle)
    due = list(range(1, steps + 1))

    quarter = max(1, steps // 4)

    def input_steps(count, *others):
        for _ in range(min(count, len(due))):
            input_step(due.pop(0), *others)

    given, last = [], grad_all
    for part in range(parts):
        last = act_grad_piece(after(at((1 - core) * parts + part), last), grad_all, weight_out, width, jnp.bfloat16)
        given.append(lax.ppermute(last, "col", twin))
    input_steps(quarter, last)
    sums, arrived = [], []
    for part in range(parts):
        start = after(at(core * parts + part), last)
        total = act_grad_piece(start, grad_all, weight_out, width, jnp.float32) + given[part].astype(jnp.float32)
        last = total.astype(jnp.bfloat16)
        sums.append(total)
        arrived.append([lax.ppermute(last, "col", hop) for hop in hops])
    before = input_pieces()
    input_steps(quarter, last)
    grad_weight_out = weight_out_grad_piece(after(act, last, *before), grad_all, 0, 2, None)

    hid_pieces, where, partial, far = [], [], grad_weight_out, None
    for part in range(parts):
        arrived[part], partial, *_ = lax.optimization_barrier((arrived[part], partial, *input_pieces()))
        if part == 0:
            grad_weight_out, partial = partial, None
        total = sums[part]
        for value in arrived[part]:
            total = total + value.astype(jnp.float32)
        mine = (total * slope[:, part * width : (part + 1) * width]).astype(jnp.bfloat16)
        other = [lax.ppermute(piece, "col", twin) for piece in jnp.split(mine, 2)]
        end = part == parts - 1
        input_steps(rows if end else quarter, mine)
        here = at(core * parts + part, (1 - core) * parts + part)
        made = input_grad_piece(here, mine, other, weight_in, partial, share, steps if end else None)
        partial = made[0]
        if end:
            far = made[1]
        hid_pieces += [[mine], other]
        where += [core * parts + part, (1 - core) * parts + part]
    input_all = input_pieces()
    where = at(*where)

    tile = tile_of(inputs.shape[1], 256)
    tiles = inputs.shape[1] // tile
    plan = [1, 1, 6, 12] if steps == 4 else [12] * steps
    state = {"in": None, "out": grad_weight_out, "first": 0, "calls": 0}

    def block(shift):
        spot = shift % rows * share
        return far if shift == steps else partial[spot : spot + share]

    def fill(sent, received):
        call = state["calls"]
        state["calls"] += 1
        if call == min(1, steps - 1):
            state["out"] = weight_out_grad_piece(after(act, *sent), grad_all, 1, 2, state["out"])
            received, state["out"] = lax.optimization_barrier((received, state["out"]))
        count = min(tiles * plan[call] // 12, tiles) - state["first"]
        if count > 0:
            state["in"] = weight_in_grad_piece(
                after(where, *sent), input_all, hid_pieces, state["first"], count, tile, state["in"]
            )
            state["first"] += count
            received, state["in"] = lax.optimization_barrier((received, state["in"]))
        return received

    grad_in = ring_sum(block, cycle, share, inputs.shape[1], jnp.bfloat16, fill)
    return (grad_in, state["in"], state["out"])


def solution(mesh):
    return jax.shard_map(
        functools.partial(body, row_cycle(mesh)),
        mesh=mesh,
        in_specs=(
            P("row", "col"),
            P(None, "row"),
            P("row", "col"),
            P("col", "row"),
            P("row", "col"),
        ),
        out_specs=(P("row", "col"), P("col", "row"), P("row", "col")),
        check_vma=False,
    )
```

time: 182 us -> 154 us (0.85)
  Pallas kernels: 95.1 us -> 80.1 us
  starting transfers between devices: 37 us -> 29.5 us
  local copies, waits for them, and re-layouts: 10.7 us -> 5.96 us
  other arithmetic: 12.1 us -> 8.54 us
  waiting for transfers between devices: 24.9 us -> 28.4 us
    ppermute x12 -> x8, starting transfers between devices: 19.8 us -> 9.85 us  [step(): lax.ppermute(fore, 'row', ahead)]
    pallas_call x6 -> x5, Pallas kernels: 31.9 us -> 23.1 us  [the longest x4 18.9 us: act_grad_piece(): pl.pallas_call(kernel, in_specs=[SCALAR, NEAR, FAR], out_specs=NEAR, out_...]
    ppermute x4, waiting for transfers between devices: 8.5 us -> 0.49 us  [move(): lax.ppermute(sent[0], 'row', ahead)]
    ppermute x12 -> x8, waiting for transfers between devices: 12.5 us -> 18.9 us  [step(): lax.ppermute(fore, 'row', ahead)]
    unnamed x44 -> x20, local copies, waits for them, and re-layouts: 8.06 us -> 3.09 us
    pallas_call x2, Pallas kernels: 18.3 us -> 14.6 us  [weight_out_grad_piece(): pl.pallas_call(kernel, grid=(share // tile,), in_specs=[pl.BlockSpec((tok...]
    ppermute x2, waiting for transfers between devices: 0.01 us -> 3.36 us  [body(): arrived.append([lax.ppermute(last, 'col', hop) for hop in hops])]
    another operation x2 -> x0, other arithmetic: 3.33 us -> none
  transfers between devices with their start and end apart: 38 -> 32, of which waited for: 16 -> 16; matrix products, arithmetic and copies ran while one was open for 6% -> 6% of each run, Pallas kernels for 42% -> 49%
where the time goes in v2:
time: 154 us
  Pallas kernels  80.1 us (52%)
  starting transfers between devices  29.5 us (19%)
  waiting for transfers between devices  28.4 us (18%)
  other arithmetic  8.54 us (6%)
  local copies, waits for them, and re-layouts  5.96 us (4%)
    pallas_call x2, Pallas kernels, input_grad_piece(): pl.pallas_call(kernel, grid_spec=pltpu.PrefetchScalarGridSpec(num_scalar_...  21.5 us
    pallas_call x3, Pallas kernels, weight_in_grad_piece(): pl.pallas_call(kernel, grid_spec=pltpu.PrefetchScalarGridSpec(num_scalar_...  20.9 us
    ppermute x8, waiting for transfers between devices, step(): lax.ppermute(fore, 'row', ahead)  18.9 us
    pallas_call x4, Pallas kernels, act_grad_piece(): pl.pallas_call(kernel, in_specs=[SCALAR, NEAR, FAR], out_specs=NEAR, out_...  18.9 us
    pallas_call x2, Pallas kernels, weight_out_grad_piece(): pl.pallas_call(kernel, grid=(share // tile,), in_specs=[pl.BlockSpec((tok...  14.6 us
    ppermute x8, starting transfers between devices, step(): lax.ppermute(fore, 'row', ahead)  9.85 us
    ppermute x8, starting transfers between devices, step(): lax.ppermute(back, 'row', behind)  7.57 us
    ppermute x4, starting transfers between devices, move(): lax.ppermute(sent[1], 'row', behind)  4.83 us
  transfers between devices with their start and end apart: 32, of which 16 were waited for; matrix products, arithmetic and copies ran while one was open for 6% of the time, Pallas kernels for 49%

profile of v2, /device:TPU:0, one launch (start us, length us, event | category | flops | bytes accessed | tf_op | source)
XLA Modules:
  0.0 153.7 jit_solution(1853887882572921312)
XLA Ops:
  0.6 3.1 %collective-permute-start.1 = (bf16[64,3072]{1,0:T(8,128)(2,1)}, bf16[64,3072]{1,0:T(8,128)(2,1)S(1)}, u32[]{:S(2)}, u32[]{:S(2)}) collective-permute-start(bf16[64,3072]{1,0:T(8,128)(2,1)} %param.7), channel_id=1, source_target_pairs={{12,4},{20,12},{28,20},{24,28},{16,24},{8,16},{0,8},{4,0},{13,5},{... | collective-permute-start | bytes 1179656 | tf_op jit(solution)/shard_map/ppermute | solution.py:106
  5.5 1.9 %copy-done.5 = bf16[512,3072]{1,0:T(8,128)(2,1)S(1)} copy-done((bf16[512,3072]{1,0:T(8,128)(2,1)S(1)}, bf16[512,3072]{1,0:T(8,128)(2,1)}, u32[]{:S(2)}) %copy-start.5) | copy-done | bytes 3145752
  7.4 4.3 %gelu_blocks.1 = (bf16[512,3072]{1,0:T(8,128)(2,1)S(1)}, f32[512,1536]{1,0:T(8,128)S(1)}) custom-call(s32[9]{0:T(128)S(1)} %stack.73.order_ref, bf16[512,3072]{1,0:T(8,128)(2,1)S(1)} %copy-done.5), custom_call_target="tpu_custom_call" | custom-call | flops 7864320 | bytes 2359296 | tf_op jit(solution)/shard_map/gelu_blocks/pallas_call | solution.py:67
  13.0 1.6 %collective-permute-done = bf16[64,3072]{1,0:T(8,128)(2,1)} collective-permute-done((bf16[64,3072]{1,0:T(8,128)(2,1)}, bf16[64,3072]{1,0:T(8,128)(2,1)}, u32[]{:S(2)}, u32[]{:S(2)}) %collective-permute-start) | collective-permute-done | bytes 393248 | tf_op jit(solution)/shard_map/ppermute | solution.py:106
  14.9 1.7 %collective-permute-start.3 = (bf16[64,3072]{1,0:T(8,128)(2,1)S(1)}, bf16[64,3072]{1,0:T(8,128)(2,1)S(1)}, u32[]{:S(2)}, u32[]{:S(2)}) collective-permute-start(bf16[64,3072]{1,0:T(8,128)(2,1)S(1)} %collective-permute-done.1), channel_id=1, source_target_pairs={{12,4},{20,12},{28,20},{24,28},{16,24},{8,16},{0,8},{4,0},{13,5},{... | collective-permute-start | bytes 1179656 | tf_op jit(solution)/shard_map/ppermute | solution.py:106
  17.7 6.8 %collective-permute-done.2 = bf16[64,3072]{1,0:T(8,128)(2,1)S(1)} collective-permute-done((bf16[64,3072]{1,0:T(8,128)(2,1)}, bf16[64,3072]{1,0:T(8,128)(2,1)S(1)}, u32[]{:S(2)}, u32[]{:S(2)}) %collective-permute-start.2) | collective-permute-done | bytes 393248 | tf_op jit(solution)/shard_map/ppermute | solution.py:106
  26.7 6.7 %collective-permute-done.4 = bf16[64,3072]{1,0:T(8,128)(2,1)S(1)} collective-permute-done((bf16[64,3072]{1,0:T(8,128)(2,1)S(1)}, bf16[64,3072]{1,0:T(8,128)(2,1)S(1)}, u32[]{:S(2)}, u32[]{:S(2)}) %collective-permute-start.4) | collective-permute-done | bytes 393248 | tf_op jit(solution)/shard_map/ppermute | solution.py:106
  34.5 1.6 %collective-permute-start.6 = (bf16[32,3072]{1,0:T(8,128)(2,1)S(1)}, bf16[32,3072]{1,0:T(8,128)(2,1)S(1)}, u32[]{:S(2)}, u32[]{:S(2)}) collective-permute-start(bf16[32,3072]{1,0:T(8,128)(2,1)S(1)} %slice.60), channel_id=1, source_target_pairs={{4,12},{12,20},{20,28},{28,24},{24,16},{16,8},{8,0},{0,4},{5,13},{... | collective-permute-start | bytes 589832 | tf_op jit(solution)/shard_map/ppermute | solution.py:106
  36.6 3.6 %collective-permute-done.6 = bf16[32,3072]{1,0:T(8,128)(2,1)S(1)} collective-permute-done((bf16[32,3072]{1,0:T(8,128)(2,1)S(1)}, bf16[32,3072]{1,0:T(8,128)(2,1)S(1)}, u32[]{:S(2)}, u32[]{:S(2)}) %collective-permute-start.6) | collective-permute-done | bytes 196640 | tf_op jit(solution)/shard_map/ppermute | solution.py:106
  40.2 1.6 %collective-permute-done.7 = bf16[32,3072]{1,0:T(8,128)(2,1)S(1)} collective-permute-done((bf16[32,3072]{1,0:T(8,128)(2,1)S(1)}, bf16[32,3072]{1,0:T(8,128)(2,1)S(1)}, u32[]{:S(2)}, u32[]{:S(2)}) %collective-permute-start.7) | collective-permute-done | bytes 196640 | tf_op jit(solution)/shard_map/ppermute | solution.py:106
  41.8 5.2 %act_grad_piece.4 = bf16[512,768]{1,0:T(8,128)(2,1)} custom-call(s32[1]{0:T(128)} %bitcast.3.start_ref, bf16[512,3072]{1,0:T(8,128)(2,1)S(1)} %constant_dynamic-update-slice_fusion.g_ref, bf16[3072,3072]{1,0:T(8,128)(2,1)} %w_ref.7), custom_call_target="tpu_custom_call" | custom-call | flops 603979776 | bytes 1572864 | tf_op jit(solution)/shard_map/act_grad_piece/pallas_call | solution.py:187
  47.1 5.2 %act_grad_piece.5 = bf16[512,768]{1,0:T(8,128)(2,1)} custom-call(s32[1]{0:T(128)} %bitcast.1.start_ref, bf16[512,3072]{1,0:T(8,128)(2,1)S(1)} %constant_dynamic-update-slice_fusion.g_ref, bf16[3072,3072]{1,0:T(8,128)(2,1)} %w_ref.7), custom_call_target="tpu_custom_call" | custom-call | flops 603979776 | bytes 1572864 | tf_op jit(solution)/shard_map/act_grad_piece/pallas_call | solution.py:187
  53.3 1.6 %collective-permute-start.13 = (bf16[64,3072]{1,0:T(8,128)(2,1)S(1)}, bf16[64,3072]{1,0:T(8,128)(2,1)}, u32[]{:S(2)}, u32[]{:S(2)}) collective-permute-start(bf16[64,3072]{1,0:T(8,128)(2,1)S(1)} %copy-done.4), channel_id=1, source_target_pairs={{4,12},{12,20},{20,28},{28,24},{24,16},{16,8},{8,0},{0,4},{5,13},{... | collective-permute-start | bytes 1179656 | tf_op jit(solution)/shard_map/ppermute | solution.py:106
  54.8 4.3 %act_grad_piece.6 = f32[512,768]{1,0:T(8,128)S(1)} custom-call(s32[1]{0:T(128)} %bitcast.2.start_ref, bf16[512,3072]{1,0:T(8,128)(2,1)S(1)} %constant_dynamic-update-slice_fusion.g_ref, bf16[3072,3072]{1,0:T(8,128)(2,1)} %w_ref.7), custom_call_target="tpu_custom_call" | custom-call | flops 603979776 | bytes 1572864 | tf_op jit(solution)/shard_map/act_grad_piece/pallas_call | solution.py:187
  60.3 2.2 %fusion = bf16[512,768]{1,0:T(8,128)(2,1)} fusion(f32[512,768]{1,0:T(8,128)S(1)} %act_grad_piece.6, bf16[512,768]{1,0:T(8,128)(2,1)} %collective-permute-done.8), kind=kLoop, calls=%fused_computation.4 | loop fusion | flops 1179648 | bytes 3145728 | tf_op jit(solution)/shard_map/convert_element_type | solution.py:363
  64.0 4.2 %act_grad_piece.7 = f32[512,768]{1,0:T(8,128)S(1)} custom-call(s32[1]{0:T(128)} %bitcast.start_ref, bf16[512,3072]{1,0:T(8,128)(2,1)S(1)} %constant_dynamic-update-slice_fusion.g_ref, bf16[3072,3072]{1,0:T(8,128)(2,1)} %w_ref.7), custom_call_target="tpu_custom_call" | custom-call | flops 603979776 | bytes 1572864 | tf_op jit(solution)/shard_map/act_grad_piece/pallas_call | solution.py:187
  70.2 1.6 %collective-permute-start.15 = (bf16[64,3072]{1,0:T(8,128)(2,1)}, bf16[64,3072]{1,0:T(8,128)(2,1)S(1)}, u32[]{:S(2)}, u32[]{:S(2)}) collective-permute-start(bf16[64,3072]{1,0:T(8,128)(2,1)} %collective-permute-done.13.refs_8_), channel_id=1, source_target_pairs={{4,12},{12,20},{20,28},{28,24},{24,16},{16,8},{8,0},{0,4},{5,13},{... | collective-permute-start | bytes 1179656 | tf_op jit(solution)/shard_map/ppermute | solution.py:106
  72.4 7.3 %weight_out_grad_piece.2.refs_0_ = bf16[3072,3072]{1,0:T(8,128)(2,1)} custom-call(bf16[512,3072]{1,0:T(8,128)(2,1)S(1)} %copy-done.3, bf16[512,3072]{1,0:T(8,128)(2,1)S(1)} %constant_dynamic-update-slice_fusion.g_ref), custom_call_target="tpu_custom_call" | custom-call | flops 1207959552 | bytes 3145728 | tf_op jit(solution)/shard_map/weight_out_grad_piece/pallas_call | solution.py:253
  80.5 2.8 %collective-permute-done.11 = bf16[512,768]{1,0:T(8,128)(2,1)} collective-permute-done((bf16[512,768]{1,0:T(8,128)(2,1)}, bf16[512,768]{1,0:T(8,128)(2,1)}, u32[]{:S(2)}, u32[]{:S(2)}) %collective-permute-start.11) | collective-permute-done | bytes 786464 | tf_op jit(solution)/shard_map/ppermute | solution.py:365
  83.3 1.9 %multiply_convert_fusion.1.m_ref.refs_9_ = bf16[512,768]{1,0:T(8,128)(2,1)S(1)} fusion(f32[512,1536]{1,0:T(8,128)S(1)} %copy-done.7, bf16[512,768]{1,0:T(8,128)(2,1)} %collective-permute-done.11, f32[512,768]{1,0:T(8,128)S(1)} %copy-done.1, bf16[512,768]{1,0:T(8,128)(2,1)} %collective-permute-done.8), kind=kLoop, calls=%fused_computation.1 | loop fusion | flops 2359296 | bytes 5505024 | tf_op jit(solution)/shard_map/convert_element_type | solution.py:378
  86.2 1.6 %collective-permute-start.19 = (bf16[64,3072]{1,0:T(8,128)(2,1)S(1)}, bf16[64,3072]{1,0:T(8,128)(2,1)S(1)}, u32[]{:S(2)}, u32[]{:S(2)}) collective-permute-start(bf16[64,3072]{1,0:T(8,128)(2,1)S(1)} %collective-permute-done.15.refs_7_), channel_id=1, source_target_pairs={{4,12},{12,20},{20,28},{28,24},{24,16},{16,8},{8,0},{0,4},{5,13},{... | collective-permute-start | bytes 1179656 | tf_op jit(solution)/shard_map/ppermute | solution.py:106
  87.9 10.0 %input_grad_piece.2.refs_4_ = f32[512,3072]{1,0:T(8,128)} custom-call(s32[2]{0:T(128)S(1)} %pad_add_fusion.1._, bf16[512,768]{1,0:T(8,128)(2,1)S(1)} %multiply_convert_fusion.1.m_ref.refs_9_, bf16[256,768]{1,0:T(8,128)(2,1)S(1)} %collective-permute-done.16.refs_0_.refs_10_, bf16[256,768]{1,0:T(8,128)(2,1)S(1)} %collective-permute-done.17.refs_1_.refs_11_, ...), custom_call_target="tpu_custom_call" | custom-call | flops 1207959552 | bytes 5505024 | tf_op jit(solution)/shard_map/input_grad_piece/pallas_call | solution.py:221
  98.5 1.5 multiply_convert_fusion.m_ref.refs_12_
  100.8 1.7 %collective-permute-start.24 = (bf16[32,3072]{1,0:T(8,128)(2,1)S(1)}, bf16[32,3072]{1,0:T(8,128)(2,1)S(1)}, u32[]{:S(2)}, u32[]{:S(2)}) collective-permute-start(bf16[32,3072]{1,0:T(8,128)(2,1)S(1)} %slice.62), channel_id=1, source_target_pairs={{4,12},{12,20},{20,28},{28,24},{24,16},{16,8},{8,0},{0,4},{5,13},{... | collective-permute-start | bytes 589832 | tf_op jit(solution)/shard_map/ppermute | solution.py:106
  102.9 11.5 %input_grad_piece.3 = (f32[512,3072]{1,0:T(8,128)}, bf16[64,3072]{1,0:T(8,128)(2,1)S(1)}) custom-call(s32[2]{0:T(128)S(1)} %pad_add_fusion._, bf16[512,768]{1,0:T(8,128)(2,1)S(1)} %multiply_convert_fusion.m_ref.refs_12_, bf16[256,768]{1,0:T(8,128)(2,1)S(1)} %collective-permute-done.20.refs_0_.refs_13_, ...), custom_call_target="tpu_custom_call" | custom-call | flops 1207959552 | bytes 5505024 | tf_op jit(solution)/shard_map/input_grad_piece/pallas_call | solution.py:221
  114.9 1.6 %collective-permute-start.22 = (bf16[64,1536]{1,0:T(8,128)(2,1)S(1)}, bf16[64,1536]{1,0:T(8,128)(2,1)S(1)}, u32[]{:S(2)}, u32[]{:S(2)}) collective-permute-start(bf16[64,1536]{1,0:T(8,128)(2,1)S(1)} %get-tuple-element.106), channel_id=1, source_target_pairs={{4,12},{12,20},{20,28},{28,24},{24,16},{16,8},{8,0},{0,4},{5,13},{... | collective-permute-start | bytes 589832 | tf_op jit(solution)/shard_map/ppermute | solution.py:128
  116.5 3.8 %weight_in_grad_piece.3.refs_15_ = bf16[3072,3072]{1,0:T(8,128)(2,1)} custom-call(s32[4]{0:T(128)S(1)} %pad_add_fusion.2.where_ref, bf16[64,3072]{1,0:T(8,128)(2,1)S(1)} %copy-done.4, bf16[64,3072]{1,0:T(8,128)(2,1)} %collective-permute-done.12.refs_1_, bf16[64,3072]{1,0:T(8,128)(2,1)S(1)} %collective-permute-done.14.refs_2_, ...), custom_call_target="tpu_custom_call" | custom-call | flops 201326592 | bytes 393216 | tf_op jit(solution)/shard_map/weight_in_grad_piece/pallas_call | solution.py:288
  123.3 7.3 %weight_out_grad_piece.3 = bf16[3072,3072]{1,0:T(8,128)(2,1)} custom-call(bf16[512,3072]{1,0:T(8,128)(2,1)S(1)} %copy-done.3, bf16[512,3072]{1,0:T(8,128)(2,1)S(1)} %constant_dynamic-update-slice_fusion.g_ref, bf16[3072,3072]{1,0:T(8,128)(2,1)} %weight_out_grad_piece.2.refs_0_), custom_call_target="tpu_custom_call", output_to_operand_aliasing={{}: (2, {})} | custom-call | flops 1207959552 | bytes 3145728 | tf_op jit(solution)/shard_map/weight_out_grad_piece/pallas_call | solution.py:253
  131.5 1.8 %collective-permute-start.29 = (bf16[64,3072]{1,0:T(8,128)(2,1)S(1)}, bf16[64,3072]{1,0:T(8,128)(2,1)S(1)}, u32[]{:S(2)}, u32[]{:S(2)}) collective-permute-start(bf16[64,3072]{1,0:T(8,128)(2,1)S(1)} %get-tuple-element.97), channel_id=1, source_target_pairs={{12,4},{20,12},{28,20},{24,28},{16,24},{8,16},{0,8},{4,0},{13,5},{... | collective-permute-start | bytes 1179656 | tf_op jit(solution)/shard_map/ppermute | solution.py:128
  133.5 8.0 %weight_in_grad_piece.4.refs_15_ = bf16[3072,3072]{1,0:T(8,128)(2,1)} custom-call(s32[4]{0:T(128)S(1)} %pad_add_fusion.2.where_ref, bf16[64,3072]{1,0:T(8,128)(2,1)S(1)} %copy-done.4, bf16[64,3072]{1,0:T(8,128)(2,1)} %collective-permute-done.12.refs_1_, bf16[64,3072]{1,0:T(8,128)(2,1)S(1)} %collective-permute-done.14.refs_2_, ...), custom_call_target="tpu_custom_call", output_to_operand_aliasing={{}: (16, {})} | custom-call | flops 1006632960 | bytes 1966080 | tf_op jit(solution)/shard_map/weight_in_grad_piece/pallas_call | solution.py:288
  141.7 1.8 %collective-permute-start.31 = (bf16[64,3072]{1,0:T(8,128)(2,1)S(1)}, bf16[64,3072]{1,0:T(8,128)(2,1)S(1)}, u32[]{:S(2)}, u32[]{:S(2)}) collective-permute-start(bf16[64,3072]{1,0:T(8,128)(2,1)S(1)} %get-tuple-element.95), channel_id=1, source_target_pairs={{12,4},{20,12},{28,20},{24,28},{16,24},{8,16},{0,8},{4,0},{13,5},{... | collective-permute-start | bytes 1179656 | tf_op jit(solution)/shard_map/ppermute | solution.py:128
  143.7 9.1 %weight_in_grad_piece.5 = bf16[3072,3072]{1,0:T(8,128)(2,1)} custom-call(s32[4]{0:T(128)S(1)} %pad_add_fusion.2.where_ref, bf16[64,3072]{1,0:T(8,128)(2,1)S(1)} %copy-done.4, bf16[64,3072]{1,0:T(8,128)(2,1)} %collective-permute-done.12.refs_1_, bf16[64,3072]{1,0:T(8,128)(2,1)S(1)} %collective-permute-done.14.refs_2_, ...), custom_call_target="tpu_custom_call", output_to_operand_aliasing={{}: (16, {})} | custom-call | flops 1207959552 | bytes 2359296 | tf_op jit(solution)/shard_map/weight_in_grad_piece/pallas_call | solution.py:288
  (93 shorter events, 24.0 us)
Async XLA Ops:
  0.6 12.3 %collective-permute-start.1 = (bf16[64,3072]{1,0:T(8,128)(2,1)}, bf16[64,3072]{1,0:T(8,128)(2,1)S(1)}, u32[]{:S(2)}, u32[]{:S(2)}) collective-permute-start(bf16[64,3072]{1,0:T(8,128)(2,1)} %param.7), channel_id=1, source_target_pairs={{12,4},{20,12},{28,20},{24,28},{16,24},{8,16},{0,8},{4,0},{13,5},{... | collective-permute-start | bytes 1179656 | tf_op jit(solution)/shard_map/ppermute | solution.py:106
  3.7 10.9 %collective-permute-start = (bf16[64,3072]{1,0:T(8,128)(2,1)}, bf16[64,3072]{1,0:T(8,128)(2,1)}, u32[]{:S(2)}, u32[]{:S(2)}) collective-permute-start(bf16[64,3072]{1,0:T(8,128)(2,1)} %param.7), channel_id=1, source_target_pairs={{4,12},{12,20},{20,28},{28,24},{24,16},{16,8},{8,0},{0,4},{5,13},{... | collective-permute-start | bytes 1179656 | tf_op jit(solution)/shard_map/ppermute | solution.py:106
  14.6 9.9 %collective-permute-start.2 = (bf16[64,3072]{1,0:T(8,128)(2,1)}, bf16[64,3072]{1,0:T(8,128)(2,1)S(1)}, u32[]{:S(2)}, u32[]{:S(2)}) collective-permute-start(bf16[64,3072]{1,0:T(8,128)(2,1)} %collective-permute-done), channel_id=1, source_target_pairs={{4,12},{12,20},{20,28},{28,24},{24,16},{16,8},{8,0},{0,4},{5,13},{... | collective-permute-start | bytes 1179656 | tf_op jit(solution)/shard_map/ppermute | solution.py:106
  14.9 9.7 %collective-permute-start.3 = (bf16[64,3072]{1,0:T(8,128)(2,1)S(1)}, bf16[64,3072]{1,0:T(8,128)(2,1)S(1)}, u32[]{:S(2)}, u32[]{:S(2)}) collective-permute-start(bf16[64,3072]{1,0:T(8,128)(2,1)S(1)} %collective-permute-done.1), channel_id=1, source_target_pairs={{12,4},{20,12},{28,20},{24,28},{16,24},{8,16},{0,8},{4,0},{13,5},{... | collective-permute-start | bytes 1179656 | tf_op jit(solution)/shard_map/ppermute | solution.py:106
  24.6 8.8 %collective-permute-start.4 = (bf16[64,3072]{1,0:T(8,128)(2,1)S(1)}, bf16[64,3072]{1,0:T(8,128)(2,1)S(1)}, u32[]{:S(2)}, u32[]{:S(2)}) collective-permute-start(bf16[64,3072]{1,0:T(8,128)(2,1)S(1)} %collective-permute-done.2), channel_id=1, source_target_pairs={{4,12},{12,20},{20,28},{28,24},{24,16},{16,8},{8,0},{0,4},{5,13},{... | collective-permute-start | bytes 1179656 | tf_op jit(solution)/shard_map/ppermute | solution.py:106
  26.1 8.3 %collective-permute-start.5 = (bf16[64,3072]{1,0:T(8,128)(2,1)S(1)}, bf16[64,3072]{1,0:T(8,128)(2,1)S(1)}, u32[]{:S(2)}, u32[]{:S(2)}) collective-permute-start(bf16[64,3072]{1,0:T(8,128)(2,1)S(1)} %collective-permute-done.3), channel_id=1, source_target_pairs={{12,4},{20,12},{28,20},{24,28},{16,24},{8,16},{0,8},{4,0},{13,5},{... | collective-permute-start | bytes 1179656 | tf_op jit(solution)/shard_map/ppermute | solution.py:106
  34.5 5.7 %collective-permute-start.6 = (bf16[32,3072]{1,0:T(8,128)(2,1)S(1)}, bf16[32,3072]{1,0:T(8,128)(2,1)S(1)}, u32[]{:S(2)}, u32[]{:S(2)}) collective-permute-start(bf16[32,3072]{1,0:T(8,128)(2,1)S(1)} %slice.60), channel_id=1, source_target_pairs={{4,12},{12,20},{20,28},{28,24},{24,16},{16,8},{8,0},{0,4},{5,13},{... | collective-permute-start | bytes 589832 | tf_op jit(solution)/shard_map/ppermute | solution.py:106
  36.1 5.7 %collective-permute-start.7 = (bf16[32,3072]{1,0:T(8,128)(2,1)S(1)}, bf16[32,3072]{1,0:T(8,128)(2,1)S(1)}, u32[]{:S(2)}, u32[]{:S(2)}) collective-permute-start(bf16[32,3072]{1,0:T(8,128)(2,1)S(1)} %slice.61), channel_id=1, source_target_pairs={{12,4},{20,12},{28,20},{24,28},{16,24},{8,16},{0,8},{4,0},{13,5},{... | collective-permute-start | bytes 589832 | tf_op jit(solution)/shard_map/ppermute | solution.py:106
  47.0 12.2 %collective-permute-start.8 = (bf16[512,768]{1,0:T(8,128)(2,1)}, bf16[512,768]{1,0:T(8,128)(2,1)}, u32[]{:S(2)}, u32[]{:S(2)}) collective-permute-start(bf16[512,768]{1,0:T(8,128)(2,1)} %act_grad_piece.4), channel_id=1, source_target_pairs={{0,1},{1,0},{2,3},{3,2},{4,5},{5,4},{6,7},{7,6},{8,9},{9,8},{10,11... | collective-permute-start | bytes 2359304 | tf_op jit(solution)/shard_map/ppermute | solution.py:357
  52.3 16.0 %collective-permute-start.9 = (bf16[512,768]{1,0:T(8,128)(2,1)}, bf16[512,768]{1,0:T(8,128)(2,1)}, u32[]{:S(2)}, u32[]{:S(2)}) collective-permute-start(bf16[512,768]{1,0:T(8,128)(2,1)} %act_grad_piece.5), channel_id=1, source_target_pairs={{0,1},{1,0},{2,3},{3,2},{4,5},{5,4},{6,7},{7,6},{8,9},{9,8},{10,11... | collective-permute-start | bytes 2359304 | tf_op jit(solution)/shard_map/ppermute | solution.py:357
  52.8 16.9 %collective-permute-start.12 = (bf16[64,3072]{1,0:T(8,128)(2,1)S(1)}, bf16[64,3072]{1,0:T(8,128)(2,1)}, u32[]{:S(2)}, u32[]{:S(2)}) collective-permute-start(bf16[64,3072]{1,0:T(8,128)(2,1)S(1)} %copy-done.4), channel_id=1, source_target_pairs={{12,4},{20,12},{28,20},{24,28},{16,24},{8,16},{0,8},{4,0},{13,5},{... | collective-permute-start | bytes 1179656 | tf_op jit(solution)/shard_map/ppermute | solution.py:106
  53.3 16.5 %collective-permute-start.13 = (bf16[64,3072]{1,0:T(8,128)(2,1)S(1)}, bf16[64,3072]{1,0:T(8,128)(2,1)}, u32[]{:S(2)}, u32[]{:S(2)}) collective-permute-start(bf16[64,3072]{1,0:T(8,128)(2,1)S(1)} %copy-done.4), channel_id=1, source_target_pairs={{4,12},{12,20},{20,28},{28,24},{24,16},{16,8},{8,0},{0,4},{5,13},{... | collective-permute-start | bytes 1179656 | tf_op jit(solution)/shard_map/ppermute | solution.py:106
  62.5 20.8 %collective-permute-start.11 = (bf16[512,768]{1,0:T(8,128)(2,1)}, bf16[512,768]{1,0:T(8,128)(2,1)}, u32[]{:S(2)}, u32[]{:S(2)}) collective-permute-start(bf16[512,768]{1,0:T(8,128)(2,1)} %fusion), channel_id=1, source_target_pairs={{0,2},{1,3},{2,0},{3,1},{4,6},{5,7},{6,4},{7,5},{8,10},{9,11},{10,... | collective-permute-start | bytes 2359304 | tf_op jit(solution)/shard_map/ppermute | solution.py:365
  69.7 10.5 %collective-permute-start.14 = (bf16[64,3072]{1,0:T(8,128)(2,1)}, bf16[64,3072]{1,0:T(8,128)(2,1)S(1)}, u32[]{:S(2)}, u32[]{:S(2)}) collective-permute-start(bf16[64,3072]{1,0:T(8,128)(2,1)} %collective-permute-done.12.refs_1_), channel_id=1, source_target_pairs={{12,4},{20,12},{28,20},{24,28},{16,24},{8,16},{0,8},{4,0},{13,5},{... | collective-permute-start | bytes 1179656 | tf_op jit(solution)/shard_map/ppermute | solution.py:106
  70.2 10.3 %collective-permute-start.15 = (bf16[64,3072]{1,0:T(8,128)(2,1)}, bf16[64,3072]{1,0:T(8,128)(2,1)S(1)}, u32[]{:S(2)}, u32[]{:S(2)}) collective-permute-start(bf16[64,3072]{1,0:T(8,128)(2,1)} %collective-permute-done.13.refs_8_), channel_id=1, source_target_pairs={{4,12},{12,20},{20,28},{28,24},{24,16},{16,8},{8,0},{0,4},{5,13},{... | collective-permute-start | bytes 1179656 | tf_op jit(solution)/shard_map/ppermute | solution.py:106
  71.8 26.7 %collective-permute-start.10 = (bf16[512,768]{1,0:T(8,128)(2,1)S(1)}, bf16[512,768]{1,0:T(8,128)(2,1)S(1)}, u32[]{:S(2)}, u32[]{:S(2)}) collective-permute-start(bf16[512,768]{1,0:T(8,128)(2,1)S(1)} %fusion.1), channel_id=1, source_target_pairs={{0,2},{1,3},{2,0},{3,1},{4,6},{5,7},{6,4},{7,5},{8,10},{9,11},{10,... | collective-permute-start | bytes 2359304 | tf_op jit(solution)/shard_map/ppermute | solution.py:365
  85.2 2.7 %collective-permute-start.17 = (bf16[256,768]{1,0:T(8,128)(2,1)S(1)}, bf16[256,768]{1,0:T(8,128)(2,1)S(1)}, u32[]{:S(2)}, u32[]{:S(2)}) collective-permute-start(bf16[256,768]{1,0:T(8,128)(2,1)S(1)} %get-tuple-element.103), channel_id=1, source_target_pairs={{0,1},{1,0},{2,3},{3,2},{4,5},{5,4},{6,7},{7,6},{8,9},{9,8},{10,11... | collective-permute-start | bytes 1179656 | tf_op jit(solution)/shard_map/ppermute | solution.py:379
  85.3 2.6 %collective-permute-start.16 = (bf16[256,768]{1,0:T(8,128)(2,1)S(1)}, bf16[256,768]{1,0:T(8,128)(2,1)S(1)}, u32[]{:S(2)}, u32[]{:S(2)}) collective-permute-start(bf16[256,768]{1,0:T(8,128)(2,1)S(1)} %get-tuple-element.104), channel_id=1, source_target_pairs={{0,1},{1,0},{2,3},{3,2},{4,5},{5,4},{6,7},{7,6},{8,9},{9,8},{10,11... | collective-permute-start | bytes 1179656 | tf_op jit(solution)/shard_map/ppermute | solution.py:379
  85.8 12.7 %collective-permute-start.18 = (bf16[64,3072]{1,0:T(8,128)(2,1)S(1)}, bf16[64,3072]{1,0:T(8,128)(2,1)S(1)}, u32[]{:S(2)}, u32[]{:S(2)}) collective-permute-start(bf16[64,3072]{1,0:T(8,128)(2,1)S(1)} %collective-permute-done.14.refs_2_), channel_id=1, source_target_pairs={{12,4},{20,12},{28,20},{24,28},{16,24},{8,16},{0,8},{4,0},{13,5},{... | collective-permute-start | bytes 1179656 | tf_op jit(solution)/shard_map/ppermute | solution.py:106
  86.2 12.3 %collective-permute-start.19 = (bf16[64,3072]{1,0:T(8,128)(2,1)S(1)}, bf16[64,3072]{1,0:T(8,128)(2,1)S(1)}, u32[]{:S(2)}, u32[]{:S(2)}) collective-permute-start(bf16[64,3072]{1,0:T(8,128)(2,1)S(1)} %collective-permute-done.15.refs_7_), channel_id=1, source_target_pairs={{4,12},{12,20},{20,28},{28,24},{24,16},{16,8},{8,0},{0,4},{5,13},{... | collective-permute-start | bytes 1179656 | tf_op jit(solution)/shard_map/ppermute | solution.py:106
  100.1 2.8 %collective-permute-start.21 = (bf16[256,768]{1,0:T(8,128)(2,1)S(1)}, bf16[256,768]{1,0:T(8,128)(2,1)S(1)}, u32[]{:S(2)}, u32[]{:S(2)}) collective-permute-start(bf16[256,768]{1,0:T(8,128)(2,1)S(1)} %get-tuple-element.101), channel_id=1, source_target_pairs={{0,1},{1,0},{2,3},{3,2},{4,5},{5,4},{6,7},{7,6},{8,9},{9,8},{10,11... | collective-permute-start | bytes 1179656 | tf_op jit(solution)/shard_map/ppermute | solution.py:379
  100.2 2.7 %collective-permute-start.20 = (bf16[256,768]{1,0:T(8,128)(2,1)S(1)}, bf16[256,768]{1,0:T(8,128)(2,1)S(1)}, u32[]{:S(2)}, u32[]{:S(2)}) collective-permute-start(bf16[256,768]{1,0:T(8,128)(2,1)S(1)} %get-tuple-element.102), channel_id=1, source_target_pairs={{0,1},{1,0},{2,3},{3,2},{4,5},{5,4},{6,7},{7,6},{8,9},{9,8},{10,11... | collective-permute-start | bytes 1179656 | tf_op jit(solution)/shard_map/ppermute | solution.py:379
  100.8 15.7 %collective-permute-start.24 = (bf16[32,3072]{1,0:T(8,128)(2,1)S(1)}, bf16[32,3072]{1,0:T(8,128)(2,1)S(1)}, u32[]{:S(2)}, u32[]{:S(2)}) collective-permute-start(bf16[32,3072]{1,0:T(8,128)(2,1)S(1)} %slice.62), channel_id=1, source_target_pairs={{4,12},{12,20},{20,28},{28,24},{24,16},{16,8},{8,0},{0,4},{5,13},{... | collective-permute-start | bytes 589832 | tf_op jit(solution)/shard_map/ppermute | solution.py:106
  102.4 14.1 %collective-permute-start.25 = (bf16[32,3072]{1,0:T(8,128)(2,1)S(1)}, bf16[32,3072]{1,0:T(8,128)(2,1)S(1)}, u32[]{:S(2)}, u32[]{:S(2)}) collective-permute-start(bf16[32,3072]{1,0:T(8,128)(2,1)S(1)} %slice.63), channel_id=1, source_target_pairs={{12,4},{20,12},{28,20},{24,28},{16,24},{8,16},{0,8},{4,0},{13,5},{... | collective-permute-start | bytes 589832 | tf_op jit(solution)/shard_map/ppermute | solution.py:106
  114.4 6.6 %collective-permute-start.23 = (bf16[64,1536]{1,0:T(8,128)(2,1)S(1)}, bf16[64,1536]{1,0:T(8,128)(2,1)S(1)}, u32[]{:S(2)}, u32[]{:S(2)}) collective-permute-start(bf16[64,1536]{1,0:T(8,128)(2,1)S(1)} %get-tuple-element.105), channel_id=1, source_target_pairs={{12,4},{20,12},{28,20},{24,28},{16,24},{8,16},{0,8},{4,0},{13,5},{... | collective-permute-start | bytes 589832 | tf_op jit(solution)/shard_map/ppermute | solution.py:128
  114.9 6.2 %collective-permute-start.22 = (bf16[64,1536]{1,0:T(8,128)(2,1)S(1)}, bf16[64,1536]{1,0:T(8,128)(2,1)S(1)}, u32[]{:S(2)}, u32[]{:S(2)}) collective-permute-start(bf16[64,1536]{1,0:T(8,128)(2,1)S(1)} %get-tuple-element.106), channel_id=1, source_target_pairs={{4,12},{12,20},{20,28},{28,24},{24,16},{16,8},{8,0},{0,4},{5,13},{... | collective-permute-start | bytes 589832 | tf_op jit(solution)/shard_map/ppermute | solution.py:128
  121.2 9.7 %collective-permute-start.27 = (bf16[64,3072]{1,0:T(8,128)(2,1)S(1)}, bf16[64,3072]{1,0:T(8,128)(2,1)S(1)}, u32[]{:S(2)}, u32[]{:S(2)}) collective-permute-start(bf16[64,3072]{1,0:T(8,128)(2,1)S(1)} %get-tuple-element.99), channel_id=1, source_target_pairs={{12,4},{20,12},{28,20},{24,28},{16,24},{8,16},{0,8},{4,0},{13,5},{... | collective-permute-start | bytes 1179656 | tf_op jit(solution)/shard_map/ppermute | solution.py:128
  122.0 9.2 %collective-permute-start.26 = (bf16[64,3072]{1,0:T(8,128)(2,1)S(1)}, bf16[64,3072]{1,0:T(8,128)(2,1)S(1)}, u32[]{:S(2)}, u32[]{:S(2)}) collective-permute-start(bf16[64,3072]{1,0:T(8,128)(2,1)S(1)} %get-tuple-element.100), channel_id=1, source_target_pairs={{4,12},{12,20},{20,28},{28,24},{24,16},{16,8},{8,0},{0,4},{5,13},{... | collective-permute-start | bytes 1179656 | tf_op jit(solution)/shard_map/ppermute | solution.py:128
  131.5 10.0 %collective-permute-start.29 = (bf16[64,3072]{1,0:T(8,128)(2,1)S(1)}, bf16[64,3072]{1,0:T(8,128)(2,1)S(1)}, u32[]{:S(2)}, u32[]{:S(2)}) collective-permute-start(bf16[64,3072]{1,0:T(8,128)(2,1)S(1)} %get-tuple-element.97), channel_id=1, source_target_pairs={{12,4},{20,12},{28,20},{24,28},{16,24},{8,16},{0,8},{4,0},{13,5},{... | collective-permute-start | bytes 1179656 | tf_op jit(solution)/shard_map/ppermute | solution.py:128
  133.2 8.3 %collective-permute-start.28 = (bf16[64,3072]{1,0:T(8,128)(2,1)S(1)}, bf16[64,3072]{1,0:T(8,128)(2,1)S(1)}, u32[]{:S(2)}, u32[]{:S(2)}) collective-permute-start(bf16[64,3072]{1,0:T(8,128)(2,1)S(1)} %get-tuple-element.98), channel_id=1, source_target_pairs={{4,12},{12,20},{20,28},{28,24},{24,16},{16,8},{8,0},{0,4},{5,13},{... | collective-permute-start | bytes 1179656 | tf_op jit(solution)/shard_map/ppermute | solution.py:128
  141.7 11.2 %collective-permute-start.31 = (bf16[64,3072]{1,0:T(8,128)(2,1)S(1)}, bf16[64,3072]{1,0:T(8,128)(2,1)S(1)}, u32[]{:S(2)}, u32[]{:S(2)}) collective-permute-start(bf16[64,3072]{1,0:T(8,128)(2,1)S(1)} %get-tuple-element.95), channel_id=1, source_target_pairs={{12,4},{20,12},{28,20},{24,28},{16,24},{8,16},{0,8},{4,0},{13,5},{... | collective-permute-start | bytes 1179656 | tf_op jit(solution)/shard_map/ppermute | solution.py:128
  143.4 9.4 %collective-permute-start.30 = (bf16[64,3072]{1,0:T(8,128)(2,1)S(1)}, bf16[64,3072]{1,0:T(8,128)(2,1)S(1)}, u32[]{:S(2)}, u32[]{:S(2)}) collective-permute-start(bf16[64,3072]{1,0:T(8,128)(2,1)S(1)} %get-tuple-element.96), channel_id=1, source_target_pairs={{4,12},{12,20},{20,28},{28,24},{24,16},{16,8},{8,0},{0,4},{5,13},{... | collective-permute-start | bytes 1179656 | tf_op jit(solution)/shard_map/ppermute | solution.py:128
  (10 other events, 109.7 us)

commit v3 on v2

--- a/solution.py
+++ b/solution.py
@@ -50,7 +50,8 @@
     share = tokens // count
     half = hidden // 2
 
-    def kernel(order_ref, h_ref, act_ref, slope_ref):
+    def kernel(order_ref, h_ref, act_ref, slope_ref, mark_ref):
+        mark_ref[...] = jnp.zeros_like(mark_ref)
         for index in range(2):
             at = slice(index * half, (index + 1) * half)
 
@@ -73,11 +74,13 @@
             out_specs=[
                 pl.BlockSpec((share, hidden), lambda i, s: (i, 0)),
                 pl.BlockSpec((share, half), lambda i, s: (i, 0)),
+                pl.BlockSpec((8, 128), lambda i, s: (0, 0)),
             ],
         ),
         out_shape=[
-            jax.ShapeDtypeStruct((tokens, hidden), jnp.bfloat16),
-            jax.ShapeDtypeStruct((tokens, half), jnp.float32),
+            pltpu.HBM((tokens, hidden), jnp.bfloat16),
+            pltpu.HBM((tokens, half), jnp.float32),
+            jax.ShapeDtypeStruct((8, 128), jnp.float32),
         ],
         compiler_params=pltpu.CompilerParams(vmem_limit_bytes=VMEM_BYTES),
         cost_estimate=cost(20 * tokens * hidden, 6 * tokens * hidden),
@@ -163,6 +166,46 @@
     return [(0, first), (first, length - first)] if first < length else [(0, length)]
 
 
+def near_rows(start, weight, width):
+    def kernel(start_ref, w_ref, o_ref, sem):
+        rows = pl.ds(pl.multiple_of(start_ref[0] * width, width), width)
+        copy = pltpu.make_async_copy(w_ref.at[rows], o_ref, sem)
+        copy.start()
+        copy.wait()
+
+    return pl.pallas_call(
+        kernel,
+        in_specs=[SCALAR, FAR],
+        out_specs=NEAR,
+        out_shape=pltpu.VMEM((width, weight.shape[1]), weight.dtype),
+        scratch_shapes=[pltpu.SemaphoreType.DMA],
+        compiler_params=pltpu.CompilerParams(vmem_limit_bytes=STREAM_VMEM_BYTES),
+        cost_estimate=cost(0, 4 * width * weight.shape[1]),
+        name="near_rows",
+    )(start, weight)
+
+
+def near_grad_piece(grads, rows, taken):
+    def kernel(g_ref, w_ref, *refs):
+        value = lax.dot_general(g_ref[...], w_ref[...], LAST_DIMS, preferred_element_type=jnp.float32)
+        if taken is not None:
+            value += refs[0][...].astype(jnp.float32)
+            refs[1][...] = value
+        refs[-1][...] = value.astype(jnp.bfloat16)
+
+    shape = (grads.shape[0], rows.shape[0])
+    sent = jax.ShapeDtypeStruct(shape, jnp.bfloat16)
+    return pl.pallas_call(
+        kernel,
+        in_specs=[NEAR, NEAR] + ([] if taken is None else [NEAR]),
+        out_specs=NEAR if taken is None else [NEAR, NEAR],
+        out_shape=sent if taken is None else [jax.ShapeDtypeStruct(shape, jnp.float32), sent],
+        compiler_params=pltpu.CompilerParams(vmem_limit_bytes=12 * 2**20),
+        cost_estimate=cost(2 * grads.shape[1] * shape[0] * shape[1], 2 * rows.shape[0] * rows.shape[1]),
+        name="near_grad_piece",
+    )(grads, rows, *([] if taken is None else [taken]))
+
+
 def act_grad_piece(start, grads, weight_out, width, dtype):
     tokens, depth = grads.shape
     runs = run_of(width, tile_of(width, 256))
@@ -267,40 +310,64 @@
     )(act, grads, *([] if held is None else [held]))
 
 
-def weight_in_grad_piece(where, input_pieces, hid_pieces, first, tiles, tile, held):
+def near_hidden(where, hid_pieces):
+    width = hid_pieces[0][0].shape[1]
+    blocks = [block for piece in hid_pieces for block in piece]
+    places = []
+    for index, piece in enumerate(hid_pieces):
+        row = 0
+        for block in piece:
+            places.append((index, row, block.shape[0]))
+            row += block.shape[0]
+
+    def kernel(where_ref, *refs):
+        out_ref, sem = refs[-2:]
+        copies = []
+        for spot, (index, row, size) in enumerate(places):
+            columns = pl.ds(pl.multiple_of(where_ref[index] * width, 128), width)
+            copies.append(
+                pltpu.make_async_copy(refs[spot], out_ref.at[pl.ds(row, size), columns], sem.at[spot])
+            )
+        for copy in copies:
+            copy.start()
+        for copy in copies:
+            copy.wait()
+
+    shape = (sum(block.shape[0] for block in hid_pieces[0]), width * len(hid_pieces))
+    return pl.pallas_call(
+        kernel,
+        in_specs=[SCALAR] + [pl.BlockSpec(memory_space=pl.ANY)] * len(blocks),
+        out_specs=NEAR,
+        out_shape=pltpu.VMEM(shape, blocks[0].dtype),
+        scratch_shapes=[pltpu.SemaphoreType.DMA((len(blocks),))],
+        compiler_params=pltpu.CompilerParams(vmem_limit_bytes=2**20),
+        cost_estimate=cost(0, 4 * shape[0] * shape[1]),
+        name="near_hidden",
+    )(where, *blocks)
+
+
+def weight_in_grad_piece(hidden, input_pieces, first, tiles, tile, held):
     rows = input_pieces[0].shape[1]
-    tokens, width = hid_pieces[0][0].shape
-    count, blocks = len(hid_pieces), len(input_pieces)
-    hid_blocks = [block for piece in hid_pieces for block in piece]
-    columns = width * count
-
-    def kernel(where_ref, *refs):
+    tokens, columns = hidden.shape
+    blocks = len(input_pieces)
+
+    def kernel(h_ref, *refs):
         left = jnp.concatenate([ref[...] for ref in refs[:blocks]], 0).T
-        spot = blocks
-        for index, piece in enumerate(hid_pieces):
-            at = pl.multiple_of(where_ref[index] * width, 128)
-            right = jnp.concatenate([ref[...] for ref in refs[spot : spot + len(piece)]], 0)
-            spot += len(piece)
-            refs[-1][:, pl.ds(at, width)] = jnp.dot(left, right, preferred_element_type=jnp.float32).astype(
-                jnp.bfloat16
-            )
-
-    return pl.pallas_call(
-        kernel,
-        grid_spec=pltpu.PrefetchScalarGridSpec(
-            num_scalar_prefetch=1,
-            grid=(tiles,),
-            in_specs=[pl.BlockSpec((piece.shape[0], tile), lambda i, s: (0, first + i)) for piece in input_pieces]
-            + [NEAR] * len(hid_blocks)
-            + ([] if held is None else [pl.BlockSpec(memory_space=pl.ANY)]),
-            out_specs=pl.BlockSpec((tile, columns), lambda i, s: (first + i, 0)),
-        ),
+        refs[-1][...] = jnp.dot(left, h_ref[...], preferred_element_type=jnp.float32).astype(jnp.bfloat16)
+
+    return pl.pallas_call(
+        kernel,
+        grid=(tiles,),
+        in_specs=[NEAR]
+        + [pl.BlockSpec((piece.shape[0], tile), lambda i: (0, first + i)) for piece in input_pieces]
+        + ([] if held is None else [pl.BlockSpec(memory_space=pl.ANY)]),
+        out_specs=pl.BlockSpec((tile, columns), lambda i: (first + i, 0)),
         out_shape=jax.ShapeDtypeStruct((rows, columns), jnp.bfloat16),
-        input_output_aliases={} if held is None else {1 + blocks + len(hid_blocks): 0},
+        input_output_aliases={} if held is None else {1 + blocks: 0},
         compiler_params=pltpu.CompilerParams(vmem_limit_bytes=VMEM_BYTES),
         cost_estimate=cost(2 * tokens * tiles * tile * columns, 2 * tiles * tile * columns),
         name="weight_in_grad_piece",
-    )(where, *input_pieces, *hid_blocks, *([] if held is None else [held]))
+    )(hidden, *input_pieces, *([] if held is None else [held]))
 
 
 def body(cycle, inputs, hidden_pre, out_grad, weight_in, weight_out):
@@ -332,16 +399,20 @@
             whole = lax.dynamic_update_slice_in_dim(whole, piece, start, 0)
         return whole
 
-    new = [(0, out_grad)]
-    act = slope = None
+    new, loaded = [(0, out_grad)], []
+    act = slope = mark = None
     for k in range(1, steps + 1):
-        fresh = grad_step(k, *([] if k == 1 else [act, slope, grad_all]))
+        fresh = grad_step(k, *([] if k == 1 else [mark, grad_all, *loaded]))
         if k == 1:
-            act, slope = gelu_blocks(order, hidden_pre, rows)
+            act, slope, mark = gelu_blocks(order, hidden_pre, rows)
         grad_all = put(new)
+        for index in {2: range(parts), 3: range(parts, parts + 1)}.get(k, ()):
+            side = 1 - core if index < parts else core
+            start = after(at(side * parts + index % parts), grad_all, *loaded)
+            loaded.append(near_rows(start, weight_out, width))
         new = fresh
     grad_all = put(new)
-    grad_all, act, slope = lax.optimization_barrier((grad_all, act, slope))
+    grad_all = after(grad_all, mark)
     input_step, input_pieces = ring_gather(inputs, cycle)
     due = list(range(1, steps + 1))
 
@@ -353,14 +424,18 @@
 
     given, last = [], grad_all
     for part in range(parts):
-        last = act_grad_piece(after(at((1 - core) * parts + part), last), grad_all, weight_out, width, jnp.bfloat16)
+        last = near_grad_piece(grad_all, after(loaded[part], last), None)
         given.append(lax.ppermute(last, "col", twin))
     input_steps(quarter, last)
     sums, arrived = [], []
     for part in range(parts):
-        start = after(at(core * parts + part), last)
-        total = act_grad_piece(start, grad_all, weight_out, width, jnp.float32) + given[part].astype(jnp.float32)
-        last = total.astype(jnp.bfloat16)
+        if parts + part < len(loaded):
+            total, last = near_grad_piece(grad_all, after(loaded[parts + part], last), given[part])
+        else:
+            start = after(at(core * parts + part), last)
+            kept = act_grad_piece(start, grad_all, weight_out, width, jnp.float32)
+            total = kept + given[part].astype(jnp.float32)
+            last = total.astype(jnp.bfloat16)
         sums.append(total)
         arrived.append([lax.ppermute(last, "col", hop) for hop in hops])
     before = input_pieces()
@@ -391,8 +466,8 @@
 
     tile = tile_of(inputs.shape[1], 256)
     tiles = inputs.shape[1] // tile
-    plan = [1, 1, 6, 12] if steps == 4 else [12] * steps
-    state = {"in": None, "out": grad_weight_out, "first": 0, "calls": 0}
+    plan = [2, 2, 7, 12] if steps == 4 else [12] * steps
+    state = {"hidden": None, "in": None, "out": grad_weight_out, "first": 0, "calls": 0}
 
     def block(shift):
         spot = shift % rows * share
@@ -406,8 +481,10 @@
             received, state["out"] = lax.optimization_barrier((received, state["out"]))
         count = min(tiles * plan[call] // 12, tiles) - state["first"]
         if count > 0:
+            if state["hidden"] is None:
+                state["hidden"] = near_hidden(after(where, *sent), hid_pieces)
             state["in"] = weight_in_grad_piece(
-                after(where, *sent), input_all, hid_pieces, state["first"], count, tile, state["in"]
+                after(state["hidden"], *sent), input_all, state["first"], count, tile, state["in"]
             )
             state["first"] += count
             received, state["in"] = lax.optimization_barrier((received, state["in"]))

time: 154 us -> 149 us (0.968)
  waiting for transfers between devices: 28.4 us -> 18.3 us
  local copies, waits for them, and re-layouts: 5.96 us -> 9.88 us
  Pallas kernels: 80.1 us -> 83.4 us
  other arithmetic: 8.54 us -> 5.95 us
    pallas_call x3 -> x10, Pallas kernels: 20.9 us -> 36.7 us  [the longest x3 19 us: weight_in_grad_piece(): pl.pallas_call(kernel, grid=(tiles,), in_specs=[NEAR] + [pl.BlockSpec((pi...]
    pallas_call x4 -> x1, Pallas kernels: 18.9 us -> 4.25 us  [act_grad_piece(): pl.pallas_call(kernel, in_specs=[SCALAR, NEAR, FAR], out_specs=NEAR, out_...]
    ppermute x8, waiting for transfers between devices: 18.9 us -> 8.8 us  [step(): lax.ppermute(fore, 'row', ahead)]
    dynamic_update_slice x9, local copies, waits for them, and re-layouts: 2.59 us -> 5.58 us  [put(): whole = lax.dynamic_update_slice_in_dim(whole, piece, start, 0)]
    ppermute x4, starting transfers between devices: 4.83 us -> 2 us  [move(): lax.ppermute(sent[1], 'row', behind)]
    ppermute x4, starting transfers between devices: 3.48 us -> 6.31 us  [move(): lax.ppermute(sent[0], 'row', ahead)]
    convert_element_type x2 -> x1, other arithmetic: 3.62 us -> 1.44 us  [body(): last = total.astype(jnp.bfloat16)]
    pallas_call x1, Pallas kernels: 4.26 us -> 6.32 us  [gelu_blocks(): pl.pallas_call(kernel, grid_spec=pltpu.PrefetchScalarGridSpec(num_scalar_...]
  transfers between devices with their start and end apart: 32 -> 32, of which waited for: 16 -> 13; matrix products, arithmetic and copies ran while one was open for 6% -> 6% of each run, Pallas kernels for 49% -> 55%
where the time goes in v3:
time: 149 us; the launch traced here: 148 us
  Pallas kernels  83.4 us (56%)
  starting transfers between devices  29.5 us (20%)
  waiting for transfers between devices  18.3 us (12%)
  local copies, waits for them, and re-layouts  9.88 us (7%)
  other arithmetic  5.95 us (4%)
    pallas_call x2, Pallas kernels, input_grad_piece(): pl.pallas_call(kernel, grid_spec=pltpu.PrefetchScalarGridSpec(num_scalar_...  21.5 us
    pallas_call x3, Pallas kernels, weight_in_grad_piece(): pl.pallas_call(kernel, grid=(tiles,), in_specs=[NEAR] + [pl.BlockSpec((pi...  19 us
    pallas_call x2, Pallas kernels, weight_out_grad_piece(): pl.pallas_call(kernel, grid=(share // tile,), in_specs=[pl.BlockSpec((tok...  14.6 us
    ppermute x8, starting transfers between devices, step(): lax.ppermute(fore, 'row', ahead)  10.7 us
    pallas_call x3, Pallas kernels, near_grad_piece(): pl.pallas_call(kernel, in_specs=[NEAR, NEAR] + ([] if taken is None else...  9.67 us
    ppermute x8, waiting for transfers between devices, step(): lax.ppermute(fore, 'row', ahead)  8.8 us
    pallas_call x3, Pallas kernels, near_rows(): pl.pallas_call(kernel, in_specs=[SCALAR, FAR], out_specs=NEAR, out_shape=...  7.05 us
    ppermute x8, starting transfers between devices, step(): lax.ppermute(back, 'row', behind)  6.77 us
  transfers between devices with their start and end apart: 32, of which 13 were waited for; matrix products, arithmetic and copies ran while one was open for 6% of the time, Pallas kernels for 55%

profile of v3, /device:TPU:0, one launch (start us, length us, event | category | flops | bytes accessed | tf_op | source)
XLA Modules:
  0.0 148.1 jit_solution(10553391097733243907)
XLA Ops:
  0.6 3.1 %collective-permute-start.1 = (bf16[64,3072]{1,0:T(8,128)(2,1)}, bf16[64,3072]{1,0:T(8,128)(2,1)S(1)}, u32[]{:S(2)}, u32[]{:S(2)}) collective-permute-start(bf16[64,3072]{1,0:T(8,128)(2,1)} %param.7), channel_id=1, source_target_pairs={{12,4},{20,12},{28,20},{24,28},{16,24},{8,16},{0,8},{4,0},{13,5},{... | collective-permute-start | bytes 1179656 | tf_op jit(solution)/shard_map/ppermute | solution.py:109
  5.5 1.9 %copy-done.2 = bf16[512,3072]{1,0:T(8,128)(2,1)S(1)} copy-done((bf16[512,3072]{1,0:T(8,128)(2,1)S(1)}, bf16[512,3072]{1,0:T(8,128)(2,1)}, u32[]{:S(2)}) %copy-start.2) | copy-done | bytes 3145752
  7.4 6.3 %gelu_blocks.1 = (bf16[512,3072]{1,0:T(8,128)(2,1)}, f32[512,1536]{1,0:T(8,128)}, f32[8,128]{1,0:T(8,128)}) custom-call(s32[9]{0:T(128)S(1)} %stack.71.order_ref, bf16[512,3072]{1,0:T(8,128)(2,1)S(1)} %copy-done.2), custom_call_target="tpu_custom_call" | custom-call | flops 7864320 | bytes 2359296 | tf_op jit(solution)/shard_map/gelu_blocks/pallas_call | solution.py:68
  17.7 2.4 %near_rows.3.w_ref = bf16[768,3072]{1,0:T(8,128)(2,1)S(1)} custom-call(s32[1]{0:T(128)} %bitcast.11.start_ref, bf16[3072,3072]{1,0:T(8,128)(2,1)} %w_ref.7), custom_call_target="tpu_custom_call" | custom-call | bytes 2359296 | tf_op jit(solution)/shard_map/near_rows/pallas_call | solution.py:176
  20.0 2.4 %near_rows.4.w_ref = bf16[768,3072]{1,0:T(8,128)(2,1)S(1)} custom-call(s32[1]{0:T(128)} %bitcast.1.start_ref, bf16[3072,3072]{1,0:T(8,128)(2,1)} %w_ref.7), custom_call_target="tpu_custom_call" | custom-call | bytes 2359296 | tf_op jit(solution)/shard_map/near_rows/pallas_call | solution.py:176
  22.4 2.2 %collective-permute-done.2 = bf16[64,3072]{1,0:T(8,128)(2,1)} collective-permute-done((bf16[64,3072]{1,0:T(8,128)(2,1)}, bf16[64,3072]{1,0:T(8,128)(2,1)}, u32[]{:S(2)}, u32[]{:S(2)}) %collective-permute-start.2) | collective-permute-done | bytes 393248 | tf_op jit(solution)/shard_map/ppermute | solution.py:109
  25.8 1.6 %collective-permute-start.4 = (bf16[64,3072]{1,0:T(8,128)(2,1)}, bf16[64,3072]{1,0:T(8,128)(2,1)S(1)}, u32[]{:S(2)}, u32[]{:S(2)}) collective-permute-start(bf16[64,3072]{1,0:T(8,128)(2,1)} %collective-permute-done.2), channel_id=1, source_target_pairs={{4,12},{12,20},{20,28},{28,24},{24,16},{16,8},{8,0},{0,4},{5,13},{... | collective-permute-start | bytes 1179656 | tf_op jit(solution)/shard_map/ppermute | solution.py:109
  29.9 2.4 %near_rows.5.w_ref = bf16[768,3072]{1,0:T(8,128)(2,1)S(1)} custom-call(s32[1]{0:T(128)} %bitcast.12.start_ref, bf16[3072,3072]{1,0:T(8,128)(2,1)} %w_ref.7), custom_call_target="tpu_custom_call" | custom-call | bytes 2359296 | tf_op jit(solution)/shard_map/near_rows/pallas_call | solution.py:176
  32.2 2.8 %collective-permute-done.4 = bf16[64,3072]{1,0:T(8,128)(2,1)S(1)} collective-permute-done((bf16[64,3072]{1,0:T(8,128)(2,1)}, bf16[64,3072]{1,0:T(8,128)(2,1)S(1)}, u32[]{:S(2)}, u32[]{:S(2)}) %collective-permute-start.4) | collective-permute-done | bytes 393248 | tf_op jit(solution)/shard_map/ppermute | solution.py:109
  37.4 1.6 %collective-permute-start.6 = (bf16[32,3072]{1,0:T(8,128)(2,1)S(1)}, bf16[32,3072]{1,0:T(8,128)(2,1)S(1)}, u32[]{:S(2)}, u32[]{:S(2)}) collective-permute-start(bf16[32,3072]{1,0:T(8,128)(2,1)S(1)} %slice.60), channel_id=1, source_target_pairs={{4,12},{12,20},{20,28},{28,24},{24,16},{16,8},{8,0},{0,4},{5,13},{... | collective-permute-start | bytes 589832 | tf_op jit(solution)/shard_map/ppermute | solution.py:109
  40.5 2.6 %collective-permute-done.6 = bf16[32,3072]{1,0:T(8,128)(2,1)S(1)} collective-permute-done((bf16[32,3072]{1,0:T(8,128)(2,1)S(1)}, bf16[32,3072]{1,0:T(8,128)(2,1)S(1)}, u32[]{:S(2)}, u32[]{:S(2)}) %collective-permute-start.6) | collective-permute-done | bytes 196640 | tf_op jit(solution)/shard_map/ppermute | solution.py:109
  43.1 1.6 %collective-permute-done.7 = bf16[32,3072]{1,0:T(8,128)(2,1)S(1)} collective-permute-done((bf16[32,3072]{1,0:T(8,128)(2,1)S(1)}, bf16[32,3072]{1,0:T(8,128)(2,1)S(1)}, u32[]{:S(2)}, u32[]{:S(2)}) %collective-permute-start.7) | collective-permute-done | bytes 196640 | tf_op jit(solution)/shard_map/ppermute | solution.py:109
  44.7 2.6 %near_grad_piece.3 = bf16[512,768]{1,0:T(8,128)(2,1)S(1)} custom-call(bf16[512,3072]{1,0:T(8,128)(2,1)S(1)} %constant_dynamic-update-slice_fusion.g_ref, bf16[768,3072]{1,0:T(8,128)(2,1)S(1)} %near_rows.3.w_ref), custom_call_target="tpu_custom_call" | custom-call | flops 603979776 | bytes 1179648 | tf_op jit(solution)/shard_map/near_grad_piece/pallas_call | solution.py:198
  47.4 3.5 %near_grad_piece.4 = bf16[512,768]{1,0:T(8,128)(2,1)} custom-call(bf16[512,3072]{1,0:T(8,128)(2,1)S(1)} %constant_dynamic-update-slice_fusion.g_ref, bf16[768,3072]{1,0:T(8,128)(2,1)S(1)} %near_rows.4.w_ref), custom_call_target="tpu_custom_call" | custom-call | flops 603979776 | bytes 1179648 | tf_op jit(solution)/shard_map/near_grad_piece/pallas_call | solution.py:198
  51.9 1.6 %collective-permute-start.13 = (bf16[64,3072]{1,0:T(8,128)(2,1)S(1)}, bf16[64,3072]{1,0:T(8,128)(2,1)}, u32[]{:S(2)}, u32[]{:S(2)}) collective-permute-start(bf16[64,3072]{1,0:T(8,128)(2,1)S(1)} %copy-done.1), channel_id=1, source_target_pairs={{4,12},{12,20},{20,28},{28,24},{24,16},{16,8},{8,0},{0,4},{5,13},{... | collective-permute-start | bytes 1179656 | tf_op jit(solution)/shard_map/ppermute | solution.py:109
  53.5 3.5 %near_grad_piece.5 = (f32[512,768]{1,0:T(8,128)S(1)}, bf16[512,768]{1,0:T(8,128)(2,1)}) custom-call(bf16[512,3072]{1,0:T(8,128)(2,1)S(1)} %constant_dynamic-update-slice_fusion.g_ref, bf16[768,3072]{1,0:T(8,128)(2,1)S(1)} %near_rows.5.w_ref, bf16[512,768]{1,0:T(8,128)(2,1)S(1)} %collective-permute-done.8.refs_0_), custom_call_target="tpu_custom_call" | custom-call | flops 603979776 | bytes 1179648 | tf_op jit(solution)/shard_map/near_grad_piece/pallas_call | solution.py:198
  59.7 4.2 %act_grad_piece.1 = f32[512,768]{1,0:T(8,128)S(1)} custom-call(s32[1]{0:T(128)} %bitcast.start_ref, bf16[512,3072]{1,0:T(8,128)(2,1)S(1)} %constant_dynamic-update-slice_fusion.g_ref, bf16[3072,3072]{1,0:T(8,128)(2,1)} %w_ref.7), custom_call_target="tpu_custom_call" | custom-call | flops 603979776 | bytes 1572864 | tf_op jit(solution)/shard_map/act_grad_piece/pallas_call | solution.py:230
  65.9 1.6 %collective-permute-start.15 = (bf16[64,3072]{1,0:T(8,128)(2,1)}, bf16[64,3072]{1,0:T(8,128)(2,1)S(1)}, u32[]{:S(2)}, u32[]{:S(2)}) collective-permute-start(bf16[64,3072]{1,0:T(8,128)(2,1)} %collective-permute-done.13.refs_8_), channel_id=1, source_target_pairs={{4,12},{12,20},{20,28},{28,24},{24,16},{16,8},{8,0},{0,4},{5,13},{... | collective-permute-start | bytes 1179656 | tf_op jit(solution)/shard_map/ppermute | solution.py:109
  68.1 7.3 %weight_out_grad_piece.2.refs_0_ = bf16[3072,3072]{1,0:T(8,128)(2,1)} custom-call(bf16[512,3072]{1,0:T(8,128)(2,1)S(1)} %copy-done, bf16[512,3072]{1,0:T(8,128)(2,1)S(1)} %constant_dynamic-update-slice_fusion.g_ref), custom_call_target="tpu_custom_call" | custom-call | flops 1207959552 | bytes 3145728 | tf_op jit(solution)/shard_map/weight_out_grad_piece/pallas_call | solution.py:296
  76.2 2.8 %collective-permute-done.11 = bf16[512,768]{1,0:T(8,128)(2,1)} collective-permute-done((bf16[512,768]{1,0:T(8,128)(2,1)}, bf16[512,768]{1,0:T(8,128)(2,1)}, u32[]{:S(2)}, u32[]{:S(2)}) %collective-permute-start.11) | collective-permute-done | bytes 786464 | tf_op jit(solution)/shard_map/ppermute | solution.py:440
  81.6 1.6 %collective-permute-start.19 = (bf16[64,3072]{1,0:T(8,128)(2,1)S(1)}, bf16[64,3072]{1,0:T(8,128)(2,1)S(1)}, u32[]{:S(2)}, u32[]{:S(2)}) collective-permute-start(bf16[64,3072]{1,0:T(8,128)(2,1)S(1)} %collective-permute-done.15.refs_7_), channel_id=1, source_target_pairs={{4,12},{12,20},{20,28},{28,24},{24,16},{16,8},{8,0},{0,4},{5,13},{... | collective-permute-start | bytes 1179656 | tf_op jit(solution)/shard_map/ppermute | solution.py:109
  83.2 10.0 %input_grad_piece.2.refs_4_ = f32[512,3072]{1,0:T(8,128)} custom-call(s32[2]{0:T(128)S(1)} %pad_add_fusion.1._, bf16[512,768]{1,0:T(8,128)(2,1)S(1)} %multiply_convert_fusion.1.m_ref.refs_0_, bf16[256,768]{1,0:T(8,128)(2,1)S(1)} %collective-permute-done.16.refs_0_.refs_1_, bf16[256,768]{1,0:T(8,128)(2,1)S(1)} %collective-permute-done.17.refs_1_.refs_2_, ...), custom_call_target="tpu_custom_call" | custom-call | flops 1207959552 | bytes 5505024 | tf_op jit(solution)/shard_map/input_grad_piece/pallas_call | solution.py:264
  96.5 1.6 %collective-permute-start.24 = (bf16[32,3072]{1,0:T(8,128)(2,1)S(1)}, bf16[32,3072]{1,0:T(8,128)(2,1)S(1)}, u32[]{:S(2)}, u32[]{:S(2)}) collective-permute-start(bf16[32,3072]{1,0:T(8,128)(2,1)S(1)} %slice.62), channel_id=1, source_target_pairs={{4,12},{12,20},{20,28},{28,24},{24,16},{16,8},{8,0},{0,4},{5,13},{... | collective-permute-start | bytes 589832 | tf_op jit(solution)/shard_map/ppermute | solution.py:109
  98.5 11.5 %input_grad_piece.3 = (f32[512,3072]{1,0:T(8,128)}, bf16[64,3072]{1,0:T(8,128)(2,1)S(1)}) custom-call(s32[2]{0:T(128)S(1)} %pad_add_fusion._, bf16[512,768]{1,0:T(8,128)(2,1)S(1)} %multiply_convert_fusion.m_ref.refs_3_, bf16[256,768]{1,0:T(8,128)(2,1)S(1)} %collective-permute-done.20.refs_0_.refs_4_, ...), custom_call_target="tpu_custom_call" | custom-call | flops 1207959552 | bytes 5505024 | tf_op jit(solution)/shard_map/input_grad_piece/pallas_call | solution.py:264
  110.6 1.6 %collective-permute-start.22 = (bf16[64,1536]{1,0:T(8,128)(2,1)S(1)}, bf16[64,1536]{1,0:T(8,128)(2,1)S(1)}, u32[]{:S(2)}, u32[]{:S(2)}) collective-permute-start(bf16[64,1536]{1,0:T(8,128)(2,1)S(1)} %get-tuple-element.116), channel_id=1, source_target_pairs={{4,12},{12,20},{20,28},{28,24},{24,16},{16,8},{8,0},{0,4},{5,13},{... | collective-permute-start | bytes 589832 | tf_op jit(solution)/shard_map/ppermute | solution.py:131
  113.3 4.3 %weight_in_grad_piece.3.refs_9_ = bf16[3072,3072]{1,0:T(8,128)(2,1)} custom-call(bf16[512,3072]{1,0:T(8,128)(2,1)S(1)} %near_hidden.1.h_ref, bf16[64,3072]{1,0:T(8,128)(2,1)S(1)} %copy-done.1, bf16[64,3072]{1,0:T(8,128)(2,1)} %collective-permute-done.12.refs_1_, bf16[64,3072]{1,0:T(8,128)(2,1)S(1)} %collective-permute-done.14.refs_2_, ...), custom_call_target="tpu_custom_call" | custom-call | flops 402653184 | bytes 786432 | tf_op jit(solution)/shard_map/weight_in_grad_piece/pallas_call | solution.py:358
  118.3 1.6 %collective-permute-start.26 = (bf16[64,3072]{1,0:T(8,128)(2,1)S(1)}, bf16[64,3072]{1,0:T(8,128)(2,1)S(1)}, u32[]{:S(2)}, u32[]{:S(2)}) collective-permute-start(bf16[64,3072]{1,0:T(8,128)(2,1)S(1)} %get-tuple-element.110), channel_id=1, source_target_pairs={{4,12},{12,20},{20,28},{28,24},{24,16},{16,8},{8,0},{0,4},{5,13},{... | collective-permute-start | bytes 1179656 | tf_op jit(solution)/shard_map/ppermute | solution.py:131
  119.8 7.3 %weight_out_grad_piece.3 = bf16[3072,3072]{1,0:T(8,128)(2,1)} custom-call(bf16[512,3072]{1,0:T(8,128)(2,1)S(1)} %copy-done, bf16[512,3072]{1,0:T(8,128)(2,1)S(1)} %constant_dynamic-update-slice_fusion.g_ref, bf16[3072,3072]{1,0:T(8,128)(2,1)} %weight_out_grad_piece.2.refs_0_), custom_call_target="tpu_custom_call", output_to_operand_aliasing={{}: (2, {})} | custom-call | flops 1207959552 | bytes 3145728 | tf_op jit(solution)/shard_map/weight_out_grad_piece/pallas_call | solution.py:296
  128.8 1.6 %collective-permute-start.28 = (bf16[64,3072]{1,0:T(8,128)(2,1)S(1)}, bf16[64,3072]{1,0:T(8,128)(2,1)S(1)}, u32[]{:S(2)}, u32[]{:S(2)}) collective-permute-start(bf16[64,3072]{1,0:T(8,128)(2,1)S(1)} %get-tuple-element.108), channel_id=1, source_target_pairs={{4,12},{12,20},{20,28},{28,24},{24,16},{16,8},{8,0},{0,4},{5,13},{... | collective-permute-start | bytes 1179656 | tf_op jit(solution)/shard_map/ppermute | solution.py:131
  130.4 7.3 %weight_in_grad_piece.4.refs_9_ = bf16[3072,3072]{1,0:T(8,128)(2,1)} custom-call(bf16[512,3072]{1,0:T(8,128)(2,1)S(1)} %near_hidden.1.h_ref, bf16[64,3072]{1,0:T(8,128)(2,1)S(1)} %copy-done.1, bf16[64,3072]{1,0:T(8,128)(2,1)} %collective-permute-done.12.refs_1_, ...), custom_call_target="tpu_custom_call", output_to_operand_aliasing={{}: (10, {})} | custom-call | flops 1006632960 | bytes 1966080 | tf_op jit(solution)/shard_map/weight_in_grad_piece/pallas_call | solution.py:358
  138.4 1.6 %collective-permute-start.30 = (bf16[64,3072]{1,0:T(8,128)(2,1)S(1)}, bf16[64,3072]{1,0:T(8,128)(2,1)S(1)}, u32[]{:S(2)}, u32[]{:S(2)}) collective-permute-start(bf16[64,3072]{1,0:T(8,128)(2,1)S(1)} %get-tuple-element.106), channel_id=1, source_target_pairs={{4,12},{12,20},{20,28},{28,24},{24,16},{16,8},{8,0},{0,4},{5,13},{... | collective-permute-start | bytes 1179656 | tf_op jit(solution)/shard_map/ppermute | solution.py:131
  140.0 7.3 %weight_in_grad_piece.5 = bf16[3072,3072]{1,0:T(8,128)(2,1)} custom-call(bf16[512,3072]{1,0:T(8,128)(2,1)S(1)} %near_hidden.1.h_ref, bf16[64,3072]{1,0:T(8,128)(2,1)S(1)} %copy-done.1, bf16[64,3072]{1,0:T(8,128)(2,1)} %collective-permute-done.12.refs_1_, bf16[64,3072]{1,0:T(8,128)(2,1)S(1)} %collective-permute-done.14.refs_2_, ...), custom_call_target="tpu_custom_call", output_to_operand_aliasing={{}: (10, {})} | custom-call | flops 1006632960 | bytes 1966080 | tf_op jit(solution)/shard_map/weight_in_grad_piece/pallas_call | solution.py:358
  (92 shorter events, 31.7 us)
Async XLA Ops:
  0.6 13.1 %collective-permute-start.1 = (bf16[64,3072]{1,0:T(8,128)(2,1)}, bf16[64,3072]{1,0:T(8,128)(2,1)S(1)}, u32[]{:S(2)}, u32[]{:S(2)}) collective-permute-start(bf16[64,3072]{1,0:T(8,128)(2,1)} %param.7), channel_id=1, source_target_pairs={{12,4},{20,12},{28,20},{24,28},{16,24},{8,16},{0,8},{4,0},{13,5},{... | collective-permute-start | bytes 1179656 | tf_op jit(solution)/shard_map/ppermute | solution.py:109
  3.7 10.9 %collective-permute-start = (bf16[64,3072]{1,0:T(8,128)(2,1)}, bf16[64,3072]{1,0:T(8,128)(2,1)}, u32[]{:S(2)}, u32[]{:S(2)}) collective-permute-start(bf16[64,3072]{1,0:T(8,128)(2,1)} %param.7), channel_id=1, source_target_pairs={{4,12},{12,20},{20,28},{28,24},{24,16},{16,8},{8,0},{0,4},{5,13},{... | collective-permute-start | bytes 1179656 | tf_op jit(solution)/shard_map/ppermute | solution.py:109
  14.6 10.0 %collective-permute-start.2 = (bf16[64,3072]{1,0:T(8,128)(2,1)}, bf16[64,3072]{1,0:T(8,128)(2,1)}, u32[]{:S(2)}, u32[]{:S(2)}) collective-permute-start(bf16[64,3072]{1,0:T(8,128)(2,1)} %collective-permute-done), channel_id=1, source_target_pairs={{4,12},{12,20},{20,28},{28,24},{24,16},{16,8},{8,0},{0,4},{5,13},{... | collective-permute-start | bytes 1179656 | tf_op jit(solution)/shard_map/ppermute | solution.py:109
  15.7 10.1 %collective-permute-start.3 = (bf16[64,3072]{1,0:T(8,128)(2,1)S(1)}, bf16[64,3072]{1,0:T(8,128)(2,1)}, u32[]{:S(2)}, u32[]{:S(2)}) collective-permute-start(bf16[64,3072]{1,0:T(8,128)(2,1)S(1)} %collective-permute-done.1), channel_id=1, source_target_pairs={{12,4},{20,12},{28,20},{24,28},{16,24},{8,16},{0,8},{4,0},{13,5},{... | collective-permute-start | bytes 1179656 | tf_op jit(solution)/shard_map/ppermute | solution.py:109
  25.8 9.3 %collective-permute-start.4 = (bf16[64,3072]{1,0:T(8,128)(2,1)}, bf16[64,3072]{1,0:T(8,128)(2,1)S(1)}, u32[]{:S(2)}, u32[]{:S(2)}) collective-permute-start(bf16[64,3072]{1,0:T(8,128)(2,1)} %collective-permute-done.2), channel_id=1, source_target_pairs={{4,12},{12,20},{20,28},{28,24},{24,16},{16,8},{8,0},{0,4},{5,13},{... | collective-permute-start | bytes 1179656 | tf_op jit(solution)/shard_map/ppermute | solution.py:109
  27.4 9.1 %collective-permute-start.5 = (bf16[64,3072]{1,0:T(8,128)(2,1)}, bf16[64,3072]{1,0:T(8,128)(2,1)}, u32[]{:S(2)}, u32[]{:S(2)}) collective-permute-start(bf16[64,3072]{1,0:T(8,128)(2,1)} %collective-permute-done.3), channel_id=1, source_target_pairs={{12,4},{20,12},{28,20},{24,28},{16,24},{8,16},{0,8},{4,0},{13,5},{... | collective-permute-start | bytes 1179656 | tf_op jit(solution)/shard_map/ppermute | solution.py:109
  37.4 5.7 %collective-permute-start.6 = (bf16[32,3072]{1,0:T(8,128)(2,1)S(1)}, bf16[32,3072]{1,0:T(8,128)(2,1)S(1)}, u32[]{:S(2)}, u32[]{:S(2)}) collective-permute-start(bf16[32,3072]{1,0:T(8,128)(2,1)S(1)} %slice.60), channel_id=1, source_target_pairs={{4,12},{12,20},{20,28},{28,24},{24,16},{16,8},{8,0},{0,4},{5,13},{... | collective-permute-start | bytes 589832 | tf_op jit(solution)/shard_map/ppermute | solution.py:109
  39.0 5.7 %collective-permute-start.7 = (bf16[32,3072]{1,0:T(8,128)(2,1)S(1)}, bf16[32,3072]{1,0:T(8,128)(2,1)S(1)}, u32[]{:S(2)}, u32[]{:S(2)}) collective-permute-start(bf16[32,3072]{1,0:T(8,128)(2,1)S(1)} %slice.61), channel_id=1, source_target_pairs={{12,4},{20,12},{28,20},{24,28},{16,24},{8,16},{0,8},{4,0},{13,5},{... | collective-permute-start | bytes 589832 | tf_op jit(solution)/shard_map/ppermute | solution.py:109
  47.4 6.1 %collective-permute-start.8 = (bf16[512,768]{1,0:T(8,128)(2,1)S(1)}, bf16[512,768]{1,0:T(8,128)(2,1)S(1)}, u32[]{:S(2)}, u32[]{:S(2)}) collective-permute-start(bf16[512,768]{1,0:T(8,128)(2,1)S(1)} %near_grad_piece.3), channel_id=1, source_target_pairs={{0,1},{1,0},{2,3},{3,2},{4,5},{5,4},{6,7},{7,6},{8,9},{9,8},{10,11... | collective-permute-start | bytes 2359304 | tf_op jit(solution)/shard_map/ppermute | solution.py:428
  51.0 13.0 %collective-permute-start.9 = (bf16[512,768]{1,0:T(8,128)(2,1)}, bf16[512,768]{1,0:T(8,128)(2,1)}, u32[]{:S(2)}, u32[]{:S(2)}) collective-permute-start(bf16[512,768]{1,0:T(8,128)(2,1)} %near_grad_piece.4), channel_id=1, source_target_pairs={{0,1},{1,0},{2,3},{3,2},{4,5},{5,4},{6,7},{7,6},{8,9},{9,8},{10,11... | collective-permute-start | bytes 2359304 | tf_op jit(solution)/shard_map/ppermute | solution.py:428
  51.5 14.0 %collective-permute-start.12 = (bf16[64,3072]{1,0:T(8,128)(2,1)S(1)}, bf16[64,3072]{1,0:T(8,128)(2,1)}, u32[]{:S(2)}, u32[]{:S(2)}) collective-permute-start(bf16[64,3072]{1,0:T(8,128)(2,1)S(1)} %copy-done.1), channel_id=1, source_target_pairs={{12,4},{20,12},{28,20},{24,28},{16,24},{8,16},{0,8},{4,0},{13,5},{... | collective-permute-start | bytes 1179656 | tf_op jit(solution)/shard_map/ppermute | solution.py:109
  51.9 13.5 %collective-permute-start.13 = (bf16[64,3072]{1,0:T(8,128)(2,1)S(1)}, bf16[64,3072]{1,0:T(8,128)(2,1)}, u32[]{:S(2)}, u32[]{:S(2)}) collective-permute-start(bf16[64,3072]{1,0:T(8,128)(2,1)S(1)} %copy-done.1), channel_id=1, source_target_pairs={{4,12},{12,20},{20,28},{28,24},{24,16},{16,8},{8,0},{0,4},{5,13},{... | collective-permute-start | bytes 1179656 | tf_op jit(solution)/shard_map/ppermute | solution.py:109
  58.2 20.8 %collective-permute-start.11 = (bf16[512,768]{1,0:T(8,128)(2,1)}, bf16[512,768]{1,0:T(8,128)(2,1)}, u32[]{:S(2)}, u32[]{:S(2)}) collective-permute-start(bf16[512,768]{1,0:T(8,128)(2,1)} %get-tuple-element.68), channel_id=1, source_target_pairs={{0,2},{1,3},{2,0},{3,1},{4,6},{5,7},{6,4},{7,5},{8,10},{9,11},{10,... | collective-permute-start | bytes 2359304 | tf_op jit(solution)/shard_map/ppermute | solution.py:440
  65.4 10.5 %collective-permute-start.14 = (bf16[64,3072]{1,0:T(8,128)(2,1)}, bf16[64,3072]{1,0:T(8,128)(2,1)S(1)}, u32[]{:S(2)}, u32[]{:S(2)}) collective-permute-start(bf16[64,3072]{1,0:T(8,128)(2,1)} %collective-permute-done.12.refs_1_), channel_id=1, source_target_pairs={{12,4},{20,12},{28,20},{24,28},{16,24},{8,16},{0,8},{4,0},{13,5},{... | collective-permute-start | bytes 1179656 | tf_op jit(solution)/shard_map/ppermute | solution.py:109
  65.9 10.2 %collective-permute-start.15 = (bf16[64,3072]{1,0:T(8,128)(2,1)}, bf16[64,3072]{1,0:T(8,128)(2,1)S(1)}, u32[]{:S(2)}, u32[]{:S(2)}) collective-permute-start(bf16[64,3072]{1,0:T(8,128)(2,1)} %collective-permute-done.13.refs_8_), channel_id=1, source_target_pairs={{4,12},{12,20},{20,28},{28,24},{24,16},{16,8},{8,0},{0,4},{5,13},{... | collective-permute-start | bytes 1179656 | tf_op jit(solution)/shard_map/ppermute | solution.py:109
  67.5 26.7 %collective-permute-start.10 = (bf16[512,768]{1,0:T(8,128)(2,1)S(1)}, bf16[512,768]{1,0:T(8,128)(2,1)S(1)}, u32[]{:S(2)}, u32[]{:S(2)}) collective-permute-start(bf16[512,768]{1,0:T(8,128)(2,1)S(1)} %fusion), channel_id=1, source_target_pairs={{0,2},{1,3},{2,0},{3,1},{4,6},{5,7},{6,4},{7,5},{8,10},{9,11},{10,... | collective-permute-start | bytes 2359304 | tf_op jit(solution)/shard_map/ppermute | solution.py:440
  80.5 2.7 %collective-permute-start.17 = (bf16[256,768]{1,0:T(8,128)(2,1)S(1)}, bf16[256,768]{1,0:T(8,128)(2,1)S(1)}, u32[]{:S(2)}, u32[]{:S(2)}) collective-permute-start(bf16[256,768]{1,0:T(8,128)(2,1)S(1)} %get-tuple-element.113), channel_id=1, source_target_pairs={{0,1},{1,0},{2,3},{3,2},{4,5},{5,4},{6,7},{7,6},{8,9},{9,8},{10,11... | collective-permute-start | bytes 1179656 | tf_op jit(solution)/shard_map/ppermute | solution.py:454
  80.6 2.6 %collective-permute-start.16 = (bf16[256,768]{1,0:T(8,128)(2,1)S(1)}, bf16[256,768]{1,0:T(8,128)(2,1)S(1)}, u32[]{:S(2)}, u32[]{:S(2)}) collective-permute-start(bf16[256,768]{1,0:T(8,128)(2,1)S(1)} %get-tuple-element.114), channel_id=1, source_target_pairs={{0,1},{1,0},{2,3},{3,2},{4,5},{5,4},{6,7},{7,6},{8,9},{9,8},{10,11... | collective-permute-start | bytes 1179656 | tf_op jit(solution)/shard_map/ppermute | solution.py:454
  81.1 13.1 %collective-permute-start.18 = (bf16[64,3072]{1,0:T(8,128)(2,1)S(1)}, bf16[64,3072]{1,0:T(8,128)(2,1)S(1)}, u32[]{:S(2)}, u32[]{:S(2)}) collective-permute-start(bf16[64,3072]{1,0:T(8,128)(2,1)S(1)} %collective-permute-done.14.refs_2_), channel_id=1, source_target_pairs={{12,4},{20,12},{28,20},{24,28},{16,24},{8,16},{0,8},{4,0},{13,5},{... | collective-permute-start | bytes 1179656 | tf_op jit(solution)/shard_map/ppermute | solution.py:109
  81.6 12.6 %collective-permute-start.19 = (bf16[64,3072]{1,0:T(8,128)(2,1)S(1)}, bf16[64,3072]{1,0:T(8,128)(2,1)S(1)}, u32[]{:S(2)}, u32[]{:S(2)}) collective-permute-start(bf16[64,3072]{1,0:T(8,128)(2,1)S(1)} %collective-permute-done.15.refs_7_), channel_id=1, source_target_pairs={{4,12},{12,20},{20,28},{28,24},{24,16},{16,8},{8,0},{0,4},{5,13},{... | collective-permute-start | bytes 1179656 | tf_op jit(solution)/shard_map/ppermute | solution.py:109
  95.8 2.8 %collective-permute-start.21 = (bf16[256,768]{1,0:T(8,128)(2,1)S(1)}, bf16[256,768]{1,0:T(8,128)(2,1)S(1)}, u32[]{:S(2)}, u32[]{:S(2)}) collective-permute-start(bf16[256,768]{1,0:T(8,128)(2,1)S(1)} %get-tuple-element.111), channel_id=1, source_target_pairs={{0,1},{1,0},{2,3},{3,2},{4,5},{5,4},{6,7},{7,6},{8,9},{9,8},{10,11... | collective-permute-start | bytes 1179656 | tf_op jit(solution)/shard_map/ppermute | solution.py:454
  95.8 2.7 %collective-permute-start.20 = (bf16[256,768]{1,0:T(8,128)(2,1)S(1)}, bf16[256,768]{1,0:T(8,128)(2,1)S(1)}, u32[]{:S(2)}, u32[]{:S(2)}) collective-permute-start(bf16[256,768]{1,0:T(8,128)(2,1)S(1)} %get-tuple-element.112), channel_id=1, source_target_pairs={{0,1},{1,0},{2,3},{3,2},{4,5},{5,4},{6,7},{7,6},{8,9},{9,8},{10,11... | collective-permute-start | bytes 1179656 | tf_op jit(solution)/shard_map/ppermute | solution.py:454
  96.5 16.8 %collective-permute-start.24 = (bf16[32,3072]{1,0:T(8,128)(2,1)S(1)}, bf16[32,3072]{1,0:T(8,128)(2,1)S(1)}, u32[]{:S(2)}, u32[]{:S(2)}) collective-permute-start(bf16[32,3072]{1,0:T(8,128)(2,1)S(1)} %slice.62), channel_id=1, source_target_pairs={{4,12},{12,20},{20,28},{28,24},{24,16},{16,8},{8,0},{0,4},{5,13},{... | collective-permute-start | bytes 589832 | tf_op jit(solution)/shard_map/ppermute | solution.py:109
  98.1 15.2 %collective-permute-start.25 = (bf16[32,3072]{1,0:T(8,128)(2,1)S(1)}, bf16[32,3072]{1,0:T(8,128)(2,1)S(1)}, u32[]{:S(2)}, u32[]{:S(2)}) collective-permute-start(bf16[32,3072]{1,0:T(8,128)(2,1)S(1)} %slice.63), channel_id=1, source_target_pairs={{12,4},{20,12},{28,20},{24,28},{16,24},{8,16},{0,8},{4,0},{13,5},{... | collective-permute-start | bytes 589832 | tf_op jit(solution)/shard_map/ppermute | solution.py:109
  110.1 7.5 %collective-permute-start.23 = (bf16[64,1536]{1,0:T(8,128)(2,1)S(1)}, bf16[64,1536]{1,0:T(8,128)(2,1)S(1)}, u32[]{:S(2)}, u32[]{:S(2)}) collective-permute-start(bf16[64,1536]{1,0:T(8,128)(2,1)S(1)} %get-tuple-element.115), channel_id=1, source_target_pairs={{12,4},{20,12},{28,20},{24,28},{16,24},{8,16},{0,8},{4,0},{13,5},{... | collective-permute-start | bytes 589832 | tf_op jit(solution)/shard_map/ppermute | solution.py:131
  110.6 7.0 %collective-permute-start.22 = (bf16[64,1536]{1,0:T(8,128)(2,1)S(1)}, bf16[64,1536]{1,0:T(8,128)(2,1)S(1)}, u32[]{:S(2)}, u32[]{:S(2)}) collective-permute-start(bf16[64,1536]{1,0:T(8,128)(2,1)S(1)} %get-tuple-element.116), channel_id=1, source_target_pairs={{4,12},{12,20},{20,28},{28,24},{24,16},{16,8},{8,0},{0,4},{5,13},{... | collective-permute-start | bytes 589832 | tf_op jit(solution)/shard_map/ppermute | solution.py:131
  117.8 10.2 %collective-permute-start.27 = (bf16[64,3072]{1,0:T(8,128)(2,1)S(1)}, bf16[64,3072]{1,0:T(8,128)(2,1)S(1)}, u32[]{:S(2)}, u32[]{:S(2)}) collective-permute-start(bf16[64,3072]{1,0:T(8,128)(2,1)S(1)} %get-tuple-element.109), channel_id=1, source_target_pairs={{12,4},{20,12},{28,20},{24,28},{16,24},{8,16},{0,8},{4,0},{13,5},{... | collective-permute-start | bytes 1179656 | tf_op jit(solution)/shard_map/ppermute | solution.py:131
  118.3 9.9 %collective-permute-start.26 = (bf16[64,3072]{1,0:T(8,128)(2,1)S(1)}, bf16[64,3072]{1,0:T(8,128)(2,1)S(1)}, u32[]{:S(2)}, u32[]{:S(2)}) collective-permute-start(bf16[64,3072]{1,0:T(8,128)(2,1)S(1)} %get-tuple-element.110), channel_id=1, source_target_pairs={{4,12},{12,20},{20,28},{28,24},{24,16},{16,8},{8,0},{0,4},{5,13},{... | collective-permute-start | bytes 1179656 | tf_op jit(solution)/shard_map/ppermute | solution.py:131
  128.3 9.4 %collective-permute-start.29 = (bf16[64,3072]{1,0:T(8,128)(2,1)S(1)}, bf16[64,3072]{1,0:T(8,128)(2,1)S(1)}, u32[]{:S(2)}, u32[]{:S(2)}) collective-permute-start(bf16[64,3072]{1,0:T(8,128)(2,1)S(1)} %get-tuple-element.107), channel_id=1, source_target_pairs={{12,4},{20,12},{28,20},{24,28},{16,24},{8,16},{0,8},{4,0},{13,5},{... | collective-permute-start | bytes 1179656 | tf_op jit(solution)/shard_map/ppermute | solution.py:131
  128.8 8.9 %collective-permute-start.28 = (bf16[64,3072]{1,0:T(8,128)(2,1)S(1)}, bf16[64,3072]{1,0:T(8,128)(2,1)S(1)}, u32[]{:S(2)}, u32[]{:S(2)}) collective-permute-start(bf16[64,3072]{1,0:T(8,128)(2,1)S(1)} %get-tuple-element.108), channel_id=1, source_target_pairs={{4,12},{12,20},{20,28},{28,24},{24,16},{16,8},{8,0},{0,4},{5,13},{... | collective-permute-start | bytes 1179656 | tf_op jit(solution)/shard_map/ppermute | solution.py:131
  137.9 9.4 %collective-permute-start.31 = (bf16[64,3072]{1,0:T(8,128)(2,1)S(1)}, bf16[64,3072]{1,0:T(8,128)(2,1)S(1)}, u32[]{:S(2)}, u32[]{:S(2)}) collective-permute-start(bf16[64,3072]{1,0:T(8,128)(2,1)S(1)} %get-tuple-element.105), channel_id=1, source_target_pairs={{12,4},{20,12},{28,20},{24,28},{16,24},{8,16},{0,8},{4,0},{13,5},{... | collective-permute-start | bytes 1179656 | tf_op jit(solution)/shard_map/ppermute | solution.py:131
  138.4 8.9 %collective-permute-start.30 = (bf16[64,3072]{1,0:T(8,128)(2,1)S(1)}, bf16[64,3072]{1,0:T(8,128)(2,1)S(1)}, u32[]{:S(2)}, u32[]{:S(2)}) collective-permute-start(bf16[64,3072]{1,0:T(8,128)(2,1)S(1)} %get-tuple-element.106), channel_id=1, source_target_pairs={{4,12},{12,20},{20,28},{28,24},{24,16},{16,8},{8,0},{0,4},{5,13},{... | collective-permute-start | bytes 1179656 | tf_op jit(solution)/shard_map/ppermute | solution.py:131
  (8 other events, 42.9 us)

commit v4 on v3

--- a/solution.py
+++ b/solution.py
@@ -9,6 +9,7 @@
 
 VMEM_BYTES = 20 * 2**20
 STREAM_VMEM_BYTES = 47 * 2**20
+SUM_VMEM_BYTES = 41 * 2**20
 
 
 def row_cycle(mesh):
@@ -249,15 +250,15 @@
         wm_ref, wo_ref, *refs = refs[len(other) :]
         value = lax.dot_general(m_ref[...], wm_ref[...], LAST_DIMS, preferred_element_type=jnp.float32)
         value += lax.dot_general(theirs, wo_ref[...], LAST_DIMS, preferred_element_type=jnp.float32)
+        here = pl.ds(pl.multiple_of(pl.program_id(0) * tile, tile), tile)
         if total is not None:
-            value += refs[0][...]
+            value += refs[0][:, here]
             refs = refs[1:]
-        refs[0][...] = value
+        refs[0][:, here] = value
         if far is not None:
             refs[1][...] = value[far * share : (far + 1) * share].astype(jnp.bfloat16)
 
-    block = pl.BlockSpec((tokens, tile), lambda i, s: (0, i))
-    out_specs, out_shape = [block], [jax.ShapeDtypeStruct((tokens, out), jnp.float32)]
+    out_specs, out_shape = [NEAR], [pltpu.VMEM((tokens, out), jnp.float32)]
     if far is not None:
         out_specs.append(pl.BlockSpec((share, tile), lambda i, s: (0, i)))
         out_shape.append(jax.ShapeDtypeStruct((share, out), jnp.bfloat16))
@@ -271,11 +272,12 @@
                 pl.BlockSpec((tile, width), lambda i, s: (i, s[0])),
                 pl.BlockSpec((tile, width), lambda i, s: (i, s[1])),
             ]
-            + ([] if total is None else [block]),
+            + ([] if total is None else [NEAR]),
             out_specs=out_specs,
         ),
         out_shape=out_shape,
-        compiler_params=pltpu.CompilerParams(vmem_limit_bytes=STREAM_VMEM_BYTES),
+        input_output_aliases={} if total is None else {4 + len(other): 0},
+        compiler_params=pltpu.CompilerParams(vmem_limit_bytes=SUM_VMEM_BYTES),
         cost_estimate=cost(4 * tokens * width * out, 4 * width * out + 8 * tokens * out),
         name="input_grad_piece",
     )(where, mine, *other, weight_in, weight_in, *([] if total is None else [total]))

time: 149 us -> 146 us (0.980)
  Pallas kernels: 83.4 us -> 78 us
  waiting for transfers between devices: 18.3 us -> 20.2 us
    pallas_call x2, Pallas kernels: 21.5 us -> 16.4 us  [input_grad_piece(): pl.pallas_call(kernel, grid_spec=pltpu.PrefetchScalarGridSpec(num_scalar_...]
    ppermute x2, waiting for transfers between devices: 3.77 us -> 5.73 us  [body(): arrived.append([lax.ppermute(last, 'col', hop) for hop in hops])]
    unnamed x16 -> x12, local copies, waits for them, and re-layouts: 3.1 us -> 3.09 us
  transfers between devices with their start and end apart: 32 -> 32, of which waited for: 13 -> 13; matrix products, arithmetic and copies ran while one was open for 6% -> 6% of each run, Pallas kernels for 55% -> 52%
where the time goes in v4:
time: 146 us; the launch traced here: 145 us
  Pallas kernels  78 us (53%)
  starting transfers between devices  29.5 us (20%)
  waiting for transfers between devices  20.2 us (14%)
  local copies, waits for them, and re-layouts  9.87 us (7%)
  other arithmetic  6.18 us (4%)
    pallas_call x3, Pallas kernels, weight_in_grad_piece(): pl.pallas_call(kernel, grid=(tiles,), in_specs=[NEAR] + [pl.BlockSpec((pi...  18.6 us
    pallas_call x2, Pallas kernels, input_grad_piece(): pl.pallas_call(kernel, grid_spec=pltpu.PrefetchScalarGridSpec(num_scalar_...  16.4 us
    pallas_call x2, Pallas kernels, weight_out_grad_piece(): pl.pallas_call(kernel, grid=(share // tile,), in_specs=[pl.BlockSpec((tok...  14.6 us
    ppermute x8, starting transfers between devices, step(): lax.ppermute(fore, 'row', ahead)  10.7 us
    pallas_call x3, Pallas kernels, near_grad_piece(): pl.pallas_call(kernel, in_specs=[NEAR, NEAR] + ([] if taken is None else...  9.68 us
    ppermute x8, waiting for transfers between devices, step(): lax.ppermute(fore, 'row', ahead)  8.8 us
    pallas_call x3, Pallas kernels, near_rows(): pl.pallas_call(kernel, in_specs=[SCALAR, FAR], out_specs=NEAR, out_shape=...  7.05 us
    ppermute x8, starting transfers between devices, step(): lax.ppermute(back, 'row', behind)  6.76 us
  transfers between devices with their start and end apart: 32, of which 13 were waited for; matrix products, arithmetic and copies ran while one was open for 6% of the time, Pallas kernels for 52%

profile of v4, /device:TPU:0, one launch (start us, length us, event | category | flops | bytes accessed | tf_op | source)
XLA Modules:
  0.0 144.9 jit_solution(6649738609572791399)
XLA Ops:
  0.6 3.1 %collective-permute-start.1 = (bf16[64,3072]{1,0:T(8,128)(2,1)}, bf16[64,3072]{1,0:T(8,128)(2,1)S(1)}, u32[]{:S(2)}, u32[]{:S(2)}) collective-permute-start(bf16[64,3072]{1,0:T(8,128)(2,1)} %param.7), channel_id=1, source_target_pairs={{12,4},{20,12},{28,20},{24,28},{16,24},{8,16},{0,8},{4,0},{13,5},{... | collective-permute-start | bytes 1179656 | tf_op jit(solution)/shard_map/ppermute | solution.py:110
  5.5 1.9 %copy-done.2 = bf16[512,3072]{1,0:T(8,128)(2,1)S(1)} copy-done((bf16[512,3072]{1,0:T(8,128)(2,1)S(1)}, bf16[512,3072]{1,0:T(8,128)(2,1)}, u32[]{:S(2)}) %copy-start.2) | copy-done | bytes 3145752
  7.4 6.3 %gelu_blocks.1 = (bf16[512,3072]{1,0:T(8,128)(2,1)}, f32[512,1536]{1,0:T(8,128)}, f32[8,128]{1,0:T(8,128)}) custom-call(s32[9]{0:T(128)S(1)} %stack.71.order_ref, bf16[512,3072]{1,0:T(8,128)(2,1)S(1)} %copy-done.2), custom_call_target="tpu_custom_call" | custom-call | flops 7864320 | bytes 2359296 | tf_op jit(solution)/shard_map/gelu_blocks/pallas_call | solution.py:69
  17.7 2.4 %near_rows.3.w_ref = bf16[768,3072]{1,0:T(8,128)(2,1)S(1)} custom-call(s32[1]{0:T(128)} %bitcast.11.start_ref, bf16[3072,3072]{1,0:T(8,128)(2,1)} %w_ref.7), custom_call_target="tpu_custom_call" | custom-call | bytes 2359296 | tf_op jit(solution)/shard_map/near_rows/pallas_call | solution.py:177
  20.0 2.4 %near_rows.4.w_ref = bf16[768,3072]{1,0:T(8,128)(2,1)S(1)} custom-call(s32[1]{0:T(128)} %bitcast.1.start_ref, bf16[3072,3072]{1,0:T(8,128)(2,1)} %w_ref.7), custom_call_target="tpu_custom_call" | custom-call | bytes 2359296 | tf_op jit(solution)/shard_map/near_rows/pallas_call | solution.py:177
  22.4 2.2 %collective-permute-done.2 = bf16[64,3072]{1,0:T(8,128)(2,1)} collective-permute-done((bf16[64,3072]{1,0:T(8,128)(2,1)}, bf16[64,3072]{1,0:T(8,128)(2,1)}, u32[]{:S(2)}, u32[]{:S(2)}) %collective-permute-start.2) | collective-permute-done | bytes 393248 | tf_op jit(solution)/shard_map/ppermute | solution.py:110
  25.8 1.6 %collective-permute-start.4 = (bf16[64,3072]{1,0:T(8,128)(2,1)}, bf16[64,3072]{1,0:T(8,128)(2,1)S(1)}, u32[]{:S(2)}, u32[]{:S(2)}) collective-permute-start(bf16[64,3072]{1,0:T(8,128)(2,1)} %collective-permute-done.2), channel_id=1, source_target_pairs={{4,12},{12,20},{20,28},{28,24},{24,16},{16,8},{8,0},{0,4},{5,13},{... | collective-permute-start | bytes 1179656 | tf_op jit(solution)/shard_map/ppermute | solution.py:110
  29.9 2.4 %near_rows.5.w_ref = bf16[768,3072]{1,0:T(8,128)(2,1)S(1)} custom-call(s32[1]{0:T(128)} %bitcast.12.start_ref, bf16[3072,3072]{1,0:T(8,128)(2,1)} %w_ref.7), custom_call_target="tpu_custom_call" | custom-call | bytes 2359296 | tf_op jit(solution)/shard_map/near_rows/pallas_call | solution.py:177
  32.2 2.8 %collective-permute-done.4 = bf16[64,3072]{1,0:T(8,128)(2,1)S(1)} collective-permute-done((bf16[64,3072]{1,0:T(8,128)(2,1)}, bf16[64,3072]{1,0:T(8,128)(2,1)S(1)}, u32[]{:S(2)}, u32[]{:S(2)}) %collective-permute-start.4) | collective-permute-done | bytes 393248 | tf_op jit(solution)/shard_map/ppermute | solution.py:110
  37.4 1.6 %collective-permute-start.6 = (bf16[32,3072]{1,0:T(8,128)(2,1)S(1)}, bf16[32,3072]{1,0:T(8,128)(2,1)S(1)}, u32[]{:S(2)}, u32[]{:S(2)}) collective-permute-start(bf16[32,3072]{1,0:T(8,128)(2,1)S(1)} %slice.60), channel_id=1, source_target_pairs={{4,12},{12,20},{20,28},{28,24},{24,16},{16,8},{8,0},{0,4},{5,13},{... | collective-permute-start | bytes 589832 | tf_op jit(solution)/shard_map/ppermute | solution.py:110
  40.5 2.6 %collective-permute-done.6 = bf16[32,3072]{1,0:T(8,128)(2,1)S(1)} collective-permute-done((bf16[32,3072]{1,0:T(8,128)(2,1)S(1)}, bf16[32,3072]{1,0:T(8,128)(2,1)S(1)}, u32[]{:S(2)}, u32[]{:S(2)}) %collective-permute-start.6) | collective-permute-done | bytes 196640 | tf_op jit(solution)/shard_map/ppermute | solution.py:110
  44.7 2.6 %near_grad_piece.3 = bf16[512,768]{1,0:T(8,128)(2,1)S(1)} custom-call(bf16[512,3072]{1,0:T(8,128)(2,1)S(1)} %constant_dynamic-update-slice_fusion.g_ref, bf16[768,3072]{1,0:T(8,128)(2,1)S(1)} %near_rows.3.w_ref), custom_call_target="tpu_custom_call" | custom-call | flops 603979776 | bytes 1179648 | tf_op jit(solution)/shard_map/near_grad_piece/pallas_call | solution.py:199
  47.4 3.5 %near_grad_piece.4 = bf16[512,768]{1,0:T(8,128)(2,1)} custom-call(bf16[512,3072]{1,0:T(8,128)(2,1)S(1)} %constant_dynamic-update-slice_fusion.g_ref, bf16[768,3072]{1,0:T(8,128)(2,1)S(1)} %near_rows.4.w_ref), custom_call_target="tpu_custom_call" | custom-call | flops 603979776 | bytes 1179648 | tf_op jit(solution)/shard_map/near_grad_piece/pallas_call | solution.py:199
  51.9 1.6 %collective-permute-start.13 = (bf16[64,3072]{1,0:T(8,128)(2,1)S(1)}, bf16[64,3072]{1,0:T(8,128)(2,1)}, u32[]{:S(2)}, u32[]{:S(2)}) collective-permute-start(bf16[64,3072]{1,0:T(8,128)(2,1)S(1)} %copy-done.1), channel_id=1, source_target_pairs={{4,12},{12,20},{20,28},{28,24},{24,16},{16,8},{8,0},{0,4},{5,13},{... | collective-permute-start | bytes 1179656 | tf_op jit(solution)/shard_map/ppermute | solution.py:110
  53.5 3.5 %near_grad_piece.5 = (f32[512,768]{1,0:T(8,128)S(1)}, bf16[512,768]{1,0:T(8,128)(2,1)}) custom-call(bf16[512,3072]{1,0:T(8,128)(2,1)S(1)} %constant_dynamic-update-slice_fusion.g_ref, bf16[768,3072]{1,0:T(8,128)(2,1)S(1)} %near_rows.5.w_ref, bf16[512,768]{1,0:T(8,128)(2,1)S(1)} %collective-permute-done.8.refs_0_), custom_call_target="tpu_custom_call" | custom-call | flops 603979776 | bytes 1179648 | tf_op jit(solution)/shard_map/near_grad_piece/pallas_call | solution.py:199
  59.7 4.3 %act_grad_piece.1 = f32[512,768]{1,0:T(8,128)S(1)} custom-call(s32[1]{0:T(128)} %bitcast.start_ref, bf16[512,3072]{1,0:T(8,128)(2,1)S(1)} %constant_dynamic-update-slice_fusion.g_ref, bf16[3072,3072]{1,0:T(8,128)(2,1)} %w_ref.7), custom_call_target="tpu_custom_call" | custom-call | flops 603979776 | bytes 1572864 | tf_op jit(solution)/shard_map/act_grad_piece/pallas_call | solution.py:231
  66.0 1.6 %collective-permute-start.15 = (bf16[64,3072]{1,0:T(8,128)(2,1)}, bf16[64,3072]{1,0:T(8,128)(2,1)S(1)}, u32[]{:S(2)}, u32[]{:S(2)}) collective-permute-start(bf16[64,3072]{1,0:T(8,128)(2,1)} %collective-permute-done.13.refs_8_), channel_id=1, source_target_pairs={{4,12},{12,20},{20,28},{28,24},{24,16},{16,8},{8,0},{0,4},{5,13},{... | collective-permute-start | bytes 1179656 | tf_op jit(solution)/shard_map/ppermute | solution.py:110
  68.1 7.3 %weight_out_grad_piece.2.refs_0_ = bf16[3072,3072]{1,0:T(8,128)(2,1)} custom-call(bf16[512,3072]{1,0:T(8,128)(2,1)S(1)} %copy-done, bf16[512,3072]{1,0:T(8,128)(2,1)S(1)} %constant_dynamic-update-slice_fusion.g_ref), custom_call_target="tpu_custom_call" | custom-call | flops 1207959552 | bytes 3145728 | tf_op jit(solution)/shard_map/weight_out_grad_piece/pallas_call | solution.py:298
  76.2 2.9 %collective-permute-done.11 = bf16[512,768]{1,0:T(8,128)(2,1)} collective-permute-done((bf16[512,768]{1,0:T(8,128)(2,1)}, bf16[512,768]{1,0:T(8,128)(2,1)}, u32[]{:S(2)}, u32[]{:S(2)}) %collective-permute-start.11) | collective-permute-done | bytes 786464 | tf_op jit(solution)/shard_map/ppermute | solution.py:442
  81.6 1.6 %collective-permute-start.19 = (bf16[64,3072]{1,0:T(8,128)(2,1)S(1)}, bf16[64,3072]{1,0:T(8,128)(2,1)S(1)}, u32[]{:S(2)}, u32[]{:S(2)}) collective-permute-start(bf16[64,3072]{1,0:T(8,128)(2,1)S(1)} %collective-permute-done.15.refs_7_), channel_id=1, source_target_pairs={{4,12},{12,20},{20,28},{28,24},{24,16},{16,8},{8,0},{0,4},{5,13},{... | collective-permute-start | bytes 1179656 | tf_op jit(solution)/shard_map/ppermute | solution.py:110
  83.2 8.2 %input_grad_piece.2.refs_4_ = f32[512,3072]{1,0:T(8,128)S(1)} custom-call(s32[2]{0:T(128)S(1)} %pad_add_fusion.1._, bf16[512,768]{1,0:T(8,128)(2,1)S(1)} %multiply_convert_fusion.1.m_ref.refs_0_, bf16[256,768]{1,0:T(8,128)(2,1)S(1)} %collective-permute-done.16.refs_0_.refs_1_, bf16[256,768]{1,0:T(8,128)(2,1)S(1)} %collective-permute-done.17.refs_1_.refs_2_, ...), custom_call_target="tpu_custom_call" | custom-call | flops 1207959552 | bytes 5505024 | tf_op jit(solution)/shard_map/input_grad_piece/pallas_call | solution.py:265
  91.4 2.9 %collective-permute-done.10 = bf16[512,768]{1,0:T(8,128)(2,1)} collective-permute-done((bf16[512,768]{1,0:T(8,128)(2,1)S(1)}, bf16[512,768]{1,0:T(8,128)(2,1)}, u32[]{:S(2)}, u32[]{:S(2)}) %collective-permute-start.10) | collective-permute-done | bytes 786464 | tf_op jit(solution)/shard_map/ppermute | solution.py:442
  94.3 1.8 %multiply_convert_fusion.m_ref.refs_3_ = bf16[512,768]{1,0:T(8,128)(2,1)S(1)} fusion(f32[512,1536]{1,0:T(8,128)S(1)} %copy-done.5, bf16[512,768]{1,0:T(8,128)(2,1)} %collective-permute-done.10, f32[512,768]{1,0:T(8,128)S(1)} %act_grad_piece.1, bf16[512,768]{1,0:T(8,128)(2,1)} %collective-permute-done.9), kind=kLoop, calls=%fused_computation | loop fusion | flops 2359296 | bytes 5505024 | tf_op jit(solution)/shard_map/convert_element_type | solution.py:455
  96.8 1.6 %collective-permute-start.24 = (bf16[32,3072]{1,0:T(8,128)(2,1)S(1)}, bf16[32,3072]{1,0:T(8,128)(2,1)S(1)}, u32[]{:S(2)}, u32[]{:S(2)}) collective-permute-start(bf16[32,3072]{1,0:T(8,128)(2,1)S(1)} %slice.62), channel_id=1, source_target_pairs={{4,12},{12,20},{20,28},{28,24},{24,16},{16,8},{8,0},{0,4},{5,13},{... | collective-permute-start | bytes 589832 | tf_op jit(solution)/shard_map/ppermute | solution.py:110
  98.9 8.3 %input_grad_piece.3 = (f32[512,3072]{1,0:T(8,128)S(1)}, bf16[64,3072]{1,0:T(8,128)(2,1)S(1)}) custom-call(s32[2]{0:T(128)S(1)} %pad_add_fusion._, bf16[512,768]{1,0:T(8,128)(2,1)S(1)} %multiply_convert_fusion.m_ref.refs_3_, bf16[256,768]{1,0:T(8,128)(2,1)S(1)} %collective-permute-done.20.refs_0_.refs_4_, ...), custom_call_target="tpu_custom_call", output_to_operand_aliasing={{0}: (6, {})} | custom-call | flops 1207959552 | bytes 5505024 | tf_op jit(solution)/shard_map/input_grad_piece/pallas_call | solution.py:265
  107.7 1.6 %collective-permute-start.22 = (bf16[64,1536]{1,0:T(8,128)(2,1)S(1)}, bf16[64,1536]{1,0:T(8,128)(2,1)S(1)}, u32[]{:S(2)}, u32[]{:S(2)}) collective-permute-start(bf16[64,1536]{1,0:T(8,128)(2,1)S(1)} %get-tuple-element.116), channel_id=1, source_target_pairs={{4,12},{12,20},{20,28},{28,24},{24,16},{16,8},{8,0},{0,4},{5,13},{... | collective-permute-start | bytes 589832 | tf_op jit(solution)/shard_map/ppermute | solution.py:132
  110.4 4.0 %weight_in_grad_piece.3.refs_9_ = bf16[3072,3072]{1,0:T(8,128)(2,1)} custom-call(bf16[512,3072]{1,0:T(8,128)(2,1)S(1)} %near_hidden.1.h_ref, bf16[64,3072]{1,0:T(8,128)(2,1)S(1)} %copy-done.1, bf16[64,3072]{1,0:T(8,128)(2,1)} %collective-permute-done.12.refs_1_, bf16[64,3072]{1,0:T(8,128)(2,1)S(1)} %collective-permute-done.14.refs_2_, ...), custom_call_target="tpu_custom_call" | custom-call | flops 402653184 | bytes 786432 | tf_op jit(solution)/shard_map/weight_in_grad_piece/pallas_call | solution.py:360
  115.0 1.6 %collective-permute-start.26 = (bf16[64,3072]{1,0:T(8,128)(2,1)S(1)}, bf16[64,3072]{1,0:T(8,128)(2,1)S(1)}, u32[]{:S(2)}, u32[]{:S(2)}) collective-permute-start(bf16[64,3072]{1,0:T(8,128)(2,1)S(1)} %get-tuple-element.110), channel_id=1, source_target_pairs={{4,12},{12,20},{20,28},{28,24},{24,16},{16,8},{8,0},{0,4},{5,13},{... | collective-permute-start | bytes 1179656 | tf_op jit(solution)/shard_map/ppermute | solution.py:132
  116.6 7.3 %weight_out_grad_piece.3 = bf16[3072,3072]{1,0:T(8,128)(2,1)} custom-call(bf16[512,3072]{1,0:T(8,128)(2,1)S(1)} %copy-done, bf16[512,3072]{1,0:T(8,128)(2,1)S(1)} %constant_dynamic-update-slice_fusion.g_ref, bf16[3072,3072]{1,0:T(8,128)(2,1)} %weight_out_grad_piece.2.refs_0_), custom_call_target="tpu_custom_call", output_to_operand_aliasing={{}: (2, {})} | custom-call | flops 1207959552 | bytes 3145728 | tf_op jit(solution)/shard_map/weight_out_grad_piece/pallas_call | solution.py:298
  127.1 7.3 %weight_in_grad_piece.4.refs_9_ = bf16[3072,3072]{1,0:T(8,128)(2,1)} custom-call(bf16[512,3072]{1,0:T(8,128)(2,1)S(1)} %near_hidden.1.h_ref, bf16[64,3072]{1,0:T(8,128)(2,1)S(1)} %copy-done.1, bf16[64,3072]{1,0:T(8,128)(2,1)} %collective-permute-done.12.refs_1_, ...), custom_call_target="tpu_custom_call", output_to_operand_aliasing={{}: (10, {})} | custom-call | flops 1006632960 | bytes 1966080 | tf_op jit(solution)/shard_map/weight_in_grad_piece/pallas_call | solution.py:360
  135.1 1.6 %collective-permute-start.30 = (bf16[64,3072]{1,0:T(8,128)(2,1)S(1)}, bf16[64,3072]{1,0:T(8,128)(2,1)S(1)}, u32[]{:S(2)}, u32[]{:S(2)}) collective-permute-start(bf16[64,3072]{1,0:T(8,128)(2,1)S(1)} %get-tuple-element.106), channel_id=1, source_target_pairs={{4,12},{12,20},{20,28},{28,24},{24,16},{16,8},{8,0},{0,4},{5,13},{... | collective-permute-start | bytes 1179656 | tf_op jit(solution)/shard_map/ppermute | solution.py:132
  136.7 7.3 %weight_in_grad_piece.5 = bf16[3072,3072]{1,0:T(8,128)(2,1)} custom-call(bf16[512,3072]{1,0:T(8,128)(2,1)S(1)} %near_hidden.1.h_ref, bf16[64,3072]{1,0:T(8,128)(2,1)S(1)} %copy-done.1, bf16[64,3072]{1,0:T(8,128)(2,1)} %collective-permute-done.12.refs_1_, bf16[64,3072]{1,0:T(8,128)(2,1)S(1)} %collective-permute-done.14.refs_2_, ...), custom_call_target="tpu_custom_call", output_to_operand_aliasing={{}: (10, {})} | custom-call | flops 1006632960 | bytes 1966080 | tf_op jit(solution)/shard_map/weight_in_grad_piece/pallas_call | solution.py:360
  (87 shorter events, 32.3 us)
Async XLA Ops:
  0.6 13.1 %collective-permute-start.1 = (bf16[64,3072]{1,0:T(8,128)(2,1)}, bf16[64,3072]{1,0:T(8,128)(2,1)S(1)}, u32[]{:S(2)}, u32[]{:S(2)}) collective-permute-start(bf16[64,3072]{1,0:T(8,128)(2,1)} %param.7), channel_id=1, source_target_pairs={{12,4},{20,12},{28,20},{24,28},{16,24},{8,16},{0,8},{4,0},{13,5},{... | collective-permute-start | bytes 1179656 | tf_op jit(solution)/shard_map/ppermute | solution.py:110
  3.7 10.9 %collective-permute-start = (bf16[64,3072]{1,0:T(8,128)(2,1)}, bf16[64,3072]{1,0:T(8,128)(2,1)}, u32[]{:S(2)}, u32[]{:S(2)}) collective-permute-start(bf16[64,3072]{1,0:T(8,128)(2,1)} %param.7), channel_id=1, source_target_pairs={{4,12},{12,20},{20,28},{28,24},{24,16},{16,8},{8,0},{0,4},{5,13},{... | collective-permute-start | bytes 1179656 | tf_op jit(solution)/shard_map/ppermute | solution.py:110
  14.6 10.0 %collective-permute-start.2 = (bf16[64,3072]{1,0:T(8,128)(2,1)}, bf16[64,3072]{1,0:T(8,128)(2,1)}, u32[]{:S(2)}, u32[]{:S(2)}) collective-permute-start(bf16[64,3072]{1,0:T(8,128)(2,1)} %collective-permute-done), channel_id=1, source_target_pairs={{4,12},{12,20},{20,28},{28,24},{24,16},{16,8},{8,0},{0,4},{5,13},{... | collective-permute-start | bytes 1179656 | tf_op jit(solution)/shard_map/ppermute | solution.py:110
  15.7 10.1 %collective-permute-start.3 = (bf16[64,3072]{1,0:T(8,128)(2,1)S(1)}, bf16[64,3072]{1,0:T(8,128)(2,1)}, u32[]{:S(2)}, u32[]{:S(2)}) collective-permute-start(bf16[64,3072]{1,0:T(8,128)(2,1)S(1)} %collective-permute-done.1), channel_id=1, source_target_pairs={{12,4},{20,12},{28,20},{24,28},{16,24},{8,16},{0,8},{4,0},{13,5},{... | collective-permute-start | bytes 1179656 | tf_op jit(solution)/shard_map/ppermute | solution.py:110
  25.8 9.3 %collective-permute-start.4 = (bf16[64,3072]{1,0:T(8,128)(2,1)}, bf16[64,3072]{1,0:T(8,128)(2,1)S(1)}, u32[]{:S(2)}, u32[]{:S(2)}) collective-permute-start(bf16[64,3072]{1,0:T(8,128)(2,1)} %collective-permute-done.2), channel_id=1, source_target_pairs={{4,12},{12,20},{20,28},{28,24},{24,16},{16,8},{8,0},{0,4},{5,13},{... | collective-permute-start | bytes 1179656 | tf_op jit(solution)/shard_map/ppermute | solution.py:110
  27.4 9.1 %collective-permute-start.5 = (bf16[64,3072]{1,0:T(8,128)(2,1)}, bf16[64,3072]{1,0:T(8,128)(2,1)}, u32[]{:S(2)}, u32[]{:S(2)}) collective-permute-start(bf16[64,3072]{1,0:T(8,128)(2,1)} %collective-permute-done.3), channel_id=1, source_target_pairs={{12,4},{20,12},{28,20},{24,28},{16,24},{8,16},{0,8},{4,0},{13,5},{... | collective-permute-start | bytes 1179656 | tf_op jit(solution)/shard_map/ppermute | solution.py:110
  37.4 5.7 %collective-permute-start.6 = (bf16[32,3072]{1,0:T(8,128)(2,1)S(1)}, bf16[32,3072]{1,0:T(8,128)(2,1)S(1)}, u32[]{:S(2)}, u32[]{:S(2)}) collective-permute-start(bf16[32,3072]{1,0:T(8,128)(2,1)S(1)} %slice.60), channel_id=1, source_target_pairs={{4,12},{12,20},{20,28},{28,24},{24,16},{16,8},{8,0},{0,4},{5,13},{... | collective-permute-start | bytes 589832 | tf_op jit(solution)/shard_map/ppermute | solution.py:110
  39.0 5.7 %collective-permute-start.7 = (bf16[32,3072]{1,0:T(8,128)(2,1)S(1)}, bf16[32,3072]{1,0:T(8,128)(2,1)S(1)}, u32[]{:S(2)}, u32[]{:S(2)}) collective-permute-start(bf16[32,3072]{1,0:T(8,128)(2,1)S(1)} %slice.61), channel_id=1, source_target_pairs={{12,4},{20,12},{28,20},{24,28},{16,24},{8,16},{0,8},{4,0},{13,5},{... | collective-permute-start | bytes 589832 | tf_op jit(solution)/shard_map/ppermute | solution.py:110
  47.4 6.1 %collective-permute-start.8 = (bf16[512,768]{1,0:T(8,128)(2,1)S(1)}, bf16[512,768]{1,0:T(8,128)(2,1)S(1)}, u32[]{:S(2)}, u32[]{:S(2)}) collective-permute-start(bf16[512,768]{1,0:T(8,128)(2,1)S(1)} %near_grad_piece.3), channel_id=1, source_target_pairs={{0,1},{1,0},{2,3},{3,2},{4,5},{5,4},{6,7},{7,6},{8,9},{9,8},{10,11... | collective-permute-start | bytes 2359304 | tf_op jit(solution)/shard_map/ppermute | solution.py:430
  51.0 13.0 %collective-permute-start.9 = (bf16[512,768]{1,0:T(8,128)(2,1)}, bf16[512,768]{1,0:T(8,128)(2,1)}, u32[]{:S(2)}, u32[]{:S(2)}) collective-permute-start(bf16[512,768]{1,0:T(8,128)(2,1)} %near_grad_piece.4), channel_id=1, source_target_pairs={{0,1},{1,0},{2,3},{3,2},{4,5},{5,4},{6,7},{7,6},{8,9},{9,8},{10,11... | collective-permute-start | bytes 2359304 | tf_op jit(solution)/shard_map/ppermute | solution.py:430
  51.5 14.0 %collective-permute-start.12 = (bf16[64,3072]{1,0:T(8,128)(2,1)S(1)}, bf16[64,3072]{1,0:T(8,128)(2,1)}, u32[]{:S(2)}, u32[]{:S(2)}) collective-permute-start(bf16[64,3072]{1,0:T(8,128)(2,1)S(1)} %copy-done.1), channel_id=1, source_target_pairs={{12,4},{20,12},{28,20},{24,28},{16,24},{8,16},{0,8},{4,0},{13,5},{... | collective-permute-start | bytes 1179656 | tf_op jit(solution)/shard_map/ppermute | solution.py:110
  51.9 13.5 %collective-permute-start.13 = (bf16[64,3072]{1,0:T(8,128)(2,1)S(1)}, bf16[64,3072]{1,0:T(8,128)(2,1)}, u32[]{:S(2)}, u32[]{:S(2)}) collective-permute-start(bf16[64,3072]{1,0:T(8,128)(2,1)S(1)} %copy-done.1), channel_id=1, source_target_pairs={{4,12},{12,20},{20,28},{28,24},{24,16},{16,8},{8,0},{0,4},{5,13},{... | collective-permute-start | bytes 1179656 | tf_op jit(solution)/shard_map/ppermute | solution.py:110
  58.2 20.8 %collective-permute-start.11 = (bf16[512,768]{1,0:T(8,128)(2,1)}, bf16[512,768]{1,0:T(8,128)(2,1)}, u32[]{:S(2)}, u32[]{:S(2)}) collective-permute-start(bf16[512,768]{1,0:T(8,128)(2,1)} %get-tuple-element.68), channel_id=1, source_target_pairs={{0,2},{1,3},{2,0},{3,1},{4,6},{5,7},{6,4},{7,5},{8,10},{9,11},{10,... | collective-permute-start | bytes 2359304 | tf_op jit(solution)/shard_map/ppermute | solution.py:442
  65.5 10.5 %collective-permute-start.14 = (bf16[64,3072]{1,0:T(8,128)(2,1)}, bf16[64,3072]{1,0:T(8,128)(2,1)S(1)}, u32[]{:S(2)}, u32[]{:S(2)}) collective-permute-start(bf16[64,3072]{1,0:T(8,128)(2,1)} %collective-permute-done.12.refs_1_), channel_id=1, source_target_pairs={{12,4},{20,12},{28,20},{24,28},{16,24},{8,16},{0,8},{4,0},{13,5},{... | collective-permute-start | bytes 1179656 | tf_op jit(solution)/shard_map/ppermute | solution.py:110
  66.0 10.2 %collective-permute-start.15 = (bf16[64,3072]{1,0:T(8,128)(2,1)}, bf16[64,3072]{1,0:T(8,128)(2,1)S(1)}, u32[]{:S(2)}, u32[]{:S(2)}) collective-permute-start(bf16[64,3072]{1,0:T(8,128)(2,1)} %collective-permute-done.13.refs_8_), channel_id=1, source_target_pairs={{4,12},{12,20},{20,28},{28,24},{24,16},{16,8},{8,0},{0,4},{5,13},{... | collective-permute-start | bytes 1179656 | tf_op jit(solution)/shard_map/ppermute | solution.py:110
  67.5 26.7 %collective-permute-start.10 = (bf16[512,768]{1,0:T(8,128)(2,1)S(1)}, bf16[512,768]{1,0:T(8,128)(2,1)}, u32[]{:S(2)}, u32[]{:S(2)}) collective-permute-start(bf16[512,768]{1,0:T(8,128)(2,1)S(1)} %fusion), channel_id=1, source_target_pairs={{0,2},{1,3},{2,0},{3,1},{4,6},{5,7},{6,4},{7,5},{8,10},{9,11},{10,... | collective-permute-start | bytes 2359304 | tf_op jit(solution)/shard_map/ppermute | solution.py:442
  80.5 2.7 %collective-permute-start.17 = (bf16[256,768]{1,0:T(8,128)(2,1)S(1)}, bf16[256,768]{1,0:T(8,128)(2,1)S(1)}, u32[]{:S(2)}, u32[]{:S(2)}) collective-permute-start(bf16[256,768]{1,0:T(8,128)(2,1)S(1)} %get-tuple-element.113), channel_id=1, source_target_pairs={{0,1},{1,0},{2,3},{3,2},{4,5},{5,4},{6,7},{7,6},{8,9},{9,8},{10,11... | collective-permute-start | bytes 1179656 | tf_op jit(solution)/shard_map/ppermute | solution.py:456
  80.6 2.6 %collective-permute-start.16 = (bf16[256,768]{1,0:T(8,128)(2,1)S(1)}, bf16[256,768]{1,0:T(8,128)(2,1)S(1)}, u32[]{:S(2)}, u32[]{:S(2)}) collective-permute-start(bf16[256,768]{1,0:T(8,128)(2,1)S(1)} %get-tuple-element.114), channel_id=1, source_target_pairs={{0,1},{1,0},{2,3},{3,2},{4,5},{5,4},{6,7},{7,6},{8,9},{9,8},{10,11... | collective-permute-start | bytes 1179656 | tf_op jit(solution)/shard_map/ppermute | solution.py:456
  81.1 13.2 %collective-permute-start.18 = (bf16[64,3072]{1,0:T(8,128)(2,1)S(1)}, bf16[64,3072]{1,0:T(8,128)(2,1)S(1)}, u32[]{:S(2)}, u32[]{:S(2)}) collective-permute-start(bf16[64,3072]{1,0:T(8,128)(2,1)S(1)} %collective-permute-done.14.refs_2_), channel_id=1, source_target_pairs={{12,4},{20,12},{28,20},{24,28},{16,24},{8,16},{0,8},{4,0},{13,5},{... | collective-permute-start | bytes 1179656 | tf_op jit(solution)/shard_map/ppermute | solution.py:110
  81.6 12.7 %collective-permute-start.19 = (bf16[64,3072]{1,0:T(8,128)(2,1)S(1)}, bf16[64,3072]{1,0:T(8,128)(2,1)S(1)}, u32[]{:S(2)}, u32[]{:S(2)}) collective-permute-start(bf16[64,3072]{1,0:T(8,128)(2,1)S(1)} %collective-permute-done.15.refs_7_), channel_id=1, source_target_pairs={{4,12},{12,20},{20,28},{28,24},{24,16},{16,8},{8,0},{0,4},{5,13},{... | collective-permute-start | bytes 1179656 | tf_op jit(solution)/shard_map/ppermute | solution.py:110
  96.1 2.8 %collective-permute-start.21 = (bf16[256,768]{1,0:T(8,128)(2,1)S(1)}, bf16[256,768]{1,0:T(8,128)(2,1)S(1)}, u32[]{:S(2)}, u32[]{:S(2)}) collective-permute-start(bf16[256,768]{1,0:T(8,128)(2,1)S(1)} %get-tuple-element.111), channel_id=1, source_target_pairs={{0,1},{1,0},{2,3},{3,2},{4,5},{5,4},{6,7},{7,6},{8,9},{9,8},{10,11... | collective-permute-start | bytes 1179656 | tf_op jit(solution)/shard_map/ppermute | solution.py:456
  96.2 2.7 %collective-permute-start.20 = (bf16[256,768]{1,0:T(8,128)(2,1)S(1)}, bf16[256,768]{1,0:T(8,128)(2,1)S(1)}, u32[]{:S(2)}, u32[]{:S(2)}) collective-permute-start(bf16[256,768]{1,0:T(8,128)(2,1)S(1)} %get-tuple-element.112), channel_id=1, source_target_pairs={{0,1},{1,0},{2,3},{3,2},{4,5},{5,4},{6,7},{7,6},{8,9},{9,8},{10,11... | collective-permute-start | bytes 1179656 | tf_op jit(solution)/shard_map/ppermute | solution.py:456
  96.8 13.5 %collective-permute-start.24 = (bf16[32,3072]{1,0:T(8,128)(2,1)S(1)}, bf16[32,3072]{1,0:T(8,128)(2,1)S(1)}, u32[]{:S(2)}, u32[]{:S(2)}) collective-permute-start(bf16[32,3072]{1,0:T(8,128)(2,1)S(1)} %slice.62), channel_id=1, source_target_pairs={{4,12},{12,20},{20,28},{28,24},{24,16},{16,8},{8,0},{0,4},{5,13},{... | collective-permute-start | bytes 589832 | tf_op jit(solution)/shard_map/ppermute | solution.py:110
  98.4 11.9 %collective-permute-start.25 = (bf16[32,3072]{1,0:T(8,128)(2,1)S(1)}, bf16[32,3072]{1,0:T(8,128)(2,1)S(1)}, u32[]{:S(2)}, u32[]{:S(2)}) collective-permute-start(bf16[32,3072]{1,0:T(8,128)(2,1)S(1)} %slice.63), channel_id=1, source_target_pairs={{12,4},{20,12},{28,20},{24,28},{16,24},{8,16},{0,8},{4,0},{13,5},{... | collective-permute-start | bytes 589832 | tf_op jit(solution)/shard_map/ppermute | solution.py:110
  107.2 7.2 %collective-permute-start.23 = (bf16[64,1536]{1,0:T(8,128)(2,1)S(1)}, bf16[64,1536]{1,0:T(8,128)(2,1)S(1)}, u32[]{:S(2)}, u32[]{:S(2)}) collective-permute-start(bf16[64,1536]{1,0:T(8,128)(2,1)S(1)} %get-tuple-element.115), channel_id=1, source_target_pairs={{12,4},{20,12},{28,20},{24,28},{16,24},{8,16},{0,8},{4,0},{13,5},{... | collective-permute-start | bytes 589832 | tf_op jit(solution)/shard_map/ppermute | solution.py:132
  107.7 6.7 %collective-permute-start.22 = (bf16[64,1536]{1,0:T(8,128)(2,1)S(1)}, bf16[64,1536]{1,0:T(8,128)(2,1)S(1)}, u32[]{:S(2)}, u32[]{:S(2)}) collective-permute-start(bf16[64,1536]{1,0:T(8,128)(2,1)S(1)} %get-tuple-element.116), channel_id=1, source_target_pairs={{4,12},{12,20},{20,28},{28,24},{24,16},{16,8},{8,0},{0,4},{5,13},{... | collective-permute-start | bytes 589832 | tf_op jit(solution)/shard_map/ppermute | solution.py:132
  114.5 10.2 %collective-permute-start.27 = (bf16[64,3072]{1,0:T(8,128)(2,1)S(1)}, bf16[64,3072]{1,0:T(8,128)(2,1)S(1)}, u32[]{:S(2)}, u32[]{:S(2)}) collective-permute-start(bf16[64,3072]{1,0:T(8,128)(2,1)S(1)} %get-tuple-element.109), channel_id=1, source_target_pairs={{12,4},{20,12},{28,20},{24,28},{16,24},{8,16},{0,8},{4,0},{13,5},{... | collective-permute-start | bytes 1179656 | tf_op jit(solution)/shard_map/ppermute | solution.py:132
  115.0 9.9 %collective-permute-start.26 = (bf16[64,3072]{1,0:T(8,128)(2,1)S(1)}, bf16[64,3072]{1,0:T(8,128)(2,1)S(1)}, u32[]{:S(2)}, u32[]{:S(2)}) collective-permute-start(bf16[64,3072]{1,0:T(8,128)(2,1)S(1)} %get-tuple-element.110), channel_id=1, source_target_pairs={{4,12},{12,20},{20,28},{28,24},{24,16},{16,8},{8,0},{0,4},{5,13},{... | collective-permute-start | bytes 1179656 | tf_op jit(solution)/shard_map/ppermute | solution.py:132
  125.1 9.4 %collective-permute-start.29 = (bf16[64,3072]{1,0:T(8,128)(2,1)S(1)}, bf16[64,3072]{1,0:T(8,128)(2,1)S(1)}, u32[]{:S(2)}, u32[]{:S(2)}) collective-permute-start(bf16[64,3072]{1,0:T(8,128)(2,1)S(1)} %get-tuple-element.107), channel_id=1, source_target_pairs={{12,4},{20,12},{28,20},{24,28},{16,24},{8,16},{0,8},{4,0},{13,5},{... | collective-permute-start | bytes 1179656 | tf_op jit(solution)/shard_map/ppermute | solution.py:132
  125.6 8.9 %collective-permute-start.28 = (bf16[64,3072]{1,0:T(8,128)(2,1)S(1)}, bf16[64,3072]{1,0:T(8,128)(2,1)S(1)}, u32[]{:S(2)}, u32[]{:S(2)}) collective-permute-start(bf16[64,3072]{1,0:T(8,128)(2,1)S(1)} %get-tuple-element.108), channel_id=1, source_target_pairs={{4,12},{12,20},{20,28},{28,24},{24,16},{16,8},{8,0},{0,4},{5,13},{... | collective-permute-start | bytes 1179656 | tf_op jit(solution)/shard_map/ppermute | solution.py:132
  134.6 9.4 %collective-permute-start.31 = (bf16[64,3072]{1,0:T(8,128)(2,1)S(1)}, bf16[64,3072]{1,0:T(8,128)(2,1)S(1)}, u32[]{:S(2)}, u32[]{:S(2)}) collective-permute-start(bf16[64,3072]{1,0:T(8,128)(2,1)S(1)} %get-tuple-element.105), channel_id=1, source_target_pairs={{12,4},{20,12},{28,20},{24,28},{16,24},{8,16},{0,8},{4,0},{13,5},{... | collective-permute-start | bytes 1179656 | tf_op jit(solution)/shard_map/ppermute | solution.py:132
  135.1 8.9 %collective-permute-start.30 = (bf16[64,3072]{1,0:T(8,128)(2,1)S(1)}, bf16[64,3072]{1,0:T(8,128)(2,1)S(1)}, u32[]{:S(2)}, u32[]{:S(2)}) collective-permute-start(bf16[64,3072]{1,0:T(8,128)(2,1)S(1)} %get-tuple-element.106), channel_id=1, source_target_pairs={{4,12},{12,20},{20,28},{28,24},{24,16},{16,8},{8,0},{0,4},{5,13},{... | collective-permute-start | bytes 1179656 | tf_op jit(solution)/shard_map/ppermute | solution.py:132
  (6 other events, 33.2 us)
